TPU v7x, 32 devices: a whole 2x2x4 slice. The times are simulated.
32 devices in a mesh: gx: 4 (over z), gy: 8 (over y, x, core).
Axes of the slice: x: 2, y: 2, z: 4, core: 2. Of those that a mesh axis runs over, the one named last changes fastest.
Arguments:
- features: bfloat16 [64, 128, 64, 128], P('gx', 'gy'), may hold values from -6 to 6
- tile_mask: int32 [64, 128, 9], P('gx', 'gy'), may hold values from 0 to 1, as said below
- pool_map: int32 [64, 128, 64], P('gx', 'gy'), may hold values from 0 to 63
- readers: int32 [32, 8], replicated, may hold values from -1 to 31, as said below
- w_query: bfloat16 [128, 128], replicated, may hold values from -0.5 to 0.5
- w_key: bfloat16 [128, 128], replicated, may hold values from -0.5 to 0.5
- w_value: bfloat16 [128, 128], replicated, may hold values from -0.5 to 0.5
- w_cquery: bfloat16 [128, 128], replicated, may hold values from -0.5 to 0.5
- w_ckey: bfloat16 [128, 128], replicated, may hold values from -0.5 to 0.5
- w_cvalue: bfloat16 [128, 128], replicated, may hold values from -0.5 to 0.5
Outputs:
- update: bfloat16 [64, 128, 64, 128], P('gx', 'gy')
Inputs may be any that keep to these rules, and one draw needn't show every extreme that they name: `tile_mask`: entry 4 (the cell with itself) is always 1; all entries are 0 or 1. `readers`: A row lists between 1 and 8 distinct domains other than its own, then -1 entries; some row lists 8.
All inputs are finite; a program needn't handle non-finite values.
Results may differ from a plain program's by a relative error of at most 0.0065.
Values may be sent and summed in bfloat16 or wider, within the bound.
No kernel may reach another device: no remote copies, remote signals or barrier semaphores. Data moves between devices by JAX's collectives and lax.ppermute only.
A program may use at most 256 MiB of HBM per device.

v0:
```python
import functools
import math

import jax
import jax.numpy as jnp
from jax import lax
from jax.experimental import pallas as pl
from jax.experimental.pallas import tpu as pltpu
from jax.sharding import PartitionSpec as P

BF16 = jnp.bfloat16
F32 = jnp.float32
S = 64
DEPTH = 2
IN_VMEM = pl.BlockSpec(memory_space=pltpu.VMEM)
IN_HBM = pl.BlockSpec(memory_space=pltpu.HBM)


def dot(a, b):
    return jnp.dot(a, b, preferred_element_type=F32)


def dot_t(a, b):
    return lax.dot_general(a, b, (((1,), (1,)), ((), ())), preferred_element_type=F32)


def t_dot(a, b):
    return lax.dot_general(a, b, (((0,), (0,)), ((), ())), preferred_element_type=F32)


def in_hbm(array):
    return pltpu.with_memory_space_constraint(array, pltpu.HBM)


def params(mib):
    return pltpu.CompilerParams(vmem_limit_bytes=mib * 1024 * 1024)


def paired(ids):
    half = ids.shape[0] // 2
    return jnp.concatenate([ids[:half], ids[half:]], axis=1)


def pool_kernel(tile, f_ref, pm_ref, tm_ref, wq_ref, wk_ref, fv_ref, pv_ref, mv_ref, m_ref, pooled_ref, up_ref, down_ref, tv, wq, wk, sems):
    rows, span, chan = fv_ref.shape
    cy = span // tile
    small = [(pm_ref, pv_ref), (tm_ref, tv), (wq_ref, wq), (wk_ref, wk)]
    first = [pltpu.make_async_copy(src, dst, sems.at[rows + i]) for i, (src, dst) in enumerate(small)]
    for copy in first:
        copy.start()
    for r in range(rows):
        pltpu.make_async_copy(f_ref.at[r], fv_ref.at[r], sems.at[r]).start()
    for copy in first:
        copy.wait()
    m_ref[...] = (dot_t(wq[...], wk[...]) * (0.5 / math.sqrt(chan))).astype(BF16)

    node = lax.broadcasted_iota(jnp.int32, (S, 2 * tile), 0)
    order = [c for i in range(cy // 2) for c in (i, i + cy // 2)]
    block = lax.broadcasted_iota(jnp.int32, (18, 12 * tile), 1) // tile
    which = lax.broadcasted_iota(jnp.int32, (18, 12 * tile), 0)
    offset, second = which % 9, which // 9
    hit = (offset // 3 == block // 4) & (offset % 3 == block % 4 - second)
    pick = jnp.where(hit, 1 / math.sqrt(tile), 0.0).astype(BF16)
    even = lax.broadcasted_iota(jnp.int32, (9, cy), 1) % 2 == 0

    def row_step(r, total):
        mask = tv[pl.ds(r, 9, stride=rows), :].astype(F32)
        both = jnp.concatenate([jnp.where(even, mask, 0.0), jnp.where(even, 0.0, mask)], axis=0)
        mv_ref[r] = t_dot(both.astype(BF16), pick)
        pairs = paired(pv_ref[r])
        onehot = jnp.concatenate(
            [(jnp.broadcast_to(pairs[i : i + 1], node.shape) == node).astype(F32).astype(BF16) for i in range(cy // 2)],
            axis=1,
        )
        pltpu.make_async_copy(f_ref.at[r], fv_ref.at[r], sems.at[r]).wait()
        beads = jnp.concatenate([fv_ref[r, tile * c : tile * (c + 1)] for c in order], axis=0)
        return total + dot(onehot, beads)

    total = lax.fori_loop(0, rows, row_step, jnp.zeros((S, chan), F32), unroll=4)
    pooled = (total * math.sqrt(S / (rows * span))).astype(BF16)
    pooled_ref[...] = pooled
    for ref, r in ((up_ref, rows - 1), (down_ref, 0)):
        ref[:span] = fv_ref[r]
        ref[span:] = pooled


def pool(features, tile_mask, pool_map, w_query, w_key):
    cx, cy, tile, chan = features.shape
    span = cy * tile
    edge = jax.ShapeDtypeStruct((span + S, chan), BF16)
    return pl.pallas_call(
        functools.partial(pool_kernel, tile),
        in_specs=[IN_HBM] * 5,
        out_specs=[IN_VMEM] * 7,
        out_shape=[
            pltpu.VMEM((cx, span, chan), BF16),
            pltpu.VMEM((cx, cy, tile), jnp.int32),
            pltpu.VMEM((cx, cy, 12 * tile), F32),
            pltpu.VMEM((chan, chan), BF16),
            jax.ShapeDtypeStruct((S, chan), BF16),
            edge,
            edge,
        ],
        scratch_shapes=[
            pltpu.VMEM((9 * cx, cy), jnp.int32),
            pltpu.VMEM((chan, chan), BF16),
            pltpu.VMEM((chan, chan), BF16),
            pltpu.SemaphoreType.DMA((cx + 4,)),
        ],
        compiler_params=params(16),
        name="pool",
    )(
        in_hbm(features.reshape(cx, span, chan)),
        in_hbm(pool_map),
        in_hbm(jnp.transpose(tile_mask, (2, 0, 1)).reshape(9 * cx, cy)),
        in_hbm(w_query),
        in_hbm(w_key),
    )


def attend(tile, tasks):
    waiting = []

    def finish(task, weights):
        _, windows, _, store = task
        near = jnp.concatenate([window() for window in windows], axis=0)
        store(dot(jnp.concatenate(weights, axis=1), near).astype(BF16))

    for task in tasks:
        query, windows, masks, _ = task
        weights = []
        for r, window in enumerate(windows):
            half = dot_t(query, window()).astype(BF16)
            lanes = slice(4 * tile * r, 4 * tile * (r + 1))
            mask = jnp.concatenate([jnp.broadcast_to(masks(h, lanes), (tile, 4 * tile)) for h in (0, 1)], axis=0)
            weights.append((half * jnp.tanh(half) + half) * mask.astype(BF16))
        waiting.append((task, weights))
        if len(waiting) > DEPTH:
            finish(*waiting.pop(0))
    while waiting:
        finish(*waiting.pop(0))


def inner_tasks(refs, row, above, here, below):
    fv, pv, mv, m, o = refs
    _, span, chan = fv.shape
    cy, tile = pv.shape[1:]
    pairs = paired(pv[row])
    node = lax.broadcasted_iota(jnp.int32, (chan, 2 * tile), 0)
    for i in range(cy // 2):
        turned = (jnp.broadcast_to(pairs[i : i + 1], node.shape) == node).astype(F32).T.astype(BF16)
        o[row, tile * i : tile * (i + 1), chan:] = turned[:tile]
        o[row, span // 2 + tile * i : span // 2 + tile * (i + 1), chan:] = turned[tile:]
    queries = dot(here(2 * tile, span - 2 * tile), m[...]).astype(BF16)
    tasks = []
    for j in range(1, cy // 2 - 1):
        lo = 2 * tile * j

        def store(value, lo=lo):
            o[row, lo : lo + 2 * tile, :chan] = value

        tasks.append((
            queries[lo - 2 * tile : lo],
            [functools.partial(near, lo - tile, lo + 3 * tile) for near in (above, here, below)],
            lambda h, lanes, j=j: mv[row, 2 * j + h : 2 * j + h + 1, lanes],
            store,
        ))
    return tasks


def rows_of(ref, row):
    return lambda lo, hi: ref[row, lo:hi]


def flat(ref):
    return lambda lo, hi: ref[lo:hi]


def inner_kernel(first, count, has_out, n_ties, fv, pv, mv, m, *rest):
    o = rest[-1]
    tile = pv.shape[2]
    refs = (fv, pv, mv, m, o)

    def body(row, many):
        tasks = []
        for k in range(many):
            tasks += inner_tasks(refs, row + k, rows_of(fv, row + k - 1), rows_of(fv, row + k), rows_of(fv, row + k + 1))
        attend(tile, tasks)

    if count // 2:

        @pl.loop(0, count // 2)
        def _(i):
            body(first + 2 * i, 2)

    if count % 2:
        body(first + count - 1, 1)


def ends_kernel(fv, pv, mv, m, out_in, above, below, o):
    tile = pv.shape[2]
    last = fv.shape[0] - 1
    refs = (fv, pv, mv, m, o)
    attend(
        tile,
        inner_tasks(refs, 0, flat(above), rows_of(fv, 0), rows_of(fv, 1))
        + inner_tasks(refs, last, rows_of(fv, last - 1), rows_of(fv, last), flat(below)),
    )


def sides_kernel(fv, pv, mv, m, out_in, above, below, left, right, *rest):
    o = rest[-1]
    rows, span, chan = fv.shape
    cy, tile = pv.shape[1:]
    side = 2 * tile
    tasks = []
    for row in range(rows):
        for j in (0, cy // 2 - 1):
            lo = side * j

            def window(r, j=j):
                near = flat(above) if r < 0 else flat(below) if r == rows else rows_of(fv, r)
                halo = (left if j == 0 else right)[tile * (r + 1) : tile * (r + 2)]
                own = near(0, 3 * tile) if j == 0 else near(span - 3 * tile, span)
                return jnp.concatenate([halo, own] if j == 0 else [own, halo], axis=0)

            def store(value, row=row, lo=lo):
                o[row, lo : lo + side, :chan] = value

            tasks.append((
                dot(fv[row, lo : lo + side], m[...]).astype(BF16),
                [functools.partial(window, r) for r in (row - 1, row, row + 1)],
                lambda h, lanes, row=row, j=j: mv[row, 2 * j + h : 2 * j + h + 1, lanes],
                store,
            ))
    attend(tile, tasks)


def piece(kernel, rows_done, name, base, out, near=(), ties=()):
    fv, _, _, _ = base
    cx, span, chan = fv.shape
    done = [] if out is None else [out]
    return pl.pallas_call(
        kernel,
        in_specs=[IN_VMEM] * (4 + len(done) + len(near)) + [pl.BlockSpec(memory_space=pl.ANY)] * len(ties),
        out_specs=IN_VMEM,
        out_shape=pltpu.VMEM((cx, span, 2 * chan), BF16),
        input_output_aliases={4: 0} if done else {},
        compiler_params=params(16),
        cost_estimate=pl.CostEstimate(
            flops=int(rows_done * 1_200_000_000), bytes_accessed=1_000_000, transcendentals=0
        ),
        name=name,
    )(*base, *done, *near, *ties)


def final_kernel(nx, ny, g0_ref, g1_ref, readers_ref, wcq_ref, wck_ref, wcv_ref, wv_ref, o_ref, out_ref, mix, rows_out, sems):
    cx, span, chan = rows_out.shape
    nodes = jnp.concatenate([g0_ref[...], g1_ref[...]], axis=0)
    count = nodes.shape[0]
    mx, my = lax.axis_index("gx"), lax.axis_index("gy")
    block = lax.broadcasted_iota(jnp.int32, (readers_ref.shape[0], count), 1) // S
    domain = ((block % nx) ^ mx) * ny + ((block // nx) ^ my)
    lane = lax.broadcasted_iota(jnp.int32, readers_ref.shape, 1)
    mine = jnp.sum(jnp.where(lane == mx * ny + my, readers_ref[...], 0), axis=1, keepdims=True)
    live = jnp.sum(jnp.where(domain == mine, 1.0, 0.0), axis=0, keepdims=True)
    query = dot(nodes[:S], wcq_ref[...]).astype(BF16)
    key = dot(nodes, wck_ref[...]).astype(BF16)
    value = dot(nodes, wcv_ref[...]).astype(BF16)
    half = dot_t(query, key) * (0.5 / math.sqrt(chan))
    weight = (half * jnp.tanh(half) + half).astype(BF16).astype(F32) * live
    mix[:chan] = wv_ref[...]
    mix[chan : chan + S] = (dot(weight.astype(BF16), value) / math.sqrt(S)).astype(BF16)
    mix[chan + S :] = jnp.zeros((chan - S, chan), BF16)

    def send(r):
        return pltpu.make_async_copy(rows_out.at[r], out_ref.at[r], sems.at[r])

    @pl.loop(0, cx)
    def _(r):
        rows_out[r] = dot(o_ref[r], mix[...]).astype(BF16)
        send(r).start()

    @pl.loop(0, cx)
    def _(r):
        send(r).wait()


def final(nx, ny, g0, g1, readers, w_cquery, w_ckey, w_cvalue, w_value, out):
    cx, span, wide = out.shape
    chan = wide // 2
    return pl.pallas_call(
        functools.partial(final_kernel, nx, ny),
        in_specs=[IN_VMEM] * 8,
        out_specs=IN_HBM,
        out_shape=jax.ShapeDtypeStruct((cx, span, chan), BF16),
        scratch_shapes=[
            pltpu.VMEM((2 * chan, chan), BF16),
            pltpu.VMEM((cx, span, chan), BF16),
            pltpu.SemaphoreType.DMA((cx,)),
        ],
        compiler_params=params(16),
        name="final",
    )(g0, g1, readers.T, w_cquery, w_ckey, w_cvalue, w_value, out)


def shift(array, axis, step):
    count = lax.axis_size(axis)
    return lax.ppermute(array, axis, [(i, i + step) for i in range(count) if 0 <= i + step < count])


def swap(array, axis, bit):
    return lax.ppermute(array, axis, [(i, i ^ bit) for i in range(lax.axis_size(axis))])


def pack_kernel(axis, lo, own_ref, before_ref, after_ref, out_ref):
    size = own_ref.shape[0]
    out_ref[:size] = own_ref[...]
    odd = lax.axis_index(axis) % 2 == 1

    @pl.when(odd)
    def _():
        out_ref[size:] = before_ref[lo : lo + size]

    @pl.when(jnp.logical_not(odd))
    def _():
        out_ref[size:] = after_ref[lo : lo + size]


def pack_pair(axis, lo, own, before, after):
    return pl.pallas_call(
        functools.partial(pack_kernel, axis, lo),
        in_specs=[IN_VMEM] * 3,
        out_specs=IN_VMEM,
        out_shape=pltpu.VMEM((2 * own.shape[0], own.shape[1]), BF16),
        compiler_params=params(4),
        name="pair_" + axis,
    )(own, before, after)


def join_kernel(first_ref, second_ref, out_ref):
    size = first_ref.shape[0]
    out_ref[:size] = first_ref[...]
    out_ref[size:] = second_ref[...]


def join(first, second):
    return pl.pallas_call(
        join_kernel,
        in_specs=[IN_VMEM] * 2,
        out_specs=IN_VMEM,
        out_shape=pltpu.VMEM((2 * first.shape[0], first.shape[1]), BF16),
        compiler_params=params(4),
        name="join",
    )(first, second)


def columns_kernel(tile, fv_ref, above_ref, below_ref, first_ref, second_ref, left_ref, right_ref, blocks_ref):
    rows, span, _ = fv_ref.shape
    size = first_ref.shape[0]
    halo = (rows + 2) * tile
    for ref, lo in ((left_ref, 0), (right_ref, span - tile)):
        ref[:tile] = above_ref[lo : lo + tile]
        for r in range(rows):
            ref[(r + 1) * tile : (r + 2) * tile] = fv_ref[r, lo : lo + tile]
        ref[halo - tile : halo] = below_ref[lo : lo + tile]
        ref[halo : halo + size] = first_ref[...]
        ref[halo + size :] = second_ref[...]
    blocks_ref[:size] = first_ref[...]
    blocks_ref[size:] = second_ref[...]


def columns(tile, fv, above, below, first, second):
    rows, _, chan = fv.shape
    count = 2 * first.shape[0]
    edge = pltpu.VMEM(((rows + 2) * tile + count, chan), BF16)
    return pl.pallas_call(
        functools.partial(columns_kernel, tile),
        in_specs=[IN_VMEM] * 5,
        out_specs=[IN_VMEM] * 3,
        out_shape=[edge, edge, pltpu.VMEM((count, chan), BF16)],
        compiler_params=params(4),
        name="columns",
    )(fv, above, below, first, second)


def per_device(features, tile_mask, pool_map, readers, w_query, w_key, w_value, w_cquery, w_ckey, w_cvalue):
    cx, cy, tile, chan = features.shape
    span = cy * tile
    nx, ny = lax.axis_size("gx"), lax.axis_size("gy")
    *base, pooled, up, down = pool(features, tile_mask, pool_map, w_query, w_key)
    fv = base[0]

    def inner(first, count, out, ties):
        kernel = functools.partial(inner_kernel, first, count, out is not None, len(ties))
        return piece(kernel, 0.75 * count, f"inner_{first}", base, out, (), ties)

    cuts = [1, 1 + (cx - 2) * 5 // 14, 1 + (cx - 2) * 7 // 14, cx - 1]
    above = shift(up, "gx", 1)
    below = shift(down, "gx", -1)
    out = inner(cuts[0], cuts[1] - cuts[0], None, ())
    first = pack_pair("gx", span, pooled, above, below)
    second = swap(first, "gx", 2)
    out = inner(cuts[1], cuts[2] - cuts[1], out, (first,))
    for bit in (1 << b for b in range(2, nx.bit_length() - 1)):
        first = join(first, second)
        second = swap(first, "gx", bit)
    to_left, to_right, blocks = columns(tile, fv, above, below, first, second)
    left = shift(to_right, "gy", 1)
    right = shift(to_left, "gy", -1)
    out = inner(cuts[2], cuts[3] - cuts[2], out, (to_right, to_left))
    first = pack_pair("gy", (cx + 2) * tile, blocks, left, right)
    second = swap(first, "gy", 2)
    out = piece(ends_kernel, 1.5, "ends", base, out, (above, below))
    for bit in (1 << b for b in range(2, ny.bit_length() - 1)):
        first = join(first, second)
        second = swap(first, "gy", bit)
    out = piece(sides_kernel, 4, "sides", base, out, (above, below, left, right), (first,))
    update = final(nx, ny, first, second, readers, w_cquery, w_ckey, w_cvalue, w_value, out)
    return update.reshape(features.shape)


def solution(mesh):
    in_specs = (P("gx", "gy", None, None), P("gx", "gy", None), P("gx", "gy", None)) + (P(),) * 7
    return jax.shard_map(
        per_device, mesh=mesh, in_specs=in_specs, out_specs=P("gx", "gy", None, None), check_vma=False
    )
```

profile of v0, /device:TPU:0, one launch (start us, length us, event | category | flops | bytes accessed | tf_op | source)
XLA Modules:
  0.0 57.3 jit_solution(7258147581589618630)
XLA Ops:
  0.0 5.1 %pool.1 = (bf16[16,1024,128]{2,1,0:T(8,128)(2,1)S(1)}, s32[16,16,64]{2,1,0:T(8,128)S(1)}, f32[16,16,768]{2,1,0:T(8,128)S(1)}, bf16[128,128]{1,0:T(8,128)(2,1)S(1...) custom-call(bf16[16,1024,128]{2,1,0:T(8,128)(2,1)} %bitcast.7, ...), custom_call_target="tpu_custom_call" | custom-call | tf_op jit(solution)/shard_map/pool/pallas_call | solution.py:91
  5.1 4.9 %collective-permute-start = (bf16[1088,128]{1,0:T(8,128)(2,1)S(1)}, bf16[1088,128]{1,0:T(8,128)(2,1)S(1)}, u32[]{:S(2)}, u32[]{:S(2)}) collective-permute-start(bf16[1088,128]{1,0:T(8,128)(2,1)S(1)} %get-tuple-element.16), channel_id=1, source_target_pairs={{0,8},{8,16},{16,24},{1,9},{9,17},{17,25},{2,10},{10,18},{18,26},{... | collective-permute-start | bytes 835592 | tf_op jit(solution)/shard_map/ppermute | solution.py:309
  10.0 1.3 %collective-permute-start.1 = (bf16[1088,128]{1,0:T(8,128)(2,1)S(1)}, bf16[1088,128]{1,0:T(8,128)(2,1)S(1)}, u32[]{:S(2)}, u32[]{:S(2)}) collective-permute-start(bf16[1088,128]{1,0:T(8,128)(2,1)S(1)} %get-tuple-element.17), channel_id=1, source_target_pairs={{8,0},{16,8},{24,16},{9,1},{17,9},{25,17},{10,2},{18,10},{26,18},{... | collective-permute-start | bytes 835592 | tf_op jit(solution)/shard_map/ppermute | solution.py:309
  11.3 4.1 %inner_1.1.rest_0_ = bf16[16,1024,256]{2,1,0:T(8,128)(2,1)S(1)} custom-call(bf16[16,1024,128]{2,1,0:T(8,128)(2,1)S(1)} %get-tuple-element.15.fv_ref.fv, s32[16,16,64]{2,1,0:T(8,128)S(1)} %get-tuple-element.22.pv, f32[16,16,768]{2,1,0:T(8,128)S(1)} %get-tuple-element.23.mv, bf16[128,128]{1,0:T(8,128)(2,1)S(1)} %get-tuple-element.24.m), custom_call_target="tpu_custom_call" | custom-call | flops 4499999744 | bytes 1000000 | tf_op jit(solution)/shard_map/inner_1/pallas_call | solution.py:243
  15.5 0.5 collective-permute-done.before_ref.above_ref.above
  15.9 4.1 %collective-permute-done.1.after_ref.below_ref.below = bf16[1088,128]{1,0:T(8,128)(2,1)S(1)} collective-permute-done((bf16[1088,128]{1,0:T(8,128)(2,1)S(1)}, bf16[1088,128]{1,0:T(8,128)(2,1)S(1)}, u32[]{:S(2)}, u32[]{:S(2)}) %collective-permute-start.1) | collective-permute-done | bytes 278560 | tf_op jit(solution)/shard_map/ppermute | solution.py:309
  20.1 2.6 %collective-permute-start.2 = (bf16[128,128]{1,0:T(8,128)(2,1)S(1)}, bf16[128,128]{1,0:T(8,128)(2,1)S(1)}, u32[]{:S(2)}, u32[]{:S(2)}) collective-permute-start(bf16[128,128]{1,0:T(8,128)(2,1)S(1)} %pair_gx.1.first_ref.rest_1_), channel_id=1, source_target_pairs={{0,16},{8,24},{16,0},{24,8},{1,17},{9,25},{17,1},{25,9},{2,18},{10... | collective-permute-start | bytes 98312 | tf_op jit(solution)/shard_map/ppermute | solution.py:313
  22.6 1.6 %inner_6.1.rest_0_ = bf16[16,1024,256]{2,1,0:T(8,128)(2,1)S(1)} custom-call(bf16[16,1024,128]{2,1,0:T(8,128)(2,1)S(1)} %get-tuple-element.15.fv_ref.fv, s32[16,16,64]{2,1,0:T(8,128)S(1)} %get-tuple-element.22.pv, f32[16,16,768]{2,1,0:T(8,128)S(1)} %get-tuple-element.23.mv, bf16[128,128]{1,0:T(8,128)(2,1)S(1)} %get-tuple-element.24.m, ...), custom_call_target="tpu_custom_call", output_to_operand_aliasing={{}: (4, {})} | custom-call | flops 1800000000 | bytes 1000000 | tf_op jit(solution)/shard_map/inner_6/pallas_call | solution.py:243
  24.2 0.7 %collective-permute-done.2.second_ref = bf16[128,128]{1,0:T(8,128)(2,1)S(1)} collective-permute-done((bf16[128,128]{1,0:T(8,128)(2,1)S(1)}, bf16[128,128]{1,0:T(8,128)(2,1)S(1)}, u32[]{:S(2)}, u32[]{:S(2)}) %collective-permute-start.2) | collective-permute-done | bytes 32800 | tf_op jit(solution)/shard_map/ppermute | solution.py:313
  24.9 0.1 columns.1
  24.9 1.3 %collective-permute-start.3 = (bf16[1408,128]{1,0:T(8,128)(2,1)S(1)}, bf16[1408,128]{1,0:T(8,128)(2,1)S(1)}, u32[]{:S(2)}, u32[]{:S(2)}) collective-permute-start(bf16[1408,128]{1,0:T(8,128)(2,1)S(1)} %get-tuple-element.20.rest_1_), channel_id=1, source_target_pairs={{0,1},{1,2},{2,3},{3,4},{4,5},{5,6},{6,7},{8,9},{9,10},{10,11},{11... | collective-permute-start | bytes 1081352 | tf_op jit(solution)/shard_map/ppermute | solution.py:309
  26.3 1.3 %collective-permute-start.4 = (bf16[1408,128]{1,0:T(8,128)(2,1)S(1)}, bf16[1408,128]{1,0:T(8,128)(2,1)S(1)}, u32[]{:S(2)}, u32[]{:S(2)}) collective-permute-start(bf16[1408,128]{1,0:T(8,128)(2,1)S(1)} %get-tuple-element.21.rest_2_), channel_id=1, source_target_pairs={{1,0},{2,1},{3,2},{4,3},{5,4},{6,5},{7,6},{9,8},{10,9},{11,10},{12... | collective-permute-start | bytes 1081352 | tf_op jit(solution)/shard_map/ppermute | solution.py:309
  27.6 5.7 %inner_8.1.out_in = bf16[16,1024,256]{2,1,0:T(8,128)(2,1)S(1)} custom-call(bf16[16,1024,128]{2,1,0:T(8,128)(2,1)S(1)} %get-tuple-element.15.fv_ref.fv, s32[16,16,64]{2,1,0:T(8,128)S(1)} %get-tuple-element.22.pv, f32[16,16,768]{2,1,0:T(8,128)S(1)} %get-tuple-element.23.mv, bf16[128,128]{1,0:T(8,128)(2,1)S(1)} %get-tuple-element.24.m, ...), custom_call_target="tpu_custom_call", output_to_operand_aliasing={{}: (4, {})} | custom-call | flops 6300000256 | bytes 1000000 | tf_op jit(solution)/shard_map/inner_8/pallas_call | solution.py:243
  33.3 0.2 pair_gy.1.first_ref
  33.5 4.8 %collective-permute-start.5 = (bf16[512,128]{1,0:T(8,128)(2,1)S(1)}, bf16[512,128]{1,0:T(8,128)(2,1)S(1)}, u32[]{:S(2)}, u32[]{:S(2)}) collective-permute-start(bf16[512,128]{1,0:T(8,128)(2,1)S(1)} %pair_gy.1.first_ref), channel_id=1, source_target_pairs={{0,2},{1,3},{2,0},{3,1},{4,6},{5,7},{6,4},{7,5},{8,10},{9,11},{10,... | collective-permute-start | bytes 393224 | tf_op jit(solution)/shard_map/ppermute | solution.py:313
  38.3 1.6 %ends.1.out_in = bf16[16,1024,256]{2,1,0:T(8,128)(2,1)S(1)} custom-call(bf16[16,1024,128]{2,1,0:T(8,128)(2,1)S(1)} %get-tuple-element.15.fv_ref.fv, s32[16,16,64]{2,1,0:T(8,128)S(1)} %get-tuple-element.22.pv, f32[16,16,768]{2,1,0:T(8,128)S(1)} %get-tuple-element.23.mv, bf16[128,128]{1,0:T(8,128)(2,1)S(1)} %get-tuple-element.24.m, ...), custom_call_target="tpu_custom_call", output_to_operand_aliasing={{}: (4, {})} | custom-call | flops 1800000000 | bytes 1000000 | tf_op jit(solution)/shard_map/ends/pallas_call | solution.py:243
  39.9 1.5 %collective-permute-done.5.second_ref = bf16[512,128]{1,0:T(8,128)(2,1)S(1)} collective-permute-done((bf16[512,128]{1,0:T(8,128)(2,1)S(1)}, bf16[512,128]{1,0:T(8,128)(2,1)S(1)}, u32[]{:S(2)}, u32[]{:S(2)}) %collective-permute-start.5) | collective-permute-done | bytes 131104 | tf_op jit(solution)/shard_map/ppermute | solution.py:313
  41.4 0.0 copy-start
  41.5 0.0 copy-start.2
  41.5 0.0 copy-start.3
  41.5 3.0 %collective-permute-start.6 = (bf16[1024,128]{1,0:T(8,128)(2,1)S(1)}, bf16[1024,128]{1,0:T(8,128)(2,1)S(1)}, u32[]{:S(2)}, u32[]{:S(2)}) collective-permute-start(bf16[1024,128]{1,0:T(8,128)(2,1)S(1)} %join.1.rest_0_.g0_ref), channel_id=1, source_target_pairs={{0,4},{1,5},{2,6},{3,7},{4,0},{5,1},{6,2},{7,3},{8,12},{9,13},{10,... | collective-permute-start | bytes 786440 | tf_op jit(solution)/shard_map/ppermute | solution.py:313
  44.5 3.8 %sides.1.o_ref = bf16[16,1024,256]{2,1,0:T(8,128)(2,1)S(1)} custom-call(bf16[16,1024,128]{2,1,0:T(8,128)(2,1)S(1)} %get-tuple-element.15.fv_ref.fv, s32[16,16,64]{2,1,0:T(8,128)S(1)} %get-tuple-element.22.pv, f32[16,16,768]{2,1,0:T(8,128)S(1)} %get-tuple-element.23.mv, bf16[128,128]{1,0:T(8,128)(2,1)S(1)} %get-tuple-element.24.m, ...), custom_call_target="tpu_custom_call", output_to_operand_aliasing={{}: (4, {})} | custom-call | flops 4800000000 | bytes 1000000 | tf_op jit(solution)/shard_map/sides/pallas_call | solution.py:243
  48.3 2.5 %collective-permute-done.6.g1_ref = bf16[1024,128]{1,0:T(8,128)(2,1)S(1)} collective-permute-done((bf16[1024,128]{1,0:T(8,128)(2,1)S(1)}, bf16[1024,128]{1,0:T(8,128)(2,1)S(1)}, u32[]{:S(2)}, u32[]{:S(2)}) %collective-permute-start.6) | collective-permute-done | bytes 262176 | tf_op jit(solution)/shard_map/ppermute | solution.py:313
  50.9 6.3 %final.1 = bf16[16,1024,128]{2,1,0:T(8,128)(2,1)} custom-call(bf16[1024,128]{1,0:T(8,128)(2,1)S(1)} %join.1.rest_0_.g0_ref, bf16[1024,128]{1,0:T(8,128)(2,1)S(1)} %collective-permute-done.6.g1_ref, s32[8,32]{1,0:T(8,128)S(1)} %bitcast.6, bf16[128,128]{1,0:T(8,128)(2,1)S(1)} %copy-done, bf16[128,128]{1,0:T(8,128)(2,1)S(1)} %copy-done.1, ...), custom_call_target="tpu_custom_call" | custom-call | tf_op jit(solution)/shard_map/final/pallas_call | solution.py:292
  (11 shorter events, 0.0 us)
Async XLA Ops:
  5.1 10.8 %collective-permute-start = (bf16[1088,128]{1,0:T(8,128)(2,1)S(1)}, bf16[1088,128]{1,0:T(8,128)(2,1)S(1)}, u32[]{:S(2)}, u32[]{:S(2)}) collective-permute-start(bf16[1088,128]{1,0:T(8,128)(2,1)S(1)} %get-tuple-element.16), channel_id=1, source_target_pairs={{0,8},{8,16},{16,24},{1,9},{9,17},{17,25},{2,10},{10,18},{18,26},{... | collective-permute-start | bytes 835592 | tf_op jit(solution)/shard_map/ppermute | solution.py:309
  10.0 10.0 %collective-permute-start.1 = (bf16[1088,128]{1,0:T(8,128)(2,1)S(1)}, bf16[1088,128]{1,0:T(8,128)(2,1)S(1)}, u32[]{:S(2)}, u32[]{:S(2)}) collective-permute-start(bf16[1088,128]{1,0:T(8,128)(2,1)S(1)} %get-tuple-element.17), channel_id=1, source_target_pairs={{8,0},{16,8},{24,16},{9,1},{17,9},{25,17},{10,2},{18,10},{26,18},{... | collective-permute-start | bytes 835592 | tf_op jit(solution)/shard_map/ppermute | solution.py:309
  20.1 4.8 %collective-permute-start.2 = (bf16[128,128]{1,0:T(8,128)(2,1)S(1)}, bf16[128,128]{1,0:T(8,128)(2,1)S(1)}, u32[]{:S(2)}, u32[]{:S(2)}) collective-permute-start(bf16[128,128]{1,0:T(8,128)(2,1)S(1)} %pair_gx.1.first_ref.rest_1_), channel_id=1, source_target_pairs={{0,16},{8,24},{16,0},{24,8},{1,17},{9,25},{17,1},{25,9},{2,18},{10... | collective-permute-start | bytes 98312 | tf_op jit(solution)/shard_map/ppermute | solution.py:313
  24.9 8.3 %collective-permute-start.3 = (bf16[1408,128]{1,0:T(8,128)(2,1)S(1)}, bf16[1408,128]{1,0:T(8,128)(2,1)S(1)}, u32[]{:S(2)}, u32[]{:S(2)}) collective-permute-start(bf16[1408,128]{1,0:T(8,128)(2,1)S(1)} %get-tuple-element.20.rest_1_), channel_id=1, source_target_pairs={{0,1},{1,2},{2,3},{3,4},{4,5},{5,6},{6,7},{8,9},{9,10},{10,11},{11... | collective-permute-start | bytes 1081352 | tf_op jit(solution)/shard_map/ppermute | solution.py:309
  26.3 7.0 %collective-permute-start.4 = (bf16[1408,128]{1,0:T(8,128)(2,1)S(1)}, bf16[1408,128]{1,0:T(8,128)(2,1)S(1)}, u32[]{:S(2)}, u32[]{:S(2)}) collective-permute-start(bf16[1408,128]{1,0:T(8,128)(2,1)S(1)} %get-tuple-element.21.rest_2_), channel_id=1, source_target_pairs={{1,0},{2,1},{3,2},{4,3},{5,4},{6,5},{7,6},{9,8},{10,9},{11,10},{12... | collective-permute-start | bytes 1081352 | tf_op jit(solution)/shard_map/ppermute | solution.py:309
  33.5 7.9 %collective-permute-start.5 = (bf16[512,128]{1,0:T(8,128)(2,1)S(1)}, bf16[512,128]{1,0:T(8,128)(2,1)S(1)}, u32[]{:S(2)}, u32[]{:S(2)}) collective-permute-start(bf16[512,128]{1,0:T(8,128)(2,1)S(1)} %pair_gy.1.first_ref), channel_id=1, source_target_pairs={{0,2},{1,3},{2,0},{3,1},{4,6},{5,7},{6,4},{7,5},{8,10},{9,11},{10,... | collective-permute-start | bytes 393224 | tf_op jit(solution)/shard_map/ppermute | solution.py:313
  41.4 9.4 %copy-start = (bf16[128,128]{1,0:T(8,128)(2,1)S(1)}, bf16[128,128]{1,0:T(8,128)(2,1)}, u32[]{:S(2)}) copy-start(bf16[128,128]{1,0:T(8,128)(2,1)} %wcq_ref.1) | copy-start | bytes 98308
  41.4 9.4 %copy-start.1 = (bf16[128,128]{1,0:T(8,128)(2,1)S(1)}, bf16[128,128]{1,0:T(8,128)(2,1)}, u32[]{:S(2)}) copy-start(bf16[128,128]{1,0:T(8,128)(2,1)} %wck_ref.1) | copy-start | bytes 98308
  41.5 9.4 %copy-start.2 = (bf16[128,128]{1,0:T(8,128)(2,1)S(1)}, bf16[128,128]{1,0:T(8,128)(2,1)}, u32[]{:S(2)}) copy-start(bf16[128,128]{1,0:T(8,128)(2,1)} %wcv_ref.1) | copy-start | bytes 98308
  41.5 9.4 %copy-start.3 = (bf16[128,128]{1,0:T(8,128)(2,1)S(1)}, bf16[128,128]{1,0:T(8,128)(2,1)}, u32[]{:S(2)}) copy-start(bf16[128,128]{1,0:T(8,128)(2,1)} %wv_ref.1) | copy-start | bytes 98308
  41.5 9.4 %copy-start.4 = (s32[32,8]{0,1:T(8,128)S(1)}, s32[32,8]{0,1:T(8,128)}, u32[]{:S(2)}) copy-start(s32[32,8]{0,1:T(8,128)} %param.13) | copy-start | bytes 3076
  41.5 9.3 %collective-permute-start.6 = (bf16[1024,128]{1,0:T(8,128)(2,1)S(1)}, bf16[1024,128]{1,0:T(8,128)(2,1)S(1)}, u32[]{:S(2)}, u32[]{:S(2)}) collective-permute-start(bf16[1024,128]{1,0:T(8,128)(2,1)S(1)} %join.1.rest_0_.g0_ref), channel_id=1, source_target_pairs={{0,4},{1,5},{2,6},{3,7},{4,0},{5,1},{6,2},{7,3},{8,12},{9,13},{10,... | collective-permute-start | bytes 786440 | tf_op jit(solution)/shard_map/ppermute | solution.py:313
where the time goes:
time: 57.5 us; the launch traced here: 57.3 us
  Pallas kernels  28.4 us (49%)
  starting transfers between devices  19.3 us (34%)
  waiting for transfers between devices  9.29 us (16%)
    pallas_call x5, Pallas kernels, piece(): pl.pallas_call(kernel, in_specs=[IN_VMEM] * (4 + len(done) + len(near)) +...  16.7 us
    ppermute x3, starting transfers between devices, swap(): lax.ppermute(array, axis, [(i, i ^ bit) for i in range(lax.axis_size(axis...  10.4 us
    ppermute x4, starting transfers between devices, shift(): lax.ppermute(array, axis, [(i, i + step) for i in range(count) if 0 <= i...  8.84 us
    pallas_call x1, Pallas kernels, final(): pl.pallas_call(functools.partial(final_kernel, nx, ny), in_specs=[IN_VMEM...  6.3 us
    pallas_call x1, Pallas kernels, pool(): pl.pallas_call(functools.partial(pool_kernel, tile), in_specs=[IN_HBM] *...  5.08 us
    ppermute x3, waiting for transfers between devices, swap(): lax.ppermute(array, axis, [(i, i ^ bit) for i in range(lax.axis_size(axis...  4.69 us
    ppermute x4, waiting for transfers between devices, shift(): lax.ppermute(array, axis, [(i, i + step) for i in range(count) if 0 <= i...  4.6 us
  transfers between devices with their start and end apart: 7, of which 5 were waited for; matrix products, arithmetic and copies ran while one was open for 0% of the time, Pallas kernels for 29%

commit v1 on v0

v1 whole, which is shorter than its diff:
```python
import functools
import math

import jax
import jax.numpy as jnp
from jax import lax
from jax.experimental import pallas as pl
from jax.experimental.pallas import tpu as pltpu
from jax.sharding import PartitionSpec as P

BF16 = jnp.bfloat16
F32 = jnp.float32
S = 64
DEPTH = 2
IN_VMEM = pl.BlockSpec(memory_space=pltpu.VMEM)
IN_HBM = pl.BlockSpec(memory_space=pltpu.HBM)


def dot(a, b):
    return jnp.dot(a, b, preferred_element_type=F32)


def dot_t(a, b):
    return lax.dot_general(a, b, (((1,), (1,)), ((), ())), preferred_element_type=F32)


def t_dot(a, b):
    return lax.dot_general(a, b, (((0,), (0,)), ((), ())), preferred_element_type=F32)


def in_hbm(array):
    return pltpu.with_memory_space_constraint(array, pltpu.HBM)


def params(mib):
    return pltpu.CompilerParams(vmem_limit_bytes=mib * 1024 * 1024)


def paired(ids):
    half = ids.shape[0] // 2
    return jnp.concatenate([ids[:half], ids[half:]], axis=1)


def pool_kernel(tile, f_ref, pm_ref, tm_ref, wq_ref, wk_ref, fv_ref, pv_ref, mv_ref, m_ref, pooled_ref, left_ref, right_ref, tv, wq, wk, sems):
    rows, span, chan = fv_ref.shape
    cy = span // tile
    small = [(tm_ref, tv), (wq_ref, wq), (wk_ref, wk), (pm_ref, pv_ref)]
    first = [pltpu.make_async_copy(src, dst, sems.at[rows + i]) for i, (src, dst) in enumerate(small)]
    beads_in = [pltpu.make_async_copy(f_ref.at[r], fv_ref.at[r], sems.at[r]) for r in range(rows)]
    for copy in first + beads_in:
        copy.start()
    block = lax.broadcasted_iota(jnp.int32, (18, 12 * tile), 1) // tile
    which = lax.broadcasted_iota(jnp.int32, (18, 12 * tile), 0)
    offset, second = which % 9, which // 9
    hit = (offset // 3 == block // 4) & (offset % 3 == block % 4 - second)
    pick = jnp.where(hit, 1 / math.sqrt(tile), 0.0).astype(BF16)
    for copy in first:
        copy.wait()
    m_ref[...] = (dot_t(wq[...], wk[...]) * (0.5 / math.sqrt(chan))).astype(BF16)
    mask = jnp.concatenate([tv[pl.ds(r, 9, stride=rows), :].astype(F32) for r in range(rows)], axis=1)
    even = lax.broadcasted_iota(jnp.int32, mask.shape, 1) % 2 == 0
    both = jnp.concatenate([jnp.where(even, mask, 0.0), jnp.where(even, 0.0, mask)], axis=0)
    mv_ref[...] = t_dot(both.astype(BF16), pick)

    node = lax.broadcasted_iota(jnp.int32, (S, 2 * tile), 0)
    order = [c for i in range(cy // 2) for c in (i, i + cy // 2)]
    total = jnp.zeros((S, chan), F32)
    for r in range(rows):
        pairs = paired(pv_ref[r])
        onehot = jnp.concatenate(
            [(jnp.broadcast_to(pairs[i : i + 1], node.shape) == node).astype(F32).astype(BF16) for i in range(cy // 2)],
            axis=1,
        )
        beads_in[r].wait()
        total += dot(onehot, jnp.concatenate([fv_ref[r, tile * c : tile * (c + 1)] for c in order], axis=0))
        left_ref[tile * r : tile * (r + 1)] = fv_ref[r, :tile]
        right_ref[tile * r : tile * (r + 1)] = fv_ref[r, span - tile :]
    pooled_ref[...] = (total * math.sqrt(S / (rows * span))).astype(BF16)


def pool(features, tile_mask, pool_map, w_query, w_key):
    cx, cy, tile, chan = features.shape
    span = cy * tile
    edge = pltpu.VMEM((cx * tile, chan), BF16)
    return pl.pallas_call(
        functools.partial(pool_kernel, tile),
        in_specs=[IN_HBM] * 5,
        out_specs=[IN_VMEM] * 7,
        out_shape=[
            pltpu.VMEM((cx, span, chan), BF16),
            pltpu.VMEM((cx, cy, tile), jnp.int32),
            pltpu.VMEM((cx * cy, 12 * tile), F32),
            pltpu.VMEM((chan, chan), BF16),
            pltpu.VMEM((S, chan), BF16),
            edge,
            edge,
        ],
        scratch_shapes=[
            pltpu.VMEM((9 * cx, cy), jnp.int32),
            pltpu.VMEM((chan, chan), BF16),
            pltpu.VMEM((chan, chan), BF16),
            pltpu.SemaphoreType.DMA((cx + 4,)),
        ],
        compiler_params=params(16),
        name="pool",
    )(
        in_hbm(features.reshape(cx, span, chan)),
        in_hbm(pool_map),
        in_hbm(jnp.transpose(tile_mask, (2, 0, 1)).reshape(9 * cx, cy)),
        in_hbm(w_query),
        in_hbm(w_key),
    )


def attend(tile, tasks):
    waiting = []

    def finish(task, weights):
        _, windows, _, store = task
        near = jnp.concatenate([window() for window in windows], axis=0)
        store(dot(jnp.concatenate(weights, axis=1), near).astype(BF16))

    for task in tasks:
        query, windows, masks, _ = task
        weights = []
        for r, window in enumerate(windows):
            half = dot_t(query, window()).astype(BF16)
            lanes = slice(4 * tile * r, 4 * tile * (r + 1))
            mask = jnp.concatenate([jnp.broadcast_to(masks(h, lanes), (tile, 4 * tile)) for h in (0, 1)], axis=0)
            weights.append((half * jnp.tanh(half) + half) * mask.astype(BF16))
        waiting.append((task, weights))
        if len(waiting) > DEPTH:
            finish(*waiting.pop(0))
    while waiting:
        finish(*waiting.pop(0))


def inner_tasks(refs, row, above, here, below):
    fv, pv, mv, m, o = refs
    _, span, chan = fv.shape
    cy, tile = pv.shape[1:]
    pairs = paired(pv[row])
    node = lax.broadcasted_iota(jnp.int32, (chan, 2 * tile), 0)
    for i in range(cy // 2):
        turned = (jnp.broadcast_to(pairs[i : i + 1], node.shape) == node).astype(F32).T.astype(BF16)
        o[row, tile * i : tile * (i + 1), chan:] = turned[:tile]
        o[row, span // 2 + tile * i : span // 2 + tile * (i + 1), chan:] = turned[tile:]
    queries = dot(here(2 * tile, span - 2 * tile), m[...]).astype(BF16)
    tasks = []
    for j in range(1, cy // 2 - 1):
        lo = 2 * tile * j

        def store(value, lo=lo):
            o[row, lo : lo + 2 * tile, :chan] = value

        tasks.append((
            queries[lo - 2 * tile : lo],
            [functools.partial(near, lo - tile, lo + 3 * tile) for near in (above, here, below)],
            lambda h, lanes, j=j: mv[pl.ds(row * cy + 2 * j + h, 1), lanes],
            store,
        ))
    return tasks


def rows_of(ref, row):
    return lambda lo, hi: ref[row, lo:hi]


def wide(tile, ref):
    return lambda lo, hi: ref[lo + tile : hi + tile]


def inner_kernel(first, count, fv, pv, mv, m, *rest):
    o = rest[-1]
    tile = pv.shape[2]
    refs = (fv, pv, mv, m, o)

    def body(row, many):
        tasks = []
        for k in range(many):
            tasks += inner_tasks(refs, row + k, rows_of(fv, row + k - 1), rows_of(fv, row + k), rows_of(fv, row + k + 1))
        attend(tile, tasks)

    if count // 2:

        @pl.loop(0, count // 2)
        def _(i):
            body(first + 2 * i, 2)

    if count % 2:
        body(first + count - 1, 1)


def ends_kernel(fv, pv, mv, m, out_in, above, below, o):
    tile = pv.shape[2]
    last = fv.shape[0] - 1
    refs = (fv, pv, mv, m, o)
    attend(
        tile,
        inner_tasks(refs, 0, wide(tile, above), rows_of(fv, 0), rows_of(fv, 1))
        + inner_tasks(refs, last, rows_of(fv, last - 1), rows_of(fv, last), wide(tile, below)),
    )


def sides_kernel(fv, pv, mv, m, out_in, above, below, left, right, *rest):
    o = rest[-1]
    rows, span, chan = fv.shape
    cy, tile = pv.shape[1:]
    side = 2 * tile
    tasks = []
    for row in range(rows):
        for j in (0, cy // 2 - 1):
            lo = side * j

            def window(r, j=j):
                if r in (-1, rows):
                    lo = 0 if j == 0 else span - 2 * tile
                    return (above if r < 0 else below)[lo : lo + 4 * tile]
                halo = (left if j == 0 else right)[tile * r : tile * (r + 1)]
                own = fv[r, : 3 * tile] if j == 0 else fv[r, span - 3 * tile :]
                return jnp.concatenate([halo, own] if j == 0 else [own, halo], axis=0)

            def store(value, row=row, lo=lo):
                o[row, lo : lo + side, :chan] = value

            tasks.append((
                dot(fv[row, lo : lo + side], m[...]).astype(BF16),
                [functools.partial(window, r) for r in (row - 1, row, row + 1)],
                lambda h, lanes, lo=row * cy + 2 * j: mv[lo + h : lo + h + 1, lanes],
                store,
            ))
    attend(tile, tasks)


def piece(kernel, rows_done, name, base, out, near=(), ties=()):
    fv, _, _, _ = base
    cx, span, chan = fv.shape
    done = [] if out is None else [out]
    return pl.pallas_call(
        kernel,
        in_specs=[IN_VMEM] * (4 + len(done) + len(near)) + [pl.BlockSpec(memory_space=pl.ANY)] * len(ties),
        out_specs=IN_VMEM,
        out_shape=pltpu.VMEM((cx, span, 2 * chan), BF16),
        input_output_aliases={4: 0} if done else {},
        compiler_params=params(16),
        cost_estimate=pl.CostEstimate(
            flops=int(rows_done * 1_200_000_000), bytes_accessed=1_000_000, transcendentals=0
        ),
        name=name,
    )(*base, *done, *near, *ties)


def final_kernel(nx, ny, n_blocks, *refs):
    blocks = refs[:n_blocks]
    readers_ref, wcq_ref, wck_ref, wcv_ref, wv_ref, o_ref, out_ref, mix, rows_out, sems = refs[n_blocks:]
    cx, span, chan = rows_out.shape
    nodes = jnp.concatenate([ref[...] for ref in blocks], axis=0)
    count = nodes.shape[0]
    mx, my = lax.axis_index("gx"), lax.axis_index("gy")
    block = lax.broadcasted_iota(jnp.int32, (readers_ref.shape[0], count), 1) // S
    rest = block // nx
    turn = (rest % (ny // 2)) * 2 + rest // (ny // 2)
    domain = ((block % nx) ^ mx) * ny + (turn ^ my)
    lane = lax.broadcasted_iota(jnp.int32, readers_ref.shape, 1)
    mine = jnp.sum(jnp.where(lane == mx * ny + my, readers_ref[...], 0), axis=1, keepdims=True)
    live = jnp.sum(jnp.where(domain == mine, 1.0, 0.0), axis=0, keepdims=True)
    query = dot(nodes[:S], wcq_ref[...]).astype(BF16)
    key = dot(nodes, wck_ref[...]).astype(BF16)
    value = dot(nodes, wcv_ref[...]).astype(BF16)
    half = dot_t(query, key) * (0.5 / math.sqrt(chan))
    weight = (half * jnp.tanh(half) + half).astype(BF16).astype(F32) * live
    mix[:chan] = wv_ref[...]
    mix[chan : chan + S] = (dot(weight.astype(BF16), value) / math.sqrt(S)).astype(BF16)
    mix[chan + S :] = jnp.zeros((chan - S, chan), BF16)

    def send(r):
        return pltpu.make_async_copy(rows_out.at[r], out_ref.at[r], sems.at[r])

    for r in range(cx):
        rows_out[r] = dot(o_ref[r], mix[...]).astype(BF16)
        send(r).start()
    for r in range(cx):
        send(r).wait()


def final(nx, ny, blocks, readers, w_cquery, w_ckey, w_cvalue, w_value, out):
    cx, span, wide = out.shape
    chan = wide // 2
    return pl.pallas_call(
        functools.partial(final_kernel, nx, ny, len(blocks)),
        in_specs=[IN_VMEM] * (len(blocks) + 6),
        out_specs=IN_HBM,
        out_shape=jax.ShapeDtypeStruct((cx, span, chan), BF16),
        scratch_shapes=[
            pltpu.VMEM((2 * chan, chan), BF16),
            pltpu.VMEM((cx, span, chan), BF16),
            pltpu.SemaphoreType.DMA((cx,)),
        ],
        compiler_params=params(16),
        name="final",
    )(*blocks, readers.T, w_cquery, w_ckey, w_cvalue, w_value, out)


def shift(array, axis, step):
    count = lax.axis_size(axis)
    return lax.ppermute(array, axis, [(i, i + step) for i in range(count) if 0 <= i + step < count])


def swap(array, axis, bits):
    return lax.ppermute(array, axis, [(i, i ^ bits) for i in range(lax.axis_size(axis))])


def join_kernel(count, *refs):
    parts, out = refs[:count], refs[-1]
    at = 0
    for part in parts:
        out[at : at + part.shape[0]] = part[...]
        at += part.shape[0]


def join(parts, ties):
    rows = sum(part.shape[0] for part in parts)
    return pl.pallas_call(
        functools.partial(join_kernel, len(parts)),
        in_specs=[IN_VMEM] * len(parts) + [pl.BlockSpec(memory_space=pl.ANY)] * len(ties),
        out_specs=IN_VMEM,
        out_shape=pltpu.VMEM((rows, parts[0].shape[1]), BF16),
        compiler_params=params(4),
        name="join",
    )(*parts, *ties)


def edge_rows_kernel(tile, fv_ref, left_ref, right_ref, up_ref, down_ref):
    rows, span, _ = fv_ref.shape
    for ref, r in ((up_ref, rows - 1), (down_ref, 0)):
        ref[:tile] = left_ref[tile * r : tile * (r + 1)]
        ref[tile : tile + span] = fv_ref[r]
        ref[tile + span :] = right_ref[tile * r : tile * (r + 1)]


def edge_rows(tile, fv, left, right):
    _, span, chan = fv.shape
    edge = pltpu.VMEM((span + 2 * tile, chan), BF16)
    return pl.pallas_call(
        functools.partial(edge_rows_kernel, tile),
        in_specs=[IN_VMEM] * 3,
        out_specs=[IN_VMEM] * 2,
        out_shape=[edge, edge],
        compiler_params=params(4),
        name="edge_rows",
    )(fv, left, right)


def per_device(features, tile_mask, pool_map, readers, w_query, w_key, w_value, w_cquery, w_ckey, w_cvalue):
    cx, cy, tile, chan = features.shape
    nx, ny = lax.axis_size("gx"), lax.axis_size("gy")
    *base, pooled, left_edge, right_edge = pool(features, tile_mask, pool_map, w_query, w_key)
    fv = base[0]

    def inner(first, count, out, ties):
        return piece(functools.partial(inner_kernel, first, count), 0.75 * count, f"inner_{first}", base, out, (), ties)

    cuts = [1, 1 + (cx - 2) * 4 // 14, 1 + (cx - 2) * 10 // 14, cx - 1]
    blocks = [pooled] + [swap(pooled, "gx", bits) for bits in range(1, nx)]
    left = shift(right_edge, "gy", 1)
    right = shift(left_edge, "gy", -1)
    out = inner(cuts[0], cuts[1] - cuts[0], None, ())
    part = join(blocks, (out,))
    blocks = [part] + [swap(part, "gy", bits) for bits in range(2, ny, 2)]
    up, down = edge_rows(tile, fv, left, right)
    above = shift(up, "gx", 1)
    below = shift(down, "gx", -1)
    out = inner(cuts[1], cuts[2] - cuts[1], out, (part, up))
    part = join(blocks, (out,))
    blocks = [part, swap(part, "gy", 1)]
    out = inner(cuts[2], cuts[3] - cuts[2], out, (part,))
    out = piece(ends_kernel, 1.5, "ends", base, out, (above, below))
    out = piece(sides_kernel, 4, "sides", base, out, (above, below, left, right))
    update = final(nx, ny, blocks, readers, w_cquery, w_ckey, w_cvalue, w_value, out)
    return update.reshape(features.shape)


def solution(mesh):
    in_specs = (P("gx", "gy", None, None), P("gx", "gy", None), P("gx", "gy", None)) + (P(),) * 7
    return jax.shard_map(
        per_device, mesh=mesh, in_specs=in_specs, out_specs=P("gx", "gy", None, None), check_vma=False
    )
```

time: 57.5 us -> 50.6 us (0.88)
  the two profiles are of different devices: /device:TPU:0 before, /device:TPU:18 now
where the time goes in v1:
time: 50.6 us; the launch traced here: 50.4 us
  Pallas kernels  25 us (49%)
  starting transfers between devices  19.5 us (39%)
  waiting for transfers between devices  5.43 us (11%)
    pallas_call x5, Pallas kernels, piece(): pl.pallas_call(kernel, in_specs=[IN_VMEM] * (4 + len(done) + len(near)) +...  16.4 us
    ppermute x4, starting transfers between devices, shift(): lax.ppermute(array, axis, [(i, i + step) for i in range(count) if 0 <= i...  12 us
    ppermute x7, starting transfers between devices, swap(): lax.ppermute(array, axis, [(i, i ^ bits) for i in range(lax.axis_size(axi...  7.46 us
    ppermute x4, waiting for transfers between devices, shift(): lax.ppermute(array, axis, [(i, i + step) for i in range(count) if 0 <= i...  5.42 us
    pallas_call x1, Pallas kernels, pool(): pl.pallas_call(functools.partial(pool_kernel, tile), in_specs=[IN_HBM] *...  4.48 us
    pallas_call x1, Pallas kernels, final(): pl.pallas_call(functools.partial(final_kernel, nx, ny, len(blocks)), in_s...  4.07 us
  transfers between devices with their start and end apart: 11, of which 2 were waited for; matrix products, arithmetic and copies ran while one was open for 0% of the time, Pallas kernels for 33%

profile of v1, /device:TPU:18, one launch (start us, length us, event | category | flops | bytes accessed | tf_op | source)
XLA Modules:
  0.0 50.4 jit_solution(8239156138217469753)
XLA Ops:
  0.0 4.5 %pool.1 = (bf16[16,1024,128]{2,1,0:T(8,128)(2,1)S(1)}, s32[16,16,64]{2,1,0:T(8,128)S(1)}, f32[256,768]{1,0:T(8,128)S(1)}, bf16[128,128]{1,0:T(8,128)(2,1)S(1)}, ...) custom-call(bf16[16,1024,128]{2,1,0:T(8,128)(2,1)} %bitcast.7, ...), custom_call_target="tpu_custom_call" | custom-call | tf_op jit(solution)/shard_map/pool/pallas_call | solution.py:85
  4.5 1.6 %collective-permute-start = (bf16[64,128]{1,0:T(8,128)(2,1)S(1)}, bf16[64,128]{1,0:T(8,128)(2,1)S(1)}, u32[]{:S(2)}, u32[]{:S(2)}) collective-permute-start(bf16[64,128]{1,0:T(8,128)(2,1)S(1)} %get-tuple-element.14.refs_0_), channel_id=1, source_target_pairs={{0,8},{8,0},{16,24},{24,16},{1,9},{9,1},{17,25},{25,17},{2,10},{10... | collective-permute-start | bytes 49160 | tf_op jit(solution)/shard_map/ppermute | solution.py:310
  6.1 0.3 collective-permute-start.1
  6.5 1.6 %collective-permute-start.2 = (bf16[64,128]{1,0:T(8,128)(2,1)S(1)}, bf16[64,128]{1,0:T(8,128)(2,1)S(1)}, u32[]{:S(2)}, u32[]{:S(2)}) collective-permute-start(bf16[64,128]{1,0:T(8,128)(2,1)S(1)} %get-tuple-element.14.refs_0_), channel_id=1, source_target_pairs={{0,24},{8,16},{16,8},{24,0},{1,25},{9,17},{17,9},{25,1},{2,26},{10... | collective-permute-start | bytes 49160 | tf_op jit(solution)/shard_map/ppermute | solution.py:310
  8.0 1.9 %collective-permute-start.6 = (bf16[1024,128]{1,0:T(8,128)(2,1)S(1)}, bf16[1024,128]{1,0:T(8,128)(2,1)S(1)}, u32[]{:S(2)}, u32[]{:S(2)}) collective-permute-start(bf16[1024,128]{1,0:T(8,128)(2,1)S(1)} %get-tuple-element.19), channel_id=1, source_target_pairs={{0,1},{1,2},{2,3},{3,4},{4,5},{5,6},{6,7},{8,9},{9,10},{10,11},{11... | collective-permute-start | bytes 786440 | tf_op jit(solution)/shard_map/ppermute | solution.py:306
  10.0 3.6 %collective-permute-start.7 = (bf16[1024,128]{1,0:T(8,128)(2,1)S(1)}, bf16[1024,128]{1,0:T(8,128)(2,1)S(1)}, u32[]{:S(2)}, u32[]{:S(2)}) collective-permute-start(bf16[1024,128]{1,0:T(8,128)(2,1)S(1)} %get-tuple-element.20), channel_id=1, source_target_pairs={{1,0},{2,1},{3,2},{4,3},{5,4},{6,5},{7,6},{9,8},{10,9},{11,10},{12... | collective-permute-start | bytes 786440 | tf_op jit(solution)/shard_map/ppermute | solution.py:306
  13.6 3.2 %inner_1.1.refs_4_.rest_0_ = bf16[16,1024,256]{2,1,0:T(8,128)(2,1)S(1)} custom-call(bf16[16,1024,128]{2,1,0:T(8,128)(2,1)S(1)} %get-tuple-element.15.fv.fv_ref, s32[16,16,64]{2,1,0:T(8,128)S(1)} %get-tuple-element.16.pv, f32[256,768]{1,0:T(8,128)S(1)} %get-tuple-element.17.mv, bf16[128,128]{1,0:T(8,128)(2,1)S(1)} %get-tuple-element.18.m), custom_call_target="tpu_custom_call" | custom-call | flops 3600000000 | bytes 1000000 | tf_op jit(solution)/shard_map/inner_1/pallas_call | solution.py:239
  16.8 0.1 collective-permute-start.3
  16.9 2.9 %collective-permute-start.4 = (bf16[256,128]{1,0:T(8,128)(2,1)S(1)}, bf16[256,128]{1,0:T(8,128)(2,1)S(1)}, u32[]{:S(2)}, u32[]{:S(2)}) collective-permute-start(bf16[256,128]{1,0:T(8,128)(2,1)S(1)} %join.2.rest_1_.refs_0_), channel_id=1, source_target_pairs={{0,4},{1,5},{2,6},{3,7},{4,0},{5,1},{6,2},{7,3},{8,12},{9,13},{10,... | collective-permute-start | bytes 196616 | tf_op jit(solution)/shard_map/ppermute | solution.py:310
  19.8 0.5 %collective-permute-start.5 = (bf16[256,128]{1,0:T(8,128)(2,1)S(1)}, bf16[256,128]{1,0:T(8,128)(2,1)S(1)}, u32[]{:S(2)}, u32[]{:S(2)}) collective-permute-start(bf16[256,128]{1,0:T(8,128)(2,1)S(1)} %join.2.rest_1_.refs_0_), channel_id=1, source_target_pairs={{0,6},{1,7},{2,4},{3,5},{4,2},{5,3},{6,0},{7,1},{8,14},{9,15},{10,... | collective-permute-start | bytes 196616 | tf_op jit(solution)/shard_map/ppermute | solution.py:310
  20.4 4.7 %inner_5.1.refs_4_.rest_0_ = bf16[16,1024,256]{2,1,0:T(8,128)(2,1)S(1)} custom-call(bf16[16,1024,128]{2,1,0:T(8,128)(2,1)S(1)} %get-tuple-element.15.fv.fv_ref, s32[16,16,64]{2,1,0:T(8,128)S(1)} %get-tuple-element.16.pv, f32[256,768]{1,0:T(8,128)S(1)} %get-tuple-element.17.mv, ...), custom_call_target="tpu_custom_call", output_to_operand_aliasing={{}: (4, {})} | custom-call | flops 5400000000 | bytes 1000000 | tf_op jit(solution)/shard_map/inner_5/pallas_call | solution.py:239
  25.2 4.4 %collective-permute-start.9 = (bf16[1152,128]{1,0:T(8,128)(2,1)S(1)}, bf16[1152,128]{1,0:T(8,128)(2,1)S(1)}, u32[]{:S(2)}, u32[]{:S(2)}) collective-permute-start(bf16[1152,128]{1,0:T(8,128)(2,1)S(1)} %get-tuple-element.21.rest_2_), channel_id=1, source_target_pairs={{0,8},{8,16},{16,24},{1,9},{9,17},{17,25},{2,10},{10,18},{18,26},{... | collective-permute-start | bytes 884744 | tf_op jit(solution)/shard_map/ppermute | solution.py:306
  29.6 2.1 %collective-permute-start.10 = (bf16[1152,128]{1,0:T(8,128)(2,1)S(1)}, bf16[1152,128]{1,0:T(8,128)(2,1)S(1)}, u32[]{:S(2)}, u32[]{:S(2)}) collective-permute-start(bf16[1152,128]{1,0:T(8,128)(2,1)S(1)} %get-tuple-element.22), channel_id=1, source_target_pairs={{8,0},{16,8},{24,16},{9,1},{17,9},{25,17},{10,2},{18,10},{26,18},{... | collective-permute-start | bytes 884744 | tf_op jit(solution)/shard_map/ppermute | solution.py:306
  31.7 0.4 collective-permute-start.8
  32.1 3.2 %inner_11.1.out_in = bf16[16,1024,256]{2,1,0:T(8,128)(2,1)S(1)} custom-call(bf16[16,1024,128]{2,1,0:T(8,128)(2,1)S(1)} %get-tuple-element.15.fv.fv_ref, s32[16,16,64]{2,1,0:T(8,128)S(1)} %get-tuple-element.16.pv, f32[256,768]{1,0:T(8,128)S(1)} %get-tuple-element.17.mv, bf16[128,128]{1,0:T(8,128)(2,1)S(1)} %get-tuple-element.18.m, ...), custom_call_target="tpu_custom_call", output_to_operand_aliasing={{}: (4, {})} | custom-call | flops 3600000000 | bytes 1000000 | tf_op jit(solution)/shard_map/inner_11/pallas_call | solution.py:239
  35.2 1.3 %collective-permute-done.9.above = bf16[1152,128]{1,0:T(8,128)(2,1)S(1)} collective-permute-done((bf16[1152,128]{1,0:T(8,128)(2,1)S(1)}, bf16[1152,128]{1,0:T(8,128)(2,1)S(1)}, u32[]{:S(2)}, u32[]{:S(2)}) %collective-permute-start.9) | collective-permute-done | bytes 294944 | tf_op jit(solution)/shard_map/ppermute | solution.py:306
  36.5 4.1 %collective-permute-done.10.below = bf16[1152,128]{1,0:T(8,128)(2,1)S(1)} collective-permute-done((bf16[1152,128]{1,0:T(8,128)(2,1)S(1)}, bf16[1152,128]{1,0:T(8,128)(2,1)S(1)}, u32[]{:S(2)}, u32[]{:S(2)}) %collective-permute-start.10) | collective-permute-done | bytes 294944 | tf_op jit(solution)/shard_map/ppermute | solution.py:306
  40.7 1.6 %ends.1.out_in = bf16[16,1024,256]{2,1,0:T(8,128)(2,1)S(1)} custom-call(bf16[16,1024,128]{2,1,0:T(8,128)(2,1)S(1)} %get-tuple-element.15.fv.fv_ref, s32[16,16,64]{2,1,0:T(8,128)S(1)} %get-tuple-element.16.pv, f32[256,768]{1,0:T(8,128)S(1)} %get-tuple-element.17.mv, bf16[128,128]{1,0:T(8,128)(2,1)S(1)} %get-tuple-element.18.m, ...), custom_call_target="tpu_custom_call", output_to_operand_aliasing={{}: (4, {})} | custom-call | flops 1800000000 | bytes 1000000 | tf_op jit(solution)/shard_map/ends/pallas_call | solution.py:239
  42.2 0.0 copy-start
  42.2 0.0 copy-start.1
  42.3 0.0 copy-start.2
  42.3 0.0 copy-start.4
  42.3 3.8 %sides.1.refs_7_ = bf16[16,1024,256]{2,1,0:T(8,128)(2,1)S(1)} custom-call(bf16[16,1024,128]{2,1,0:T(8,128)(2,1)S(1)} %get-tuple-element.15.fv.fv_ref, s32[16,16,64]{2,1,0:T(8,128)S(1)} %get-tuple-element.16.pv, f32[256,768]{1,0:T(8,128)S(1)} %get-tuple-element.17.mv, bf16[128,128]{1,0:T(8,128)(2,1)S(1)} %get-tuple-element.18.m, ...), custom_call_target="tpu_custom_call", output_to_operand_aliasing={{}: (4, {})} | custom-call | flops 4800000000 | bytes 1000000 | tf_op jit(solution)/shard_map/sides/pallas_call | solution.py:239
  46.2 4.1 %final.1 = bf16[16,1024,128]{2,1,0:T(8,128)(2,1)} custom-call(bf16[1024,128]{1,0:T(8,128)(2,1)S(1)} %join.3.rest_1_.refs_0_, bf16[1024,128]{1,0:T(8,128)(2,1)S(1)} %collective-permute-done.8.refs_1_, s32[8,32]{1,0:T(8,128)S(1)} %bitcast.6, bf16[128,128]{1,0:T(8,128)(2,1)S(1)} %copy-done, bf16[128,128]{1,0:T(8,128)(2,1)S(1)} %copy-done.1, ...), custom_call_target="tpu_custom_call" | custom-call | tf_op jit(solution)/shard_map/final/pallas_call | solution.py:289
  (18 shorter events, 0.1 us)
Async XLA Ops:
  4.5 12.3 %collective-permute-start = (bf16[64,128]{1,0:T(8,128)(2,1)S(1)}, bf16[64,128]{1,0:T(8,128)(2,1)S(1)}, u32[]{:S(2)}, u32[]{:S(2)}) collective-permute-start(bf16[64,128]{1,0:T(8,128)(2,1)S(1)} %get-tuple-element.14.refs_0_), channel_id=1, source_target_pairs={{0,8},{8,0},{16,24},{24,16},{1,9},{9,1},{17,25},{25,17},{2,10},{10... | collective-permute-start | bytes 49160 | tf_op jit(solution)/shard_map/ppermute | solution.py:310
  6.1 10.7 %collective-permute-start.1 = (bf16[64,128]{1,0:T(8,128)(2,1)S(1)}, bf16[64,128]{1,0:T(8,128)(2,1)S(1)}, u32[]{:S(2)}, u32[]{:S(2)}) collective-permute-start(bf16[64,128]{1,0:T(8,128)(2,1)S(1)} %get-tuple-element.14.refs_0_), channel_id=1, source_target_pairs={{0,16},{8,24},{16,0},{24,8},{1,17},{9,25},{17,1},{25,9},{2,18},{10... | collective-permute-start | bytes 49160 | tf_op jit(solution)/shard_map/ppermute | solution.py:310
  6.5 10.3 %collective-permute-start.2 = (bf16[64,128]{1,0:T(8,128)(2,1)S(1)}, bf16[64,128]{1,0:T(8,128)(2,1)S(1)}, u32[]{:S(2)}, u32[]{:S(2)}) collective-permute-start(bf16[64,128]{1,0:T(8,128)(2,1)S(1)} %get-tuple-element.14.refs_0_), channel_id=1, source_target_pairs={{0,24},{8,16},{16,8},{24,0},{1,25},{9,17},{17,9},{25,1},{2,26},{10... | collective-permute-start | bytes 49160 | tf_op jit(solution)/shard_map/ppermute | solution.py:310
  8.0 12.3 %collective-permute-start.6 = (bf16[1024,128]{1,0:T(8,128)(2,1)S(1)}, bf16[1024,128]{1,0:T(8,128)(2,1)S(1)}, u32[]{:S(2)}, u32[]{:S(2)}) collective-permute-start(bf16[1024,128]{1,0:T(8,128)(2,1)S(1)} %get-tuple-element.19), channel_id=1, source_target_pairs={{0,1},{1,2},{2,3},{3,4},{4,5},{5,6},{6,7},{8,9},{9,10},{10,11},{11... | collective-permute-start | bytes 786440 | tf_op jit(solution)/shard_map/ppermute | solution.py:306
  10.0 10.4 %collective-permute-start.7 = (bf16[1024,128]{1,0:T(8,128)(2,1)S(1)}, bf16[1024,128]{1,0:T(8,128)(2,1)S(1)}, u32[]{:S(2)}, u32[]{:S(2)}) collective-permute-start(bf16[1024,128]{1,0:T(8,128)(2,1)S(1)} %get-tuple-element.20), channel_id=1, source_target_pairs={{1,0},{2,1},{3,2},{4,3},{5,4},{6,5},{7,6},{9,8},{10,9},{11,10},{12... | collective-permute-start | bytes 786440 | tf_op jit(solution)/shard_map/ppermute | solution.py:306
  16.8 14.9 %collective-permute-start.3 = (bf16[256,128]{1,0:T(8,128)(2,1)S(1)}, bf16[256,128]{1,0:T(8,128)(2,1)S(1)}, u32[]{:S(2)}, u32[]{:S(2)}) collective-permute-start(bf16[256,128]{1,0:T(8,128)(2,1)S(1)} %join.2.rest_1_.refs_0_), channel_id=1, source_target_pairs={{0,2},{1,3},{2,0},{3,1},{4,6},{5,7},{6,4},{7,5},{8,10},{9,11},{10,... | collective-permute-start | bytes 196616 | tf_op jit(solution)/shard_map/ppermute | solution.py:310
  16.9 14.8 %collective-permute-start.4 = (bf16[256,128]{1,0:T(8,128)(2,1)S(1)}, bf16[256,128]{1,0:T(8,128)(2,1)S(1)}, u32[]{:S(2)}, u32[]{:S(2)}) collective-permute-start(bf16[256,128]{1,0:T(8,128)(2,1)S(1)} %join.2.rest_1_.refs_0_), channel_id=1, source_target_pairs={{0,4},{1,5},{2,6},{3,7},{4,0},{5,1},{6,2},{7,3},{8,12},{9,13},{10,... | collective-permute-start | bytes 196616 | tf_op jit(solution)/shard_map/ppermute | solution.py:310
  19.8 11.8 %collective-permute-start.5 = (bf16[256,128]{1,0:T(8,128)(2,1)S(1)}, bf16[256,128]{1,0:T(8,128)(2,1)S(1)}, u32[]{:S(2)}, u32[]{:S(2)}) collective-permute-start(bf16[256,128]{1,0:T(8,128)(2,1)S(1)} %join.2.rest_1_.refs_0_), channel_id=1, source_target_pairs={{0,6},{1,7},{2,4},{3,5},{4,2},{5,3},{6,0},{7,1},{8,14},{9,15},{10,... | collective-permute-start | bytes 196616 | tf_op jit(solution)/shard_map/ppermute | solution.py:310
  25.2 11.4 %collective-permute-start.9 = (bf16[1152,128]{1,0:T(8,128)(2,1)S(1)}, bf16[1152,128]{1,0:T(8,128)(2,1)S(1)}, u32[]{:S(2)}, u32[]{:S(2)}) collective-permute-start(bf16[1152,128]{1,0:T(8,128)(2,1)S(1)} %get-tuple-element.21.rest_2_), channel_id=1, source_target_pairs={{0,8},{8,16},{16,24},{1,9},{9,17},{17,25},{2,10},{10,18},{18,26},{... | collective-permute-start | bytes 884744 | tf_op jit(solution)/shard_map/ppermute | solution.py:306
  29.6 11.1 %collective-permute-start.10 = (bf16[1152,128]{1,0:T(8,128)(2,1)S(1)}, bf16[1152,128]{1,0:T(8,128)(2,1)S(1)}, u32[]{:S(2)}, u32[]{:S(2)}) collective-permute-start(bf16[1152,128]{1,0:T(8,128)(2,1)S(1)} %get-tuple-element.22), channel_id=1, source_target_pairs={{8,0},{16,8},{24,16},{9,1},{17,9},{25,17},{10,2},{18,10},{26,18},{... | collective-permute-start | bytes 884744 | tf_op jit(solution)/shard_map/ppermute | solution.py:306
  31.7 14.4 %collective-permute-start.8 = (bf16[1024,128]{1,0:T(8,128)(2,1)S(1)}, bf16[1024,128]{1,0:T(8,128)(2,1)S(1)}, u32[]{:S(2)}, u32[]{:S(2)}) collective-permute-start(bf16[1024,128]{1,0:T(8,128)(2,1)S(1)} %join.3.rest_1_.refs_0_), channel_id=1, source_target_pairs={{0,1},{1,0},{2,3},{3,2},{4,5},{5,4},{6,7},{7,6},{8,9},{9,8},{10,11... | collective-permute-start | bytes 786440 | tf_op jit(solution)/shard_map/ppermute | solution.py:310
  42.2 3.9 %copy-start = (bf16[128,128]{1,0:T(8,128)(2,1)S(1)}, bf16[128,128]{1,0:T(8,128)(2,1)}, u32[]{:S(2)}) copy-start(bf16[128,128]{1,0:T(8,128)(2,1)} %refs_3_.1) | copy-start | bytes 98308
  42.2 3.9 %copy-start.1 = (bf16[128,128]{1,0:T(8,128)(2,1)S(1)}, bf16[128,128]{1,0:T(8,128)(2,1)}, u32[]{:S(2)}) copy-start(bf16[128,128]{1,0:T(8,128)(2,1)} %refs_4_.1) | copy-start | bytes 98308
  42.3 3.9 %copy-start.2 = (bf16[128,128]{1,0:T(8,128)(2,1)S(1)}, bf16[128,128]{1,0:T(8,128)(2,1)}, u32[]{:S(2)}) copy-start(bf16[128,128]{1,0:T(8,128)(2,1)} %refs_5_.1) | copy-start | bytes 98308
  42.3 3.9 %copy-start.3 = (bf16[128,128]{1,0:T(8,128)(2,1)S(1)}, bf16[128,128]{1,0:T(8,128)(2,1)}, u32[]{:S(2)}) copy-start(bf16[128,128]{1,0:T(8,128)(2,1)} %refs_6_.1) | copy-start | bytes 98308
  42.3 3.9 %copy-start.4 = (s32[32,8]{0,1:T(8,128)S(1)}, s32[32,8]{0,1:T(8,128)}, u32[]{:S(2)}) copy-start(s32[32,8]{0,1:T(8,128)} %param.13) | copy-start | bytes 3076

commit v2 on v1

--- a/solution.py
+++ b/solution.py
@@ -41,7 +41,7 @@
     return jnp.concatenate([ids[:half], ids[half:]], axis=1)
 
 
-def pool_kernel(tile, f_ref, pm_ref, tm_ref, wq_ref, wk_ref, fv_ref, pv_ref, mv_ref, m_ref, pooled_ref, left_ref, right_ref, tv, wq, wk, sems):
+def pool_kernel(tile, nx, ny, f_ref, pm_ref, tm_ref, wq_ref, wk_ref, fv_ref, pv_ref, mv_ref, m_ref, pooled_ref, left_ref, right_ref, tv, wq, wk, sems):
     rows, span, chan = fv_ref.shape
     cy = span // tile
     small = [(tm_ref, tv), (wq_ref, wq), (wk_ref, wk), (pm_ref, pv_ref)]
@@ -58,7 +58,15 @@
         copy.wait()
     m_ref[...] = (dot_t(wq[...], wk[...]) * (0.5 / math.sqrt(chan))).astype(BF16)
     mask = jnp.concatenate([tv[pl.ds(r, 9, stride=rows), :].astype(F32) for r in range(rows)], axis=1)
-    even = lax.broadcasted_iota(jnp.int32, mask.shape, 1) % 2 == 0
+    lane = lax.broadcasted_iota(jnp.int32, mask.shape, 1)
+    toward = lax.broadcasted_iota(jnp.int32, mask.shape, 0)
+    mx, my = lax.axis_index("gx"), lax.axis_index("gy")
+    outside = (toward // 3 == 0) & (lane // cy == jnp.where(mx == 0, 0, -1))
+    outside |= (toward // 3 == 2) & (lane // cy == jnp.where(mx == nx - 1, rows - 1, -1))
+    outside |= (toward % 3 == 0) & (lane % cy == jnp.where(my == 0, 0, -1))
+    outside |= (toward % 3 == 2) & (lane % cy == jnp.where(my == ny - 1, cy - 1, -1))
+    mask = jnp.where(outside, 0.0, mask)
+    even = lane % 2 == 0
     both = jnp.concatenate([jnp.where(even, mask, 0.0), jnp.where(even, 0.0, mask)], axis=0)
     mv_ref[...] = t_dot(both.astype(BF16), pick)
 
@@ -78,12 +86,12 @@
     pooled_ref[...] = (total * math.sqrt(S / (rows * span))).astype(BF16)
 
 
-def pool(features, tile_mask, pool_map, w_query, w_key):
+def pool(nx, ny, features, tile_mask, pool_map, w_query, w_key):
     cx, cy, tile, chan = features.shape
     span = cy * tile
     edge = pltpu.VMEM((cx * tile, chan), BF16)
     return pl.pallas_call(
-        functools.partial(pool_kernel, tile),
+        functools.partial(pool_kernel, tile, nx, ny),
         in_specs=[IN_HBM] * 5,
         out_specs=[IN_VMEM] * 7,
         out_shape=[
@@ -135,8 +143,29 @@
         finish(*waiting.pop(0))
 
 
-def inner_tasks(refs, row, above, here, below):
+def row_tasks(refs, row, first, last, window):
     fv, pv, mv, m, o = refs
+    chan = fv.shape[2]
+    cy, tile = pv.shape[1:]
+    side = 2 * tile
+    queries = dot(fv[row, side * first : side * last], m[...]).astype(BF16)
+    tasks = []
+    for j in range(first, last):
+
+        def store(value, lo=side * j):
+            o[row, lo : lo + side, :chan] = value
+
+        tasks.append((
+            queries[side * (j - first) : side * (j - first + 1)],
+            [functools.partial(window, r, j) for r in (row - 1, row, row + 1)],
+            lambda h, lanes, j=j: mv[pl.ds(row * cy + 2 * j + h, 1), lanes],
+            store,
+        ))
+    return tasks
+
+
+def node_rows(refs, row):
+    fv, pv, _, _, o = refs
     _, span, chan = fv.shape
     cy, tile = pv.shape[1:]
     pairs = paired(pv[row])
@@ -145,40 +174,20 @@
         turned = (jnp.broadcast_to(pairs[i : i + 1], node.shape) == node).astype(F32).T.astype(BF16)
         o[row, tile * i : tile * (i + 1), chan:] = turned[:tile]
         o[row, span // 2 + tile * i : span // 2 + tile * (i + 1), chan:] = turned[tile:]
-    queries = dot(here(2 * tile, span - 2 * tile), m[...]).astype(BF16)
-    tasks = []
-    for j in range(1, cy // 2 - 1):
-        lo = 2 * tile * j
-
-        def store(value, lo=lo):
-            o[row, lo : lo + 2 * tile, :chan] = value
-
-        tasks.append((
-            queries[lo - 2 * tile : lo],
-            [functools.partial(near, lo - tile, lo + 3 * tile) for near in (above, here, below)],
-            lambda h, lanes, j=j: mv[pl.ds(row * cy + 2 * j + h, 1), lanes],
-            store,
-        ))
-    return tasks
-
-
-def rows_of(ref, row):
-    return lambda lo, hi: ref[row, lo:hi]
-
-
-def wide(tile, ref):
-    return lambda lo, hi: ref[lo + tile : hi + tile]
 
 
 def inner_kernel(first, count, fv, pv, mv, m, *rest):
-    o = rest[-1]
-    tile = pv.shape[2]
-    refs = (fv, pv, mv, m, o)
+    cy, tile = pv.shape[1:]
+    refs = (fv, pv, mv, m, rest[-1])
+
+    def window(r, j):
+        return fv[r, tile * (2 * j - 1) : tile * (2 * j + 3)]
 
     def body(row, many):
         tasks = []
         for k in range(many):
-            tasks += inner_tasks(refs, row + k, rows_of(fv, row + k - 1), rows_of(fv, row + k), rows_of(fv, row + k + 1))
+            node_rows(refs, row + k)
+            tasks += row_tasks(refs, row + k, 1, cy // 2 - 1, window)
         attend(tile, tasks)
 
     if count // 2:
@@ -191,44 +200,45 @@
         body(first + count - 1, 1)
 
 
-def ends_kernel(fv, pv, mv, m, out_in, above, below, o):
-    tile = pv.shape[2]
-    last = fv.shape[0] - 1
+def side_window(fv, tile, left, right):
+    span = fv.shape[1]
+
+    def window(r, j):
+        if j == 0:
+            return jnp.concatenate([left[tile * r : tile * (r + 1)], fv[r, : 3 * tile]], axis=0)
+        if 2 * tile * (j + 1) == span:
+            return jnp.concatenate([fv[r, span - 3 * tile :], right[tile * r : tile * (r + 1)]], axis=0)
+        return fv[r, tile * (2 * j - 1) : tile * (2 * j + 3)]
+
+    return window
+
+
+def sides_kernel(fv, pv, mv, m, out_in, left, right, o):
+    cy, tile = pv.shape[1:]
     refs = (fv, pv, mv, m, o)
-    attend(
-        tile,
-        inner_tasks(refs, 0, wide(tile, above), rows_of(fv, 0), rows_of(fv, 1))
-        + inner_tasks(refs, last, rows_of(fv, last - 1), rows_of(fv, last), wide(tile, below)),
-    )
-
-
-def sides_kernel(fv, pv, mv, m, out_in, above, below, left, right, *rest):
-    o = rest[-1]
-    rows, span, chan = fv.shape
-    cy, tile = pv.shape[1:]
-    side = 2 * tile
+    window = side_window(fv, tile, left, right)
     tasks = []
-    for row in range(rows):
+    for row in range(1, fv.shape[0] - 1):
         for j in (0, cy // 2 - 1):
-            lo = side * j
-
-            def window(r, j=j):
-                if r in (-1, rows):
-                    lo = 0 if j == 0 else span - 2 * tile
-                    return (above if r < 0 else below)[lo : lo + 4 * tile]
-                halo = (left if j == 0 else right)[tile * r : tile * (r + 1)]
-                own = fv[r, : 3 * tile] if j == 0 else fv[r, span - 3 * tile :]
-                return jnp.concatenate([halo, own] if j == 0 else [own, halo], axis=0)
-
-            def store(value, row=row, lo=lo):
-                o[row, lo : lo + side, :chan] = value
-
-            tasks.append((
-                dot(fv[row, lo : lo + side], m[...]).astype(BF16),
-                [functools.partial(window, r) for r in (row - 1, row, row + 1)],
-                lambda h, lanes, lo=row * cy + 2 * j: mv[lo + h : lo + h + 1, lanes],
-                store,
-            ))
+            tasks += row_tasks(refs, row, j, j + 1, window)
+    attend(tile, tasks)
+
+
+def ends_kernel(fv, pv, mv, m, out_in, left, right, above, below, o):
+    cy, tile = pv.shape[1:]
+    rows = fv.shape[0]
+    refs = (fv, pv, mv, m, o)
+    near = side_window(fv, tile, left, right)
+
+    def window(r, j):
+        if r in (-1, rows):
+            return (above if r < 0 else below)[2 * tile * j : 2 * tile * (j + 2)]
+        return near(r, j)
+
+    tasks = []
+    for row in (0, rows - 1):
+        node_rows(refs, row)
+        tasks += row_tasks(refs, row, 0, cy // 2, window)
     attend(tile, tasks)
 
 
@@ -244,7 +254,7 @@
         input_output_aliases={4: 0} if done else {},
         compiler_params=params(16),
         cost_estimate=pl.CostEstimate(
-            flops=int(rows_done * 1_200_000_000), bytes_accessed=1_000_000, transcendentals=0
+            flops=int(rows_done * 400_000_000), bytes_accessed=1_000_000, transcendentals=0
         ),
         name=name,
     )(*base, *done, *near, *ties)
@@ -303,7 +313,7 @@
 
 def shift(array, axis, step):
     count = lax.axis_size(axis)
-    return lax.ppermute(array, axis, [(i, i + step) for i in range(count) if 0 <= i + step < count])
+    return lax.ppermute(array, axis, [(i, (i + step) % count) for i in range(count)])
 
 
 def swap(array, axis, bits):
@@ -354,7 +364,7 @@
 def per_device(features, tile_mask, pool_map, readers, w_query, w_key, w_value, w_cquery, w_ckey, w_cvalue):
     cx, cy, tile, chan = features.shape
     nx, ny = lax.axis_size("gx"), lax.axis_size("gy")
-    *base, pooled, left_edge, right_edge = pool(features, tile_mask, pool_map, w_query, w_key)
+    *base, pooled, left_edge, right_edge = pool(nx, ny, features, tile_mask, pool_map, w_query, w_key)
     fv = base[0]
 
     def inner(first, count, out, ties):
@@ -374,8 +384,8 @@
     part = join(blocks, (out,))
     blocks = [part, swap(part, "gy", 1)]
     out = inner(cuts[2], cuts[3] - cuts[2], out, (part,))
-    out = piece(ends_kernel, 1.5, "ends", base, out, (above, below))
-    out = piece(sides_kernel, 4, "sides", base, out, (above, below, left, right))
+    out = piece(sides_kernel, 3.5, "sides", base, out, (left, right))
+    out = piece(ends_kernel, 2, "ends", base, out, (left, right, above, below))
     update = final(nx, ny, blocks, readers, w_cquery, w_ckey, w_cvalue, w_value, out)
     return update.reshape(features.shape)
 

time: 50.6 us -> 43.7 us (0.86)
  the two profiles are of different devices: /device:TPU:18 before, /device:TPU:0 now
where the time goes in v2:
time: 43.7 us; the launch traced here: 43.5 us
  Pallas kernels  25 us (57%)
  starting transfers between devices  15.7 us (36%)
  waiting for transfers between devices  2.38 us (5%)
    pallas_call x5, Pallas kernels, piece(): pl.pallas_call(kernel, in_specs=[IN_VMEM] * (4 + len(done) + len(near)) +...  16.4 us
    ppermute x7, starting transfers between devices, swap(): lax.ppermute(array, axis, [(i, i ^ bits) for i in range(lax.axis_size(axi...  8.43 us
    ppermute x4, starting transfers between devices, shift(): lax.ppermute(array, axis, [(i, (i + step) % count) for i in range(count)])  7.32 us
    pallas_call x1, Pallas kernels, pool(): pl.pallas_call(functools.partial(pool_kernel, tile, nx, ny), in_specs=[IN...  4.48 us
    pallas_call x1, Pallas kernels, final(): pl.pallas_call(functools.partial(final_kernel, nx, ny, len(blocks)), in_s...  4.07 us
    ppermute x7, waiting for transfers between devices, swap(): lax.ppermute(array, axis, [(i, i ^ bits) for i in range(lax.axis_size(axi...  2.37 us
  transfers between devices with their start and end apart: 11, of which 1 were waited for; matrix products, arithmetic and copies ran while one was open for 0% of the time, Pallas kernels for 38%

profile of v2, /device:TPU:0, one launch (start us, length us, event | category | flops | bytes accessed | tf_op | source)
XLA Modules:
  0.0 43.5 jit_solution(4087933138911813637)
XLA Ops:
  0.0 4.5 %pool.1 = (bf16[16,1024,128]{2,1,0:T(8,128)(2,1)S(1)}, s32[16,16,64]{2,1,0:T(8,128)S(1)}, f32[256,768]{1,0:T(8,128)S(1)}, bf16[128,128]{1,0:T(8,128)(2,1)S(1)}, ...) custom-call(bf16[16,1024,128]{2,1,0:T(8,128)(2,1)} %bitcast.7, ...), custom_call_target="tpu_custom_call" | custom-call | tf_op jit(solution)/shard_map/pool/pallas_call | solution.py:93
  4.5 0.5 %collective-permute-start.6 = (bf16[1024,128]{1,0:T(8,128)(2,1)S(1)}, bf16[1024,128]{1,0:T(8,128)(2,1)S(1)}, u32[]{:S(2)}, u32[]{:S(2)}) collective-permute-start(bf16[1024,128]{1,0:T(8,128)(2,1)S(1)} %get-tuple-element.19), channel_id=1, source_target_pairs={{0,1},{1,2},{2,3},{3,4},{4,5},{5,6},{6,7},{7,0},{8,9},{9,10},{10,1... | collective-permute-start | bytes 786440 | tf_op jit(solution)/shard_map/ppermute | solution.py:316
  5.0 2.9 %collective-permute-start.7 = (bf16[1024,128]{1,0:T(8,128)(2,1)S(1)}, bf16[1024,128]{1,0:T(8,128)(2,1)S(1)}, u32[]{:S(2)}, u32[]{:S(2)}) collective-permute-start(bf16[1024,128]{1,0:T(8,128)(2,1)S(1)} %get-tuple-element.20), channel_id=1, source_target_pairs={{0,7},{1,0},{2,1},{3,2},{4,3},{5,4},{6,5},{7,6},{8,15},{9,8},{10,9... | collective-permute-start | bytes 786440 | tf_op jit(solution)/shard_map/ppermute | solution.py:316
  7.9 2.3 %collective-permute-start = (bf16[64,128]{1,0:T(8,128)(2,1)S(1)}, bf16[64,128]{1,0:T(8,128)(2,1)S(1)}, u32[]{:S(2)}, u32[]{:S(2)}) collective-permute-start(bf16[64,128]{1,0:T(8,128)(2,1)S(1)} %get-tuple-element.14.refs_0_), channel_id=1, source_target_pairs={{0,8},{8,0},{16,24},{24,16},{1,9},{9,1},{17,25},{25,17},{2,10},{10... | collective-permute-start | bytes 49160 | tf_op jit(solution)/shard_map/ppermute | solution.py:320
  10.2 2.6 %collective-permute-start.1 = (bf16[64,128]{1,0:T(8,128)(2,1)S(1)}, bf16[64,128]{1,0:T(8,128)(2,1)S(1)}, u32[]{:S(2)}, u32[]{:S(2)}) collective-permute-start(bf16[64,128]{1,0:T(8,128)(2,1)S(1)} %get-tuple-element.14.refs_0_), channel_id=1, source_target_pairs={{0,16},{8,24},{16,0},{24,8},{1,17},{9,25},{17,1},{25,9},{2,18},{10... | collective-permute-start | bytes 49160 | tf_op jit(solution)/shard_map/ppermute | solution.py:320
  12.8 0.0 collective-permute-start.2
  12.8 3.2 %inner_1.1.refs_4_.rest_0_ = bf16[16,1024,256]{2,1,0:T(8,128)(2,1)S(1)} custom-call(bf16[16,1024,128]{2,1,0:T(8,128)(2,1)S(1)} %get-tuple-element.15.fv.fv_ref, s32[16,16,64]{2,1,0:T(8,128)S(1)} %get-tuple-element.16.pv, f32[256,768]{1,0:T(8,128)S(1)} %get-tuple-element.17.mv, bf16[128,128]{1,0:T(8,128)(2,1)S(1)} %get-tuple-element.18.m), custom_call_target="tpu_custom_call" | custom-call | flops 1200000000 | bytes 1000000 | tf_op jit(solution)/shard_map/inner_1/pallas_call | solution.py:249
  16.0 2.4 %collective-permute-done.2.refs_3_ = bf16[64,128]{1,0:T(8,128)(2,1)S(1)} collective-permute-done((bf16[64,128]{1,0:T(8,128)(2,1)S(1)}, bf16[64,128]{1,0:T(8,128)(2,1)S(1)}, u32[]{:S(2)}, u32[]{:S(2)}) %collective-permute-start.2) | collective-permute-done | bytes 16416 | tf_op jit(solution)/shard_map/ppermute | solution.py:320
  18.3 0.6 %collective-permute-start.3 = (bf16[256,128]{1,0:T(8,128)(2,1)S(1)}, bf16[256,128]{1,0:T(8,128)(2,1)S(1)}, u32[]{:S(2)}, u32[]{:S(2)}) collective-permute-start(bf16[256,128]{1,0:T(8,128)(2,1)S(1)} %join.2.rest_1_.refs_0_), channel_id=1, source_target_pairs={{0,2},{1,3},{2,0},{3,1},{4,6},{5,7},{6,4},{7,5},{8,10},{9,11},{10,... | collective-permute-start | bytes 196616 | tf_op jit(solution)/shard_map/ppermute | solution.py:320
  18.9 1.5 %collective-permute-start.4 = (bf16[256,128]{1,0:T(8,128)(2,1)S(1)}, bf16[256,128]{1,0:T(8,128)(2,1)S(1)}, u32[]{:S(2)}, u32[]{:S(2)}) collective-permute-start(bf16[256,128]{1,0:T(8,128)(2,1)S(1)} %join.2.rest_1_.refs_0_), channel_id=1, source_target_pairs={{0,4},{1,5},{2,6},{3,7},{4,0},{5,1},{6,2},{7,3},{8,12},{9,13},{10,... | collective-permute-start | bytes 196616 | tf_op jit(solution)/shard_map/ppermute | solution.py:320
  20.5 1.4 %collective-permute-start.5 = (bf16[256,128]{1,0:T(8,128)(2,1)S(1)}, bf16[256,128]{1,0:T(8,128)(2,1)S(1)}, u32[]{:S(2)}, u32[]{:S(2)}) collective-permute-start(bf16[256,128]{1,0:T(8,128)(2,1)S(1)} %join.2.rest_1_.refs_0_), channel_id=1, source_target_pairs={{0,6},{1,7},{2,4},{3,5},{4,2},{5,3},{6,0},{7,1},{8,14},{9,15},{10,... | collective-permute-start | bytes 196616 | tf_op jit(solution)/shard_map/ppermute | solution.py:320
  21.9 0.1 collective-permute-start.9
  21.9 3.8 %collective-permute-start.10 = (bf16[1152,128]{1,0:T(8,128)(2,1)S(1)}, bf16[1152,128]{1,0:T(8,128)(2,1)S(1)}, u32[]{:S(2)}, u32[]{:S(2)}) collective-permute-start(bf16[1152,128]{1,0:T(8,128)(2,1)S(1)} %get-tuple-element.22), channel_id=1, source_target_pairs={{0,24},{8,0},{16,8},{24,16},{1,25},{9,1},{17,9},{25,17},{2,26},{10... | collective-permute-start | bytes 884744 | tf_op jit(solution)/shard_map/ppermute | solution.py:316
  25.8 4.7 %inner_5.1.refs_4_.rest_0_ = bf16[16,1024,256]{2,1,0:T(8,128)(2,1)S(1)} custom-call(bf16[16,1024,128]{2,1,0:T(8,128)(2,1)S(1)} %get-tuple-element.15.fv.fv_ref, s32[16,16,64]{2,1,0:T(8,128)S(1)} %get-tuple-element.16.pv, f32[256,768]{1,0:T(8,128)S(1)} %get-tuple-element.17.mv, ...), custom_call_target="tpu_custom_call", output_to_operand_aliasing={{}: (4, {})} | custom-call | flops 1800000000 | bytes 1000000 | tf_op jit(solution)/shard_map/inner_5/pallas_call | solution.py:249
  30.6 0.1 collective-permute-start.8
  30.6 3.2 %inner_11.1.out_in = bf16[16,1024,256]{2,1,0:T(8,128)(2,1)S(1)} custom-call(bf16[16,1024,128]{2,1,0:T(8,128)(2,1)S(1)} %get-tuple-element.15.fv.fv_ref, s32[16,16,64]{2,1,0:T(8,128)S(1)} %get-tuple-element.16.pv, f32[256,768]{1,0:T(8,128)S(1)} %get-tuple-element.17.mv, bf16[128,128]{1,0:T(8,128)(2,1)S(1)} %get-tuple-element.18.m, ...), custom_call_target="tpu_custom_call", output_to_operand_aliasing={{}: (4, {})} | custom-call | flops 1200000000 | bytes 1000000 | tf_op jit(solution)/shard_map/inner_11/pallas_call | solution.py:249
  33.8 3.3 %sides.1.out_in = bf16[16,1024,256]{2,1,0:T(8,128)(2,1)S(1)} custom-call(bf16[16,1024,128]{2,1,0:T(8,128)(2,1)S(1)} %get-tuple-element.15.fv.fv_ref, s32[16,16,64]{2,1,0:T(8,128)S(1)} %get-tuple-element.16.pv, f32[256,768]{1,0:T(8,128)S(1)} %get-tuple-element.17.mv, bf16[128,128]{1,0:T(8,128)(2,1)S(1)} %get-tuple-element.18.m, ...), custom_call_target="tpu_custom_call", output_to_operand_aliasing={{}: (4, {})} | custom-call | flops 1400000000 | bytes 1000000 | tf_op jit(solution)/shard_map/sides/pallas_call | solution.py:249
  37.1 0.0 copy-start
  37.2 0.0 copy-start.1
  37.2 0.0 copy-start.2
  37.2 0.0 copy-start.3
  37.2 0.0 copy-start.4
  37.2 2.0 %ends.1.refs_7_ = bf16[16,1024,256]{2,1,0:T(8,128)(2,1)S(1)} custom-call(bf16[16,1024,128]{2,1,0:T(8,128)(2,1)S(1)} %get-tuple-element.15.fv.fv_ref, s32[16,16,64]{2,1,0:T(8,128)S(1)} %get-tuple-element.16.pv, f32[256,768]{1,0:T(8,128)S(1)} %get-tuple-element.17.mv, bf16[128,128]{1,0:T(8,128)(2,1)S(1)} %get-tuple-element.18.m, ...), custom_call_target="tpu_custom_call", output_to_operand_aliasing={{}: (4, {})} | custom-call | flops 800000000 | bytes 1000000 | tf_op jit(solution)/shard_map/ends/pallas_call | solution.py:249
  39.3 4.1 %final.1 = bf16[16,1024,128]{2,1,0:T(8,128)(2,1)} custom-call(bf16[1024,128]{1,0:T(8,128)(2,1)S(1)} %join.3.rest_1_.refs_0_, bf16[1024,128]{1,0:T(8,128)(2,1)S(1)} %collective-permute-done.8.refs_1_, s32[8,32]{1,0:T(8,128)S(1)} %bitcast.6, bf16[128,128]{1,0:T(8,128)(2,1)S(1)} %copy-done, bf16[128,128]{1,0:T(8,128)(2,1)S(1)} %copy-done.1, ...), custom_call_target="tpu_custom_call" | custom-call | tf_op jit(solution)/shard_map/final/pallas_call | solution.py:299
  (18 shorter events, 0.1 us)
Async XLA Ops:
  4.5 17.4 %collective-permute-start.6 = (bf16[1024,128]{1,0:T(8,128)(2,1)S(1)}, bf16[1024,128]{1,0:T(8,128)(2,1)S(1)}, u32[]{:S(2)}, u32[]{:S(2)}) collective-permute-start(bf16[1024,128]{1,0:T(8,128)(2,1)S(1)} %get-tuple-element.19), channel_id=1, source_target_pairs={{0,1},{1,2},{2,3},{3,4},{4,5},{5,6},{6,7},{7,0},{8,9},{9,10},{10,1... | collective-permute-start | bytes 786440 | tf_op jit(solution)/shard_map/ppermute | solution.py:316
  5.0 16.9 %collective-permute-start.7 = (bf16[1024,128]{1,0:T(8,128)(2,1)S(1)}, bf16[1024,128]{1,0:T(8,128)(2,1)S(1)}, u32[]{:S(2)}, u32[]{:S(2)}) collective-permute-start(bf16[1024,128]{1,0:T(8,128)(2,1)S(1)} %get-tuple-element.20), channel_id=1, source_target_pairs={{0,7},{1,0},{2,1},{3,2},{4,3},{5,4},{6,5},{7,6},{8,15},{9,8},{10,9... | collective-permute-start | bytes 786440 | tf_op jit(solution)/shard_map/ppermute | solution.py:316
  7.9 8.0 %collective-permute-start = (bf16[64,128]{1,0:T(8,128)(2,1)S(1)}, bf16[64,128]{1,0:T(8,128)(2,1)S(1)}, u32[]{:S(2)}, u32[]{:S(2)}) collective-permute-start(bf16[64,128]{1,0:T(8,128)(2,1)S(1)} %get-tuple-element.14.refs_0_), channel_id=1, source_target_pairs={{0,8},{8,0},{16,24},{24,16},{1,9},{9,1},{17,25},{25,17},{2,10},{10... | collective-permute-start | bytes 49160 | tf_op jit(solution)/shard_map/ppermute | solution.py:320
  10.2 5.8 %collective-permute-start.1 = (bf16[64,128]{1,0:T(8,128)(2,1)S(1)}, bf16[64,128]{1,0:T(8,128)(2,1)S(1)}, u32[]{:S(2)}, u32[]{:S(2)}) collective-permute-start(bf16[64,128]{1,0:T(8,128)(2,1)S(1)} %get-tuple-element.14.refs_0_), channel_id=1, source_target_pairs={{0,16},{8,24},{16,0},{24,8},{1,17},{9,25},{17,1},{25,9},{2,18},{10... | collective-permute-start | bytes 49160 | tf_op jit(solution)/shard_map/ppermute | solution.py:320
  12.8 5.5 %collective-permute-start.2 = (bf16[64,128]{1,0:T(8,128)(2,1)S(1)}, bf16[64,128]{1,0:T(8,128)(2,1)S(1)}, u32[]{:S(2)}, u32[]{:S(2)}) collective-permute-start(bf16[64,128]{1,0:T(8,128)(2,1)S(1)} %get-tuple-element.14.refs_0_), channel_id=1, source_target_pairs={{0,24},{8,16},{16,8},{24,0},{1,25},{9,17},{17,9},{25,1},{2,26},{10... | collective-permute-start | bytes 49160 | tf_op jit(solution)/shard_map/ppermute | solution.py:320
  18.3 12.2 %collective-permute-start.3 = (bf16[256,128]{1,0:T(8,128)(2,1)S(1)}, bf16[256,128]{1,0:T(8,128)(2,1)S(1)}, u32[]{:S(2)}, u32[]{:S(2)}) collective-permute-start(bf16[256,128]{1,0:T(8,128)(2,1)S(1)} %join.2.rest_1_.refs_0_), channel_id=1, source_target_pairs={{0,2},{1,3},{2,0},{3,1},{4,6},{5,7},{6,4},{7,5},{8,10},{9,11},{10,... | collective-permute-start | bytes 196616 | tf_op jit(solution)/shard_map/ppermute | solution.py:320
  18.9 11.6 %collective-permute-start.4 = (bf16[256,128]{1,0:T(8,128)(2,1)S(1)}, bf16[256,128]{1,0:T(8,128)(2,1)S(1)}, u32[]{:S(2)}, u32[]{:S(2)}) collective-permute-start(bf16[256,128]{1,0:T(8,128)(2,1)S(1)} %join.2.rest_1_.refs_0_), channel_id=1, source_target_pairs={{0,4},{1,5},{2,6},{3,7},{4,0},{5,1},{6,2},{7,3},{8,12},{9,13},{10,... | collective-permute-start | bytes 196616 | tf_op jit(solution)/shard_map/ppermute | solution.py:320
  20.5 10.1 %collective-permute-start.5 = (bf16[256,128]{1,0:T(8,128)(2,1)S(1)}, bf16[256,128]{1,0:T(8,128)(2,1)S(1)}, u32[]{:S(2)}, u32[]{:S(2)}) collective-permute-start(bf16[256,128]{1,0:T(8,128)(2,1)S(1)} %join.2.rest_1_.refs_0_), channel_id=1, source_target_pairs={{0,6},{1,7},{2,4},{3,5},{4,2},{5,3},{6,0},{7,1},{8,14},{9,15},{10,... | collective-permute-start | bytes 196616 | tf_op jit(solution)/shard_map/ppermute | solution.py:320
  21.9 15.3 %collective-permute-start.9 = (bf16[1152,128]{1,0:T(8,128)(2,1)S(1)}, bf16[1152,128]{1,0:T(8,128)(2,1)S(1)}, u32[]{:S(2)}, u32[]{:S(2)}) collective-permute-start(bf16[1152,128]{1,0:T(8,128)(2,1)S(1)} %get-tuple-element.21.rest_2_), channel_id=1, source_target_pairs={{0,8},{8,16},{16,24},{24,0},{1,9},{9,17},{17,25},{25,1},{2,10},{10... | collective-permute-start | bytes 884744 | tf_op jit(solution)/shard_map/ppermute | solution.py:316
  21.9 15.3 %collective-permute-start.10 = (bf16[1152,128]{1,0:T(8,128)(2,1)S(1)}, bf16[1152,128]{1,0:T(8,128)(2,1)S(1)}, u32[]{:S(2)}, u32[]{:S(2)}) collective-permute-start(bf16[1152,128]{1,0:T(8,128)(2,1)S(1)} %get-tuple-element.22), channel_id=1, source_target_pairs={{0,24},{8,0},{16,8},{24,16},{1,25},{9,1},{17,9},{25,17},{2,26},{10... | collective-permute-start | bytes 884744 | tf_op jit(solution)/shard_map/ppermute | solution.py:316
  30.6 8.7 %collective-permute-start.8 = (bf16[1024,128]{1,0:T(8,128)(2,1)S(1)}, bf16[1024,128]{1,0:T(8,128)(2,1)S(1)}, u32[]{:S(2)}, u32[]{:S(2)}) collective-permute-start(bf16[1024,128]{1,0:T(8,128)(2,1)S(1)} %join.3.rest_1_.refs_0_), channel_id=1, source_target_pairs={{0,1},{1,0},{2,3},{3,2},{4,5},{5,4},{6,7},{7,6},{8,9},{9,8},{10,11... | collective-permute-start | bytes 786440 | tf_op jit(solution)/shard_map/ppermute | solution.py:320
  37.1 2.1 %copy-start = (bf16[128,128]{1,0:T(8,128)(2,1)S(1)}, bf16[128,128]{1,0:T(8,128)(2,1)}, u32[]{:S(2)}) copy-start(bf16[128,128]{1,0:T(8,128)(2,1)} %refs_3_.1) | copy-start | bytes 98308
  37.2 2.1 %copy-start.1 = (bf16[128,128]{1,0:T(8,128)(2,1)S(1)}, bf16[128,128]{1,0:T(8,128)(2,1)}, u32[]{:S(2)}) copy-start(bf16[128,128]{1,0:T(8,128)(2,1)} %refs_4_.1) | copy-start | bytes 98308
  37.2 2.1 %copy-start.2 = (bf16[128,128]{1,0:T(8,128)(2,1)S(1)}, bf16[128,128]{1,0:T(8,128)(2,1)}, u32[]{:S(2)}) copy-start(bf16[128,128]{1,0:T(8,128)(2,1)} %refs_5_.1) | copy-start | bytes 98308
  37.2 2.1 %copy-start.3 = (bf16[128,128]{1,0:T(8,128)(2,1)S(1)}, bf16[128,128]{1,0:T(8,128)(2,1)}, u32[]{:S(2)}) copy-start(bf16[128,128]{1,0:T(8,128)(2,1)} %refs_6_.1) | copy-start | bytes 98308
  37.2 2.1 %copy-start.4 = (s32[32,8]{0,1:T(8,128)S(1)}, s32[32,8]{0,1:T(8,128)}, u32[]{:S(2)}) copy-start(s32[32,8]{0,1:T(8,128)} %param.13) | copy-start | bytes 3076

commit v3 on v2

--- a/solution.py
+++ b/solution.py
@@ -12,6 +12,7 @@
 F32 = jnp.float32
 S = 64
 DEPTH = 2
+CUTS = (2, 6, 11)
 IN_VMEM = pl.BlockSpec(memory_space=pltpu.VMEM)
 IN_HBM = pl.BlockSpec(memory_space=pltpu.HBM)
 
@@ -41,7 +42,7 @@
     return jnp.concatenate([ids[:half], ids[half:]], axis=1)
 
 
-def pool_kernel(tile, nx, ny, f_ref, pm_ref, tm_ref, wq_ref, wk_ref, fv_ref, pv_ref, mv_ref, m_ref, pooled_ref, left_ref, right_ref, tv, wq, wk, sems):
+def pool_kernel(tile, nx, ny, f_ref, pm_ref, tm_ref, wq_ref, wk_ref, fv_ref, pv_ref, mv_ref, m_ref, pooled_ref, tv, wq, wk, sems):
     rows, span, chan = fv_ref.shape
     cy = span // tile
     small = [(tm_ref, tv), (wq_ref, wq), (wk_ref, wk), (pm_ref, pv_ref)]
@@ -81,27 +82,22 @@
         )
         beads_in[r].wait()
         total += dot(onehot, jnp.concatenate([fv_ref[r, tile * c : tile * (c + 1)] for c in order], axis=0))
-        left_ref[tile * r : tile * (r + 1)] = fv_ref[r, :tile]
-        right_ref[tile * r : tile * (r + 1)] = fv_ref[r, span - tile :]
     pooled_ref[...] = (total * math.sqrt(S / (rows * span))).astype(BF16)
 
 
 def pool(nx, ny, features, tile_mask, pool_map, w_query, w_key):
     cx, cy, tile, chan = features.shape
     span = cy * tile
-    edge = pltpu.VMEM((cx * tile, chan), BF16)
     return pl.pallas_call(
         functools.partial(pool_kernel, tile, nx, ny),
         in_specs=[IN_HBM] * 5,
-        out_specs=[IN_VMEM] * 7,
+        out_specs=[IN_VMEM] * 5,
         out_shape=[
             pltpu.VMEM((cx, span, chan), BF16),
             pltpu.VMEM((cx, cy, tile), jnp.int32),
             pltpu.VMEM((cx * cy, 12 * tile), F32),
             pltpu.VMEM((chan, chan), BF16),
             pltpu.VMEM((S, chan), BF16),
-            edge,
-            edge,
         ],
         scratch_shapes=[
             pltpu.VMEM((9 * cx, cy), jnp.int32),
@@ -132,10 +128,10 @@
         query, windows, masks, _ = task
         weights = []
         for r, window in enumerate(windows):
-            half = dot_t(query, window()).astype(BF16)
+            half = dot_t(query, window())
             lanes = slice(4 * tile * r, 4 * tile * (r + 1))
             mask = jnp.concatenate([jnp.broadcast_to(masks(h, lanes), (tile, 4 * tile)) for h in (0, 1)], axis=0)
-            weights.append((half * jnp.tanh(half) + half) * mask.astype(BF16))
+            weights.append((half * jnp.tanh(half) + half).astype(BF16) * mask.astype(BF16))
         waiting.append((task, weights))
         if len(waiting) > DEPTH:
             finish(*waiting.pop(0))
@@ -158,7 +154,7 @@
         tasks.append((
             queries[side * (j - first) : side * (j - first + 1)],
             [functools.partial(window, r, j) for r in (row - 1, row, row + 1)],
-            lambda h, lanes, j=j: mv[pl.ds(row * cy + 2 * j + h, 1), lanes],
+            lambda h, lanes, lo=row * cy + 2 * j: mv[lo + h : lo + h + 1, lanes],
             store,
         ))
     return tasks
@@ -176,28 +172,32 @@
         o[row, span // 2 + tile * i : span // 2 + tile * (i + 1), chan:] = turned[tile:]
 
 
-def inner_kernel(first, count, fv, pv, mv, m, *rest):
+def inner_tasks(refs, rows):
+    fv, pv = refs[:2]
     cy, tile = pv.shape[1:]
-    refs = (fv, pv, mv, m, rest[-1])
 
     def window(r, j):
         return fv[r, tile * (2 * j - 1) : tile * (2 * j + 3)]
 
-    def body(row, many):
-        tasks = []
-        for k in range(many):
-            node_rows(refs, row + k)
-            tasks += row_tasks(refs, row + k, 1, cy // 2 - 1, window)
-        attend(tile, tasks)
-
-    if count // 2:
-
-        @pl.loop(0, count // 2)
-        def _(i):
-            body(first + 2 * i, 2)
-
-    if count % 2:
-        body(first + count - 1, 1)
+    tasks = []
+    for row in rows:
+        node_rows(refs, row)
+        tasks += row_tasks(refs, row, 1, cy // 2 - 1, window)
+    return tasks
+
+
+def opening_kernel(rows, fv, pv, mv, m, pooled_in, o, pooled, left, right):
+    span = fv.shape[1]
+    tile = pv.shape[2]
+    pooled[...] = pooled_in[...]
+    for r in range(fv.shape[0]):
+        left[tile * r : tile * (r + 1)] = fv[r, :tile]
+        right[tile * r : tile * (r + 1)] = fv[r, span - tile :]
+    attend(tile, inner_tasks((fv, pv, mv, m, o), rows))
+
+
+def inner_kernel(rows, fv, pv, mv, m, *rest):
+    attend(pv.shape[2], inner_tasks((fv, pv, mv, m, rest[-1]), rows))
 
 
 def side_window(fv, tile, left, right):
@@ -213,11 +213,11 @@
     return window
 
 
-def sides_kernel(fv, pv, mv, m, out_in, left, right, o):
+def sides_kernel(rows, fv, pv, mv, m, out_in, left, right, *rest):
     cy, tile = pv.shape[1:]
-    refs = (fv, pv, mv, m, o)
+    refs = (fv, pv, mv, m, rest[-1])
     window = side_window(fv, tile, left, right)
-    tasks = []
+    tasks = inner_tasks(refs, rows)
     for row in range(1, fv.shape[0] - 1):
         for j in (0, cy // 2 - 1):
             tasks += row_tasks(refs, row, j, j + 1, window)
@@ -242,22 +242,36 @@
     attend(tile, tasks)
 
 
+def estimate(rows):
+    return pl.CostEstimate(flops=int(rows * 400_000_000), bytes_accessed=1_000_000, transcendentals=0)
+
+
+def opening(rows, base, pooled):
+    cx, span, chan = base[0].shape
+    cy = base[1].shape[1]
+    edge = pltpu.VMEM((cx * span // cy, chan), BF16)
+    return pl.pallas_call(
+        functools.partial(opening_kernel, rows),
+        in_specs=[IN_VMEM] * 5,
+        out_specs=[IN_VMEM] * 4,
+        out_shape=[pltpu.VMEM((cx, span, 2 * chan), BF16), pltpu.VMEM(pooled.shape, BF16), edge, edge],
+        compiler_params=params(16),
+        cost_estimate=estimate(len(rows)),
+        name="opening",
+    )(*base, pooled)
+
+
 def piece(kernel, rows_done, name, base, out, near=(), ties=()):
-    fv, _, _, _ = base
-    cx, span, chan = fv.shape
-    done = [] if out is None else [out]
     return pl.pallas_call(
         kernel,
-        in_specs=[IN_VMEM] * (4 + len(done) + len(near)) + [pl.BlockSpec(memory_space=pl.ANY)] * len(ties),
+        in_specs=[IN_VMEM] * (5 + len(near)) + [pl.BlockSpec(memory_space=pl.ANY)] * len(ties),
         out_specs=IN_VMEM,
-        out_shape=pltpu.VMEM((cx, span, 2 * chan), BF16),
-        input_output_aliases={4: 0} if done else {},
+        out_shape=pltpu.VMEM(out.shape, BF16),
+        input_output_aliases={4: 0},
         compiler_params=params(16),
-        cost_estimate=pl.CostEstimate(
-            flops=int(rows_done * 400_000_000), bytes_accessed=1_000_000, transcendentals=0
-        ),
+        cost_estimate=estimate(rows_done),
         name=name,
-    )(*base, *done, *near, *ties)
+    )(*base, out, *near, *ties)
 
 
 def final_kernel(nx, ny, n_blocks, *refs):
@@ -340,7 +354,8 @@
     )(*parts, *ties)
 
 
-def edge_rows_kernel(tile, fv_ref, left_ref, right_ref, up_ref, down_ref):
+def edge_rows_kernel(tile, fv_ref, left_ref, right_ref, *rest):
+    up_ref, down_ref = rest[-2:]
     rows, span, _ = fv_ref.shape
     for ref, r in ((up_ref, rows - 1), (down_ref, 0)):
         ref[:tile] = left_ref[tile * r : tile * (r + 1)]
@@ -348,43 +363,40 @@
         ref[tile + span :] = right_ref[tile * r : tile * (r + 1)]
 
 
-def edge_rows(tile, fv, left, right):
+def edge_rows(tile, fv, left, right, ties):
     _, span, chan = fv.shape
     edge = pltpu.VMEM((span + 2 * tile, chan), BF16)
     return pl.pallas_call(
         functools.partial(edge_rows_kernel, tile),
-        in_specs=[IN_VMEM] * 3,
+        in_specs=[IN_VMEM] * 3 + [pl.BlockSpec(memory_space=pl.ANY)] * len(ties),
         out_specs=[IN_VMEM] * 2,
         out_shape=[edge, edge],
         compiler_params=params(4),
         name="edge_rows",
-    )(fv, left, right)
+    )(fv, left, right, *ties)
 
 
 def per_device(features, tile_mask, pool_map, readers, w_query, w_key, w_value, w_cquery, w_ckey, w_cvalue):
     cx, cy, tile, chan = features.shape
     nx, ny = lax.axis_size("gx"), lax.axis_size("gy")
-    *base, pooled, left_edge, right_edge = pool(nx, ny, features, tile_mask, pool_map, w_query, w_key)
+    *base, pooled = pool(nx, ny, features, tile_mask, pool_map, w_query, w_key)
     fv = base[0]
-
-    def inner(first, count, out, ties):
-        return piece(functools.partial(inner_kernel, first, count), 0.75 * count, f"inner_{first}", base, out, (), ties)
-
-    cuts = [1, 1 + (cx - 2) * 4 // 14, 1 + (cx - 2) * 10 // 14, cx - 1]
-    blocks = [pooled] + [swap(pooled, "gx", bits) for bits in range(1, nx)]
+    cuts = [1] + [1 + (cx - 2) * part // 14 for part in CUTS] + [cx - 1]
+    rows = [range(lo, hi) for lo, hi in zip(cuts, cuts[1:])]
+    out, pooled, left_edge, right_edge = opening(rows[0], base, pooled)
     left = shift(right_edge, "gy", 1)
     right = shift(left_edge, "gy", -1)
-    out = inner(cuts[0], cuts[1] - cuts[0], None, ())
-    part = join(blocks, (out,))
-    blocks = [part] + [swap(part, "gy", bits) for bits in range(2, ny, 2)]
-    up, down = edge_rows(tile, fv, left, right)
+    blocks = [pooled] + [swap(pooled, "gx", bits) for bits in range(1, nx)]
+    out = piece(functools.partial(inner_kernel, rows[1]), len(rows[1]), "inner", base, out, (), (pooled,))
+    up, down = edge_rows(tile, fv, left, right, (out,))
     above = shift(up, "gx", 1)
     below = shift(down, "gx", -1)
-    out = inner(cuts[1], cuts[2] - cuts[1], out, (part, up))
+    part = join(blocks, (out, up))
+    blocks = [part] + [swap(part, "gy", bits) for bits in range(2, ny, 2)]
+    out = piece(functools.partial(inner_kernel, rows[2]), len(rows[2]), "middle", base, out, (), (part, up))
     part = join(blocks, (out,))
     blocks = [part, swap(part, "gy", 1)]
-    out = inner(cuts[2], cuts[3] - cuts[2], out, (part,))
-    out = piece(sides_kernel, 3.5, "sides", base, out, (left, right))
+    out = piece(functools.partial(sides_kernel, rows[3]), len(rows[3]) + 3.5, "sides", base, out, (left, right), (part,))
     out = piece(ends_kernel, 2, "ends", base, out, (left, right, above, below))
     update = final(nx, ny, blocks, readers, w_cquery, w_ckey, w_cvalue, w_value, out)
     return update.reshape(features.shape)

time: 43.7 us -> 43.6 us (level)
  transfers between devices with their start and end apart: 11 -> 11, of which waited for: 1 -> 1; matrix products, arithmetic and copies ran while one was open for 0% -> 0% of each run, Pallas kernels for 38% -> 34%
where the time goes in v3:
time: 43.6 us; the launch traced here: 43.5 us
  Pallas kernels  25 us (57%)
  starting transfers between devices  15.7 us (36%)
  waiting for transfers between devices  2.36 us (5%)
    pallas_call x4, Pallas kernels, piece(): pl.pallas_call(kernel, in_specs=[IN_VMEM] * (5 + len(near)) + [pl.BlockSp...  14.6 us
    ppermute x7, starting transfers between devices, swap(): lax.ppermute(array, axis, [(i, i ^ bits) for i in range(lax.axis_size(axi...  8.42 us
    ppermute x4, starting transfers between devices, shift(): lax.ppermute(array, axis, [(i, (i + step) % count) for i in range(count)])  7.27 us
    pallas_call x1, Pallas kernels, pool(): pl.pallas_call(functools.partial(pool_kernel, tile, nx, ny), in_specs=[IN...  4.42 us
    pallas_call x1, Pallas kernels, final(): pl.pallas_call(functools.partial(final_kernel, nx, ny, len(blocks)), in_s...  4.29 us
    ppermute x7, waiting for transfers between devices, swap(): lax.ppermute(array, axis, [(i, i ^ bits) for i in range(lax.axis_size(axi...  2.35 us
    pallas_call x1, Pallas kernels, opening(): pl.pallas_call(functools.partial(opening_kernel, rows), in_specs=[IN_VMEM...  1.61 us
  transfers between devices with their start and end apart: 11, of which 1 were waited for; matrix products, arithmetic and copies ran while one was open for 0% of the time, Pallas kernels for 34%

profile of v3, /device:TPU:0, one launch (start us, length us, event | category | flops | bytes accessed | tf_op | source)
XLA Modules:
  0.0 43.5 jit_solution(9648461347984376002)
XLA Ops:
  0.0 4.4 %pool.1 = (bf16[16,1024,128]{2,1,0:T(8,128)(2,1)S(1)}, s32[16,16,64]{2,1,0:T(8,128)S(1)}, f32[256,768]{1,0:T(8,128)S(1)}, bf16[128,128]{1,0:T(8,128)(2,1)S(1)}, bf16[64,128]{1,0:T(8,128)(2,1)S(1)}) custom-call(bf16[16,1024,128]{2,1,0:T(8,128)(2,1)} %bitcast.7, s32[16,16,64]{2,1,0:T(8,128)} %pm_ref.1, s32[144,16]{1,0:T(8,128)} %bitcast.8, ...), custom_call_target="tpu_custom_call" | custom-call | tf_op jit(solution)/shard_map/pool/pallas_call | solution.py:91
  4.4 1.6 %opening.1 = (bf16[16,1024,256]{2,1,0:T(8,128)(2,1)S(1)}, bf16[64,128]{1,0:T(8,128)(2,1)S(1)}, bf16[1024,128]{1,0:T(8,128)(2,1)S(1)}, bf16[1024,128]{1,0:T(8,128)(2,1)S(1)}) custom-call(bf16[16,1024,128]{2,1,0:T(8,128)(2,1)S(1)} %get-tuple-element.16.fv.fv_ref, s32[16,16,64]{2,1,0:T(8,128)S(1)} %get-tuple-element.17.pv, ...), custom_call_target="tpu_custom_call" | custom-call | flops 800000000 | bytes 1000000 | tf_op jit(solution)/shard_map/opening/pallas_call | solution.py:253
  6.1 0.5 %collective-permute-start.3 = (bf16[1024,128]{1,0:T(8,128)(2,1)S(1)}, bf16[1024,128]{1,0:T(8,128)(2,1)S(1)}, u32[]{:S(2)}, u32[]{:S(2)}) collective-permute-start(bf16[1024,128]{1,0:T(8,128)(2,1)S(1)} %get-tuple-element.23), channel_id=1, source_target_pairs={{0,1},{1,2},{2,3},{3,4},{4,5},{5,6},{6,7},{7,0},{8,9},{9,10},{10,1... | collective-permute-start | bytes 786440 | tf_op jit(solution)/shard_map/ppermute | solution.py:330
  6.6 2.9 %collective-permute-start.4 = (bf16[1024,128]{1,0:T(8,128)(2,1)S(1)}, bf16[1024,128]{1,0:T(8,128)(2,1)S(1)}, u32[]{:S(2)}, u32[]{:S(2)}) collective-permute-start(bf16[1024,128]{1,0:T(8,128)(2,1)S(1)} %get-tuple-element.24), channel_id=1, source_target_pairs={{0,7},{1,0},{2,1},{3,2},{4,3},{5,4},{6,5},{7,6},{8,15},{9,8},{10,9... | collective-permute-start | bytes 786440 | tf_op jit(solution)/shard_map/ppermute | solution.py:330
  9.5 2.3 %collective-permute-start = (bf16[64,128]{1,0:T(8,128)(2,1)S(1)}, bf16[64,128]{1,0:T(8,128)(2,1)S(1)}, u32[]{:S(2)}, u32[]{:S(2)}) collective-permute-start(bf16[64,128]{1,0:T(8,128)(2,1)S(1)} %get-tuple-element.21.rest_1_.refs_0_), channel_id=1, source_target_pairs={{0,8},{8,0},{16,24},{24,16},{1,9},{9,1},{17,25},{25,17},{2,10},{10... | collective-permute-start | bytes 49160 | tf_op jit(solution)/shard_map/ppermute | solution.py:334
  11.8 2.6 %collective-permute-start.1 = (bf16[64,128]{1,0:T(8,128)(2,1)S(1)}, bf16[64,128]{1,0:T(8,128)(2,1)S(1)}, u32[]{:S(2)}, u32[]{:S(2)}) collective-permute-start(bf16[64,128]{1,0:T(8,128)(2,1)S(1)} %get-tuple-element.21.rest_1_.refs_0_), channel_id=1, source_target_pairs={{0,16},{8,24},{16,0},{24,8},{1,17},{9,25},{17,1},{25,9},{2,18},{10... | collective-permute-start | bytes 49160 | tf_op jit(solution)/shard_map/ppermute | solution.py:334
  14.4 0.0 collective-permute-start.2
  14.4 3.1 %inner.1.rest_0_.refs_4_ = bf16[16,1024,256]{2,1,0:T(8,128)(2,1)S(1)} custom-call(bf16[16,1024,128]{2,1,0:T(8,128)(2,1)S(1)} %get-tuple-element.16.fv.fv_ref, s32[16,16,64]{2,1,0:T(8,128)S(1)} %get-tuple-element.17.pv, f32[256,768]{1,0:T(8,128)S(1)} %get-tuple-element.18.mv, ...), custom_call_target="tpu_custom_call", output_to_operand_aliasing={{}: (4, {})} | custom-call | flops 1600000000 | bytes 1000000 | tf_op jit(solution)/shard_map/inner/pallas_call | solution.py:265
  17.5 0.0 collective-permute-done.4.right_ref.right
  17.6 2.3 %collective-permute-done.2.refs_3_ = bf16[64,128]{1,0:T(8,128)(2,1)S(1)} collective-permute-done((bf16[64,128]{1,0:T(8,128)(2,1)S(1)}, bf16[64,128]{1,0:T(8,128)(2,1)S(1)}, u32[]{:S(2)}, u32[]{:S(2)}) %collective-permute-start.2) | collective-permute-done | bytes 16416 | tf_op jit(solution)/shard_map/ppermute | solution.py:334
  19.9 0.6 %collective-permute-start.5 = (bf16[256,128]{1,0:T(8,128)(2,1)S(1)}, bf16[256,128]{1,0:T(8,128)(2,1)S(1)}, u32[]{:S(2)}, u32[]{:S(2)}) collective-permute-start(bf16[256,128]{1,0:T(8,128)(2,1)S(1)} %join.2.rest_1_.refs_0_), channel_id=1, source_target_pairs={{0,2},{1,3},{2,0},{3,1},{4,6},{5,7},{6,4},{7,5},{8,10},{9,11},{10,... | collective-permute-start | bytes 196616 | tf_op jit(solution)/shard_map/ppermute | solution.py:334
  20.5 1.5 %collective-permute-start.6 = (bf16[256,128]{1,0:T(8,128)(2,1)S(1)}, bf16[256,128]{1,0:T(8,128)(2,1)S(1)}, u32[]{:S(2)}, u32[]{:S(2)}) collective-permute-start(bf16[256,128]{1,0:T(8,128)(2,1)S(1)} %join.2.rest_1_.refs_0_), channel_id=1, source_target_pairs={{0,4},{1,5},{2,6},{3,7},{4,0},{5,1},{6,2},{7,3},{8,12},{9,13},{10,... | collective-permute-start | bytes 196616 | tf_op jit(solution)/shard_map/ppermute | solution.py:334
  22.0 1.4 %collective-permute-start.7 = (bf16[256,128]{1,0:T(8,128)(2,1)S(1)}, bf16[256,128]{1,0:T(8,128)(2,1)S(1)}, u32[]{:S(2)}, u32[]{:S(2)}) collective-permute-start(bf16[256,128]{1,0:T(8,128)(2,1)S(1)} %join.2.rest_1_.refs_0_), channel_id=1, source_target_pairs={{0,6},{1,7},{2,4},{3,5},{4,2},{5,3},{6,0},{7,1},{8,14},{9,15},{10,... | collective-permute-start | bytes 196616 | tf_op jit(solution)/shard_map/ppermute | solution.py:334
  23.4 3.8 %collective-permute-start.10 = (bf16[1152,128]{1,0:T(8,128)(2,1)S(1)}, bf16[1152,128]{1,0:T(8,128)(2,1)S(1)}, u32[]{:S(2)}, u32[]{:S(2)}) collective-permute-start(bf16[1152,128]{1,0:T(8,128)(2,1)S(1)} %get-tuple-element.26), channel_id=1, source_target_pairs={{0,24},{8,0},{16,8},{24,16},{1,25},{9,1},{17,9},{25,17},{2,26},{10... | collective-permute-start | bytes 884744 | tf_op jit(solution)/shard_map/ppermute | solution.py:330
  27.2 3.9 %middle.1.refs_4_.out_in = bf16[16,1024,256]{2,1,0:T(8,128)(2,1)S(1)} custom-call(bf16[16,1024,128]{2,1,0:T(8,128)(2,1)S(1)} %get-tuple-element.16.fv.fv_ref, s32[16,16,64]{2,1,0:T(8,128)S(1)} %get-tuple-element.17.pv, f32[256,768]{1,0:T(8,128)S(1)} %get-tuple-element.18.mv, ...), custom_call_target="tpu_custom_call", output_to_operand_aliasing={{}: (4, {})} | custom-call | flops 2000000000 | bytes 1000000 | tf_op jit(solution)/shard_map/middle/pallas_call | solution.py:265
  31.1 0.1 collective-permute-start.8
  31.2 5.6 %sides.1.out_in = bf16[16,1024,256]{2,1,0:T(8,128)(2,1)S(1)} custom-call(bf16[16,1024,128]{2,1,0:T(8,128)(2,1)S(1)} %get-tuple-element.16.fv.fv_ref, s32[16,16,64]{2,1,0:T(8,128)S(1)} %get-tuple-element.17.pv, f32[256,768]{1,0:T(8,128)S(1)} %get-tuple-element.18.mv, bf16[128,128]{1,0:T(8,128)(2,1)S(1)} %get-tuple-element.19.m, ...), custom_call_target="tpu_custom_call", output_to_operand_aliasing={{}: (4, {})} | custom-call | flops 2600000000 | bytes 1000000 | tf_op jit(solution)/shard_map/sides/pallas_call | solution.py:265
  36.8 0.0 copy-start
  36.8 0.0 copy-start.1
  36.8 0.0 copy-start.2
  36.8 0.0 copy-start.3
  36.8 0.0 copy-start.4
  36.9 2.0 %ends.1.refs_7_ = bf16[16,1024,256]{2,1,0:T(8,128)(2,1)S(1)} custom-call(bf16[16,1024,128]{2,1,0:T(8,128)(2,1)S(1)} %get-tuple-element.16.fv.fv_ref, s32[16,16,64]{2,1,0:T(8,128)S(1)} %get-tuple-element.17.pv, f32[256,768]{1,0:T(8,128)S(1)} %get-tuple-element.18.mv, bf16[128,128]{1,0:T(8,128)(2,1)S(1)} %get-tuple-element.19.m, ...), custom_call_target="tpu_custom_call", output_to_operand_aliasing={{}: (4, {})} | custom-call | flops 800000000 | bytes 1000000 | tf_op jit(solution)/shard_map/ends/pallas_call | solution.py:265
  39.0 4.3 %final.1 = bf16[16,1024,128]{2,1,0:T(8,128)(2,1)} custom-call(bf16[1024,128]{1,0:T(8,128)(2,1)S(1)} %join.3.rest_0_.refs_0_, bf16[1024,128]{1,0:T(8,128)(2,1)S(1)} %collective-permute-done.8.refs_1_, s32[8,32]{1,0:T(8,128)S(1)} %bitcast.6, bf16[128,128]{1,0:T(8,128)(2,1)S(1)} %copy-done, bf16[128,128]{1,0:T(8,128)(2,1)S(1)} %copy-done.1, ...), custom_call_target="tpu_custom_call" | custom-call | tf_op jit(solution)/shard_map/final/pallas_call | solution.py:313
  (18 shorter events, 0.1 us)
Async XLA Ops:
  6.1 11.4 %collective-permute-start.3 = (bf16[1024,128]{1,0:T(8,128)(2,1)S(1)}, bf16[1024,128]{1,0:T(8,128)(2,1)S(1)}, u32[]{:S(2)}, u32[]{:S(2)}) collective-permute-start(bf16[1024,128]{1,0:T(8,128)(2,1)S(1)} %get-tuple-element.23), channel_id=1, source_target_pairs={{0,1},{1,2},{2,3},{3,4},{4,5},{5,6},{6,7},{7,0},{8,9},{9,10},{10,1... | collective-permute-start | bytes 786440 | tf_op jit(solution)/shard_map/ppermute | solution.py:330
  6.6 10.9 %collective-permute-start.4 = (bf16[1024,128]{1,0:T(8,128)(2,1)S(1)}, bf16[1024,128]{1,0:T(8,128)(2,1)S(1)}, u32[]{:S(2)}, u32[]{:S(2)}) collective-permute-start(bf16[1024,128]{1,0:T(8,128)(2,1)S(1)} %get-tuple-element.24), channel_id=1, source_target_pairs={{0,7},{1,0},{2,1},{3,2},{4,3},{5,4},{6,5},{7,6},{8,15},{9,8},{10,9... | collective-permute-start | bytes 786440 | tf_op jit(solution)/shard_map/ppermute | solution.py:330
  9.5 8.1 %collective-permute-start = (bf16[64,128]{1,0:T(8,128)(2,1)S(1)}, bf16[64,128]{1,0:T(8,128)(2,1)S(1)}, u32[]{:S(2)}, u32[]{:S(2)}) collective-permute-start(bf16[64,128]{1,0:T(8,128)(2,1)S(1)} %get-tuple-element.21.rest_1_.refs_0_), channel_id=1, source_target_pairs={{0,8},{8,0},{16,24},{24,16},{1,9},{9,1},{17,25},{25,17},{2,10},{10... | collective-permute-start | bytes 49160 | tf_op jit(solution)/shard_map/ppermute | solution.py:334
  11.8 5.8 %collective-permute-start.1 = (bf16[64,128]{1,0:T(8,128)(2,1)S(1)}, bf16[64,128]{1,0:T(8,128)(2,1)S(1)}, u32[]{:S(2)}, u32[]{:S(2)}) collective-permute-start(bf16[64,128]{1,0:T(8,128)(2,1)S(1)} %get-tuple-element.21.rest_1_.refs_0_), channel_id=1, source_target_pairs={{0,16},{8,24},{16,0},{24,8},{1,17},{9,25},{17,1},{25,9},{2,18},{10... | collective-permute-start | bytes 49160 | tf_op jit(solution)/shard_map/ppermute | solution.py:334
  14.4 5.5 %collective-permute-start.2 = (bf16[64,128]{1,0:T(8,128)(2,1)S(1)}, bf16[64,128]{1,0:T(8,128)(2,1)S(1)}, u32[]{:S(2)}, u32[]{:S(2)}) collective-permute-start(bf16[64,128]{1,0:T(8,128)(2,1)S(1)} %get-tuple-element.21.rest_1_.refs_0_), channel_id=1, source_target_pairs={{0,24},{8,16},{16,8},{24,0},{1,25},{9,17},{17,9},{25,1},{2,26},{10... | collective-permute-start | bytes 49160 | tf_op jit(solution)/shard_map/ppermute | solution.py:334
  19.9 11.2 %collective-permute-start.5 = (bf16[256,128]{1,0:T(8,128)(2,1)S(1)}, bf16[256,128]{1,0:T(8,128)(2,1)S(1)}, u32[]{:S(2)}, u32[]{:S(2)}) collective-permute-start(bf16[256,128]{1,0:T(8,128)(2,1)S(1)} %join.2.rest_1_.refs_0_), channel_id=1, source_target_pairs={{0,2},{1,3},{2,0},{3,1},{4,6},{5,7},{6,4},{7,5},{8,10},{9,11},{10,... | collective-permute-start | bytes 196616 | tf_op jit(solution)/shard_map/ppermute | solution.py:334
  20.5 10.6 %collective-permute-start.6 = (bf16[256,128]{1,0:T(8,128)(2,1)S(1)}, bf16[256,128]{1,0:T(8,128)(2,1)S(1)}, u32[]{:S(2)}, u32[]{:S(2)}) collective-permute-start(bf16[256,128]{1,0:T(8,128)(2,1)S(1)} %join.2.rest_1_.refs_0_), channel_id=1, source_target_pairs={{0,4},{1,5},{2,6},{3,7},{4,0},{5,1},{6,2},{7,3},{8,12},{9,13},{10,... | collective-permute-start | bytes 196616 | tf_op jit(solution)/shard_map/ppermute | solution.py:334
  22.0 9.1 %collective-permute-start.7 = (bf16[256,128]{1,0:T(8,128)(2,1)S(1)}, bf16[256,128]{1,0:T(8,128)(2,1)S(1)}, u32[]{:S(2)}, u32[]{:S(2)}) collective-permute-start(bf16[256,128]{1,0:T(8,128)(2,1)S(1)} %join.2.rest_1_.refs_0_), channel_id=1, source_target_pairs={{0,6},{1,7},{2,4},{3,5},{4,2},{5,3},{6,0},{7,1},{8,14},{9,15},{10,... | collective-permute-start | bytes 196616 | tf_op jit(solution)/shard_map/ppermute | solution.py:334
  23.4 13.5 %collective-permute-start.9 = (bf16[1152,128]{1,0:T(8,128)(2,1)S(1)}, bf16[1152,128]{1,0:T(8,128)(2,1)S(1)}, u32[]{:S(2)}, u32[]{:S(2)}) collective-permute-start(bf16[1152,128]{1,0:T(8,128)(2,1)S(1)} %get-tuple-element.25.refs_5_.rest_2_), channel_id=1, source_target_pairs={{0,8},{8,16},{16,24},{24,0},{1,9},{9,17},{17,25},{25,1},{2,10},{10... | collective-permute-start | bytes 884744 | tf_op jit(solution)/shard_map/ppermute | solution.py:330
  23.4 13.5 %collective-permute-start.10 = (bf16[1152,128]{1,0:T(8,128)(2,1)S(1)}, bf16[1152,128]{1,0:T(8,128)(2,1)S(1)}, u32[]{:S(2)}, u32[]{:S(2)}) collective-permute-start(bf16[1152,128]{1,0:T(8,128)(2,1)S(1)} %get-tuple-element.26), channel_id=1, source_target_pairs={{0,24},{8,0},{16,8},{24,16},{1,25},{9,1},{17,9},{25,17},{2,26},{10... | collective-permute-start | bytes 884744 | tf_op jit(solution)/shard_map/ppermute | solution.py:330
  31.1 7.8 %collective-permute-start.8 = (bf16[1024,128]{1,0:T(8,128)(2,1)S(1)}, bf16[1024,128]{1,0:T(8,128)(2,1)S(1)}, u32[]{:S(2)}, u32[]{:S(2)}) collective-permute-start(bf16[1024,128]{1,0:T(8,128)(2,1)S(1)} %join.3.rest_0_.refs_0_), channel_id=1, source_target_pairs={{0,1},{1,0},{2,3},{3,2},{4,5},{5,4},{6,7},{7,6},{8,9},{9,8},{10,11... | collective-permute-start | bytes 786440 | tf_op jit(solution)/shard_map/ppermute | solution.py:334
  36.8 2.1 %copy-start = (bf16[128,128]{1,0:T(8,128)(2,1)S(1)}, bf16[128,128]{1,0:T(8,128)(2,1)}, u32[]{:S(2)}) copy-start(bf16[128,128]{1,0:T(8,128)(2,1)} %refs_3_.1) | copy-start | bytes 98308
  36.8 2.1 %copy-start.1 = (bf16[128,128]{1,0:T(8,128)(2,1)S(1)}, bf16[128,128]{1,0:T(8,128)(2,1)}, u32[]{:S(2)}) copy-start(bf16[128,128]{1,0:T(8,128)(2,1)} %refs_4_.1) | copy-start | bytes 98308
  36.8 2.1 %copy-start.2 = (bf16[128,128]{1,0:T(8,128)(2,1)S(1)}, bf16[128,128]{1,0:T(8,128)(2,1)}, u32[]{:S(2)}) copy-start(bf16[128,128]{1,0:T(8,128)(2,1)} %refs_5_.1) | copy-start | bytes 98308
  36.8 2.1 %copy-start.3 = (bf16[128,128]{1,0:T(8,128)(2,1)S(1)}, bf16[128,128]{1,0:T(8,128)(2,1)}, u32[]{:S(2)}) copy-start(bf16[128,128]{1,0:T(8,128)(2,1)} %refs_6_.1) | copy-start | bytes 98308
  36.8 2.1 %copy-start.4 = (s32[32,8]{0,1:T(8,128)S(1)}, s32[32,8]{0,1:T(8,128)}, u32[]{:S(2)}) copy-start(s32[32,8]{0,1:T(8,128)} %param.13) | copy-start | bytes 3076

commit v4 on v3

--- a/solution.py
+++ b/solution.py
@@ -12,7 +12,7 @@
 F32 = jnp.float32
 S = 64
 DEPTH = 2
-CUTS = (2, 6, 11)
+CUTS = (4, 7, 10, 14)
 IN_VMEM = pl.BlockSpec(memory_space=pltpu.VMEM)
 IN_HBM = pl.BlockSpec(memory_space=pltpu.HBM)
 
@@ -42,7 +42,7 @@
     return jnp.concatenate([ids[:half], ids[half:]], axis=1)
 
 
-def pool_kernel(tile, nx, ny, f_ref, pm_ref, tm_ref, wq_ref, wk_ref, fv_ref, pv_ref, mv_ref, m_ref, pooled_ref, tv, wq, wk, sems):
+def pool_kernel(tile, nx, ny, f_ref, pm_ref, tm_ref, wq_ref, wk_ref, fv_ref, pv_ref, mv_ref, m_ref, pooled_ref, left_ref, right_ref, tv, wq, wk, sems):
     rows, span, chan = fv_ref.shape
     cy = span // tile
     small = [(tm_ref, tv), (wq_ref, wq), (wk_ref, wk), (pm_ref, pv_ref)]
@@ -82,22 +82,27 @@
         )
         beads_in[r].wait()
         total += dot(onehot, jnp.concatenate([fv_ref[r, tile * c : tile * (c + 1)] for c in order], axis=0))
+        left_ref[tile * r : tile * (r + 1)] = fv_ref[r, :tile]
+        right_ref[tile * r : tile * (r + 1)] = fv_ref[r, span - tile :]
     pooled_ref[...] = (total * math.sqrt(S / (rows * span))).astype(BF16)
 
 
 def pool(nx, ny, features, tile_mask, pool_map, w_query, w_key):
     cx, cy, tile, chan = features.shape
     span = cy * tile
+    edge = pltpu.VMEM((cx * tile, chan), BF16)
     return pl.pallas_call(
         functools.partial(pool_kernel, tile, nx, ny),
         in_specs=[IN_HBM] * 5,
-        out_specs=[IN_VMEM] * 5,
+        out_specs=[IN_VMEM] * 7,
         out_shape=[
             pltpu.VMEM((cx, span, chan), BF16),
             pltpu.VMEM((cx, cy, tile), jnp.int32),
             pltpu.VMEM((cx * cy, 12 * tile), F32),
             pltpu.VMEM((chan, chan), BF16),
             pltpu.VMEM((S, chan), BF16),
+            edge,
+            edge,
         ],
         scratch_shapes=[
             pltpu.VMEM((9 * cx, cy), jnp.int32),
@@ -186,16 +191,6 @@
     return tasks
 
 
-def opening_kernel(rows, fv, pv, mv, m, pooled_in, o, pooled, left, right):
-    span = fv.shape[1]
-    tile = pv.shape[2]
-    pooled[...] = pooled_in[...]
-    for r in range(fv.shape[0]):
-        left[tile * r : tile * (r + 1)] = fv[r, :tile]
-        right[tile * r : tile * (r + 1)] = fv[r, span - tile :]
-    attend(tile, inner_tasks((fv, pv, mv, m, o), rows))
-
-
 def inner_kernel(rows, fv, pv, mv, m, *rest):
     attend(pv.shape[2], inner_tasks((fv, pv, mv, m, rest[-1]), rows))
 
@@ -224,10 +219,10 @@
     attend(tile, tasks)
 
 
-def ends_kernel(fv, pv, mv, m, out_in, left, right, above, below, o):
+def ends_kernel(fv, pv, mv, m, out_in, left, right, above, below, *rest):
     cy, tile = pv.shape[1:]
     rows = fv.shape[0]
-    refs = (fv, pv, mv, m, o)
+    refs = (fv, pv, mv, m, rest[-1])
     near = side_window(fv, tile, left, right)
 
     def window(r, j):
@@ -246,32 +241,19 @@
     return pl.CostEstimate(flops=int(rows * 400_000_000), bytes_accessed=1_000_000, transcendentals=0)
 
 
-def opening(rows, base, pooled):
+def piece(kernel, rows_done, name, base, out, near=(), ties=()):
     cx, span, chan = base[0].shape
-    cy = base[1].shape[1]
-    edge = pltpu.VMEM((cx * span // cy, chan), BF16)
-    return pl.pallas_call(
-        functools.partial(opening_kernel, rows),
-        in_specs=[IN_VMEM] * 5,
-        out_specs=[IN_VMEM] * 4,
-        out_shape=[pltpu.VMEM((cx, span, 2 * chan), BF16), pltpu.VMEM(pooled.shape, BF16), edge, edge],
-        compiler_params=params(16),
-        cost_estimate=estimate(len(rows)),
-        name="opening",
-    )(*base, pooled)
-
-
-def piece(kernel, rows_done, name, base, out, near=(), ties=()):
+    done = [] if out is None else [out]
     return pl.pallas_call(
         kernel,
-        in_specs=[IN_VMEM] * (5 + len(near)) + [pl.BlockSpec(memory_space=pl.ANY)] * len(ties),
+        in_specs=[IN_VMEM] * (4 + len(done) + len(near)) + [pl.BlockSpec(memory_space=pl.ANY)] * len(ties),
         out_specs=IN_VMEM,
-        out_shape=pltpu.VMEM(out.shape, BF16),
-        input_output_aliases={4: 0},
+        out_shape=pltpu.VMEM((cx, span, 2 * chan), BF16),
+        input_output_aliases={4: 0} if done else {},
         compiler_params=params(16),
         cost_estimate=estimate(rows_done),
         name=name,
-    )(*base, out, *near, *ties)
+    )(*base, *done, *near, *ties)
 
 
 def final_kernel(nx, ny, n_blocks, *refs):
@@ -379,26 +361,32 @@
 def per_device(features, tile_mask, pool_map, readers, w_query, w_key, w_value, w_cquery, w_ckey, w_cvalue):
     cx, cy, tile, chan = features.shape
     nx, ny = lax.axis_size("gx"), lax.axis_size("gy")
-    *base, pooled = pool(nx, ny, features, tile_mask, pool_map, w_query, w_key)
+    *base, pooled, left_edge, right_edge = pool(nx, ny, features, tile_mask, pool_map, w_query, w_key)
     fv = base[0]
     cuts = [1] + [1 + (cx - 2) * part // 14 for part in CUTS] + [cx - 1]
     rows = [range(lo, hi) for lo, hi in zip(cuts, cuts[1:])]
-    out, pooled, left_edge, right_edge = opening(rows[0], base, pooled)
+    steps = [("gx", 1 << b) for b in range(nx.bit_length() - 1)]
+    steps += [("gy", 1 << b) for b in range(1, ny.bit_length() - 1)] + [("gy", 1)]
     left = shift(right_edge, "gy", 1)
     right = shift(left_edge, "gy", -1)
-    blocks = [pooled] + [swap(pooled, "gx", bits) for bits in range(1, nx)]
-    out = piece(functools.partial(inner_kernel, rows[1]), len(rows[1]), "inner", base, out, (), (pooled,))
-    up, down = edge_rows(tile, fv, left, right, (out,))
-    above = shift(up, "gx", 1)
-    below = shift(down, "gx", -1)
-    part = join(blocks, (out, up))
-    blocks = [part] + [swap(part, "gy", bits) for bits in range(2, ny, 2)]
-    out = piece(functools.partial(inner_kernel, rows[2]), len(rows[2]), "middle", base, out, (), (part, up))
-    part = join(blocks, (out,))
-    blocks = [part, swap(part, "gy", 1)]
-    out = piece(functools.partial(sides_kernel, rows[3]), len(rows[3]) + 3.5, "sides", base, out, (left, right), (part,))
-    out = piece(ends_kernel, 2, "ends", base, out, (left, right, above, below))
-    update = final(nx, ny, blocks, readers, w_cquery, w_ckey, w_cvalue, w_value, out)
+    out, first, ties = None, pooled, (pooled,)
+    for step, (axis, bit) in enumerate(steps):
+        second = swap(first, axis, bit)
+        if step == 1:
+            up, down = edge_rows(tile, fv, left, right, (out,))
+            above = shift(up, "gx", 1)
+            below = shift(down, "gx", -1)
+            ties += (up,)
+        if step == len(steps) - 1:
+            break
+        if step < len(rows) - 1:
+            kernel = functools.partial(inner_kernel, rows[step])
+            out = piece(kernel, len(rows[step]), f"inner_{step}", base, out, (), ties)
+        first = join((first, second), (out,))
+        ties = (first,)
+    out = piece(ends_kernel, 2, "ends", base, out, (left, right, above, below), ties)
+    out = piece(functools.partial(sides_kernel, rows[-1]), len(rows[-1]) + 3.5, "sides", base, out, (left, right))
+    update = final(nx, ny, (first, second), readers, w_cquery, w_ckey, w_cvalue, w_value, out)
     return update.reshape(features.shape)
 
 

time: 43.6 us -> 44.8 us (1.028)
  waiting for transfers between devices: 2.36 us -> 4.81 us
  starting transfers between devices: 15.7 us -> 14.6 us
    ppermute x4, waiting for transfers between devices: 0.01 us -> 4.46 us  [shift(): lax.ppermute(array, axis, [(i, (i + step) % count) for i in range(count)])]
    ppermute x7 -> x5, waiting for transfers between devices: 2.35 us -> 0.35 us  [swap(): lax.ppermute(array, axis, [(i, i ^ bits) for i in range(lax.axis_size(axi...]
    ppermute x7 -> x5, starting transfers between devices: 8.42 us -> 7.21 us  [swap(): lax.ppermute(array, axis, [(i, i ^ bits) for i in range(lax.axis_size(axi...]
    pallas_call x5 -> x6, Pallas kernels: 16.2 us -> 16.3 us  [piece(): pl.pallas_call(kernel, in_specs=[IN_VMEM] * (4 + len(done) + len(near)) +...]
  transfers between devices with their start and end apart: 11 -> 9, of which waited for: 1 -> 2; matrix products, arithmetic and copies ran while one was open for 0% -> 0% of each run, Pallas kernels for 34% -> 37%
where the time goes in v4:
time: 44.8 us; the launch traced here: 44.7 us
  Pallas kernels  24.9 us (56%)
  starting transfers between devices  14.6 us (33%)
  waiting for transfers between devices  4.81 us (11%)
    pallas_call x6, Pallas kernels, piece(): pl.pallas_call(kernel, in_specs=[IN_VMEM] * (4 + len(done) + len(near)) +...  16.3 us
    ppermute x4, starting transfers between devices, shift(): lax.ppermute(array, axis, [(i, (i + step) % count) for i in range(count)])  7.36 us
    ppermute x5, starting transfers between devices, swap(): lax.ppermute(array, axis, [(i, i ^ bits) for i in range(lax.axis_size(axi...  7.21 us
    pallas_call x1, Pallas kernels, pool(): pl.pallas_call(functools.partial(pool_kernel, tile, nx, ny), in_specs=[IN...  4.48 us
    ppermute x4, waiting for transfers between devices, shift(): lax.ppermute(array, axis, [(i, (i + step) % count) for i in range(count)])  4.46 us
    pallas_call x1, Pallas kernels, final(): pl.pallas_call(functools.partial(final_kernel, nx, ny, len(blocks)), in_s...  4.06 us
  transfers between devices with their start and end apart: 9, of which 2 were waited for; matrix products, arithmetic and copies ran while one was open for 0% of the time, Pallas kernels for 37%

profile of v4, /device:TPU:0, one launch (start us, length us, event | category | flops | bytes accessed | tf_op | source)
XLA Modules:
  0.0 44.7 jit_solution(14119275975473056538)
XLA Ops:
  0.0 4.5 %pool.1 = (bf16[16,1024,128]{2,1,0:T(8,128)(2,1)S(1)}, s32[16,16,64]{2,1,0:T(8,128)S(1)}, f32[256,768]{1,0:T(8,128)S(1)}, bf16[128,128]{1,0:T(8,128)(2,1)S(1)}, ...) custom-call(bf16[16,1024,128]{2,1,0:T(8,128)(2,1)} %bitcast.7, ...), custom_call_target="tpu_custom_call" | custom-call | tf_op jit(solution)/shard_map/pool/pallas_call | solution.py:94
  4.5 0.5 %collective-permute-start.2 = (bf16[1024,128]{1,0:T(8,128)(2,1)S(1)}, bf16[1024,128]{1,0:T(8,128)(2,1)S(1)}, u32[]{:S(2)}, u32[]{:S(2)}) collective-permute-start(bf16[1024,128]{1,0:T(8,128)(2,1)S(1)} %get-tuple-element.19), channel_id=1, source_target_pairs={{0,1},{1,2},{2,3},{3,4},{4,5},{5,6},{6,7},{7,0},{8,9},{9,10},{10,1... | collective-permute-start | bytes 786440 | tf_op jit(solution)/shard_map/ppermute | solution.py:312
  5.0 2.9 %collective-permute-start.3 = (bf16[1024,128]{1,0:T(8,128)(2,1)S(1)}, bf16[1024,128]{1,0:T(8,128)(2,1)S(1)}, u32[]{:S(2)}, u32[]{:S(2)}) collective-permute-start(bf16[1024,128]{1,0:T(8,128)(2,1)S(1)} %get-tuple-element.20), channel_id=1, source_target_pairs={{0,7},{1,0},{2,1},{3,2},{4,3},{5,4},{6,5},{7,6},{8,15},{9,8},{10,9... | collective-permute-start | bytes 786440 | tf_op jit(solution)/shard_map/ppermute | solution.py:312
  7.9 2.3 %collective-permute-start = (bf16[64,128]{1,0:T(8,128)(2,1)S(1)}, bf16[64,128]{1,0:T(8,128)(2,1)S(1)}, u32[]{:S(2)}, u32[]{:S(2)}) collective-permute-start(bf16[64,128]{1,0:T(8,128)(2,1)S(1)} %get-tuple-element.14.rest_0_.refs_0_), channel_id=1, source_target_pairs={{0,8},{8,0},{16,24},{24,16},{1,9},{9,1},{17,25},{25,17},{2,10},{10... | collective-permute-start | bytes 49160 | tf_op jit(solution)/shard_map/ppermute | solution.py:316
  10.2 3.1 %inner_0.1.refs_2_.rest_0_ = bf16[16,1024,256]{2,1,0:T(8,128)(2,1)S(1)} custom-call(bf16[16,1024,128]{2,1,0:T(8,128)(2,1)S(1)} %get-tuple-element.15.fv.fv_ref, s32[16,16,64]{2,1,0:T(8,128)S(1)} %get-tuple-element.16.pv, f32[256,768]{1,0:T(8,128)S(1)} %get-tuple-element.17.mv, bf16[128,128]{1,0:T(8,128)(2,1)S(1)} %get-tuple-element.18.m, ...), custom_call_target="tpu_custom_call" | custom-call | flops 1600000000 | bytes 1000000 | tf_op jit(solution)/shard_map/inner_0/pallas_call | solution.py:247
  13.3 2.7 %collective-permute-start.1 = (bf16[128,128]{1,0:T(8,128)(2,1)S(1)}, bf16[128,128]{1,0:T(8,128)(2,1)S(1)}, u32[]{:S(2)}, u32[]{:S(2)}) collective-permute-start(bf16[128,128]{1,0:T(8,128)(2,1)S(1)} %join.4.rest_1_.refs_0_), channel_id=1, source_target_pairs={{0,16},{8,24},{16,0},{24,8},{1,17},{9,25},{17,1},{25,9},{2,18},{10... | collective-permute-start | bytes 98312 | tf_op jit(solution)/shard_map/ppermute | solution.py:316
  16.0 2.3 %inner_1.1.refs_2_.rest_0_ = bf16[16,1024,256]{2,1,0:T(8,128)(2,1)S(1)} custom-call(bf16[16,1024,128]{2,1,0:T(8,128)(2,1)S(1)} %get-tuple-element.15.fv.fv_ref, s32[16,16,64]{2,1,0:T(8,128)S(1)} %get-tuple-element.16.pv, f32[256,768]{1,0:T(8,128)S(1)} %get-tuple-element.17.mv, ...), custom_call_target="tpu_custom_call", output_to_operand_aliasing={{}: (4, {})} | custom-call | flops 1200000000 | bytes 1000000 | tf_op jit(solution)/shard_map/inner_1/pallas_call | solution.py:247
  18.4 0.6 %collective-permute-start.7 = (bf16[1152,128]{1,0:T(8,128)(2,1)S(1)}, bf16[1152,128]{1,0:T(8,128)(2,1)S(1)}, u32[]{:S(2)}, u32[]{:S(2)}) collective-permute-start(bf16[1152,128]{1,0:T(8,128)(2,1)S(1)} %get-tuple-element.21.rest_2_), channel_id=1, source_target_pairs={{0,8},{8,16},{16,24},{24,0},{1,9},{9,17},{17,25},{25,1},{2,10},{10... | collective-permute-start | bytes 884744 | tf_op jit(solution)/shard_map/ppermute | solution.py:312
  19.0 0.6 %collective-permute-start.4 = (bf16[256,128]{1,0:T(8,128)(2,1)S(1)}, bf16[256,128]{1,0:T(8,128)(2,1)S(1)}, u32[]{:S(2)}, u32[]{:S(2)}) collective-permute-start(bf16[256,128]{1,0:T(8,128)(2,1)S(1)} %join.5.rest_1_.refs_0_), channel_id=1, source_target_pairs={{0,2},{1,3},{2,0},{3,1},{4,6},{5,7},{6,4},{7,5},{8,10},{9,11},{10,... | collective-permute-start | bytes 196616 | tf_op jit(solution)/shard_map/ppermute | solution.py:316
  19.7 3.3 %collective-permute-start.8 = (bf16[1152,128]{1,0:T(8,128)(2,1)S(1)}, bf16[1152,128]{1,0:T(8,128)(2,1)S(1)}, u32[]{:S(2)}, u32[]{:S(2)}) collective-permute-start(bf16[1152,128]{1,0:T(8,128)(2,1)S(1)} %get-tuple-element.22), channel_id=1, source_target_pairs={{0,24},{8,0},{16,8},{24,16},{1,25},{9,1},{17,9},{25,17},{2,26},{10... | collective-permute-start | bytes 884744 | tf_op jit(solution)/shard_map/ppermute | solution.py:312
  22.9 2.3 %inner_2.1.refs_2_.rest_0_ = bf16[16,1024,256]{2,1,0:T(8,128)(2,1)S(1)} custom-call(bf16[16,1024,128]{2,1,0:T(8,128)(2,1)S(1)} %get-tuple-element.15.fv.fv_ref, s32[16,16,64]{2,1,0:T(8,128)S(1)} %get-tuple-element.16.pv, f32[256,768]{1,0:T(8,128)S(1)} %get-tuple-element.17.mv, ...), custom_call_target="tpu_custom_call", output_to_operand_aliasing={{}: (4, {})} | custom-call | flops 1200000000 | bytes 1000000 | tf_op jit(solution)/shard_map/inner_2/pallas_call | solution.py:247
  25.3 1.6 %collective-permute-start.5 = (bf16[512,128]{1,0:T(8,128)(2,1)S(1)}, bf16[512,128]{1,0:T(8,128)(2,1)S(1)}, u32[]{:S(2)}, u32[]{:S(2)}) collective-permute-start(bf16[512,128]{1,0:T(8,128)(2,1)S(1)} %join.6.rest_1_.refs_0_), channel_id=1, source_target_pairs={{0,4},{1,5},{2,6},{3,7},{4,0},{5,1},{6,2},{7,3},{8,12},{9,13},{10,... | collective-permute-start | bytes 393224 | tf_op jit(solution)/shard_map/ppermute | solution.py:316
  26.9 3.1 %inner_3.1.refs_2_.out_in = bf16[16,1024,256]{2,1,0:T(8,128)(2,1)S(1)} custom-call(bf16[16,1024,128]{2,1,0:T(8,128)(2,1)S(1)} %get-tuple-element.15.fv.fv_ref, s32[16,16,64]{2,1,0:T(8,128)S(1)} %get-tuple-element.16.pv, f32[256,768]{1,0:T(8,128)S(1)} %get-tuple-element.17.mv, ...), custom_call_target="tpu_custom_call", output_to_operand_aliasing={{}: (4, {})} | custom-call | flops 1600000000 | bytes 1000000 | tf_op jit(solution)/shard_map/inner_3/pallas_call | solution.py:247
  30.0 0.3 collective-permute-done.5.refs_1_
  30.4 0.1 collective-permute-start.6
  30.5 4.5 %collective-permute-done.8.below = bf16[1152,128]{1,0:T(8,128)(2,1)S(1)} collective-permute-done((bf16[1152,128]{1,0:T(8,128)(2,1)S(1)}, bf16[1152,128]{1,0:T(8,128)(2,1)S(1)}, u32[]{:S(2)}, u32[]{:S(2)}) %collective-permute-start.8) | collective-permute-done | bytes 294944 | tf_op jit(solution)/shard_map/ppermute | solution.py:312
  34.9 2.0 %ends.1.out_in = bf16[16,1024,256]{2,1,0:T(8,128)(2,1)S(1)} custom-call(bf16[16,1024,128]{2,1,0:T(8,128)(2,1)S(1)} %get-tuple-element.15.fv.fv_ref, s32[16,16,64]{2,1,0:T(8,128)S(1)} %get-tuple-element.16.pv, f32[256,768]{1,0:T(8,128)S(1)} %get-tuple-element.17.mv, bf16[128,128]{1,0:T(8,128)(2,1)S(1)} %get-tuple-element.18.m, ...), custom_call_target="tpu_custom_call", output_to_operand_aliasing={{}: (4, {})} | custom-call | flops 800000000 | bytes 1000000 | tf_op jit(solution)/shard_map/ends/pallas_call | solution.py:247
  36.9 0.0 copy-start
  37.0 0.0 copy-start.1
  37.0 0.0 copy-start.2
  37.0 0.0 copy-start.3
  37.0 0.0 copy-start.4
  37.0 3.4 %sides.1.refs_7_ = bf16[16,1024,256]{2,1,0:T(8,128)(2,1)S(1)} custom-call(bf16[16,1024,128]{2,1,0:T(8,128)(2,1)S(1)} %get-tuple-element.15.fv.fv_ref, s32[16,16,64]{2,1,0:T(8,128)S(1)} %get-tuple-element.16.pv, f32[256,768]{1,0:T(8,128)S(1)} %get-tuple-element.17.mv, bf16[128,128]{1,0:T(8,128)(2,1)S(1)} %get-tuple-element.18.m, ...), custom_call_target="tpu_custom_call", output_to_operand_aliasing={{}: (4, {})} | custom-call | flops 1400000000 | bytes 1000000 | tf_op jit(solution)/shard_map/sides/pallas_call | solution.py:247
  40.5 4.1 %final.1 = bf16[16,1024,128]{2,1,0:T(8,128)(2,1)} custom-call(bf16[1024,128]{1,0:T(8,128)(2,1)S(1)} %join.7.rest_0_.refs_0_, bf16[1024,128]{1,0:T(8,128)(2,1)S(1)} %collective-permute-done.6.refs_1_, s32[8,32]{1,0:T(8,128)S(1)} %bitcast.6, bf16[128,128]{1,0:T(8,128)(2,1)S(1)} %copy-done, bf16[128,128]{1,0:T(8,128)(2,1)S(1)} %copy-done.1, ...), custom_call_target="tpu_custom_call" | custom-call | tf_op jit(solution)/shard_map/final/pallas_call | solution.py:295
  (17 shorter events, 0.1 us)
Async XLA Ops:
  4.5 11.5 %collective-permute-start.2 = (bf16[1024,128]{1,0:T(8,128)(2,1)S(1)}, bf16[1024,128]{1,0:T(8,128)(2,1)S(1)}, u32[]{:S(2)}, u32[]{:S(2)}) collective-permute-start(bf16[1024,128]{1,0:T(8,128)(2,1)S(1)} %get-tuple-element.19), channel_id=1, source_target_pairs={{0,1},{1,2},{2,3},{3,4},{4,5},{5,6},{6,7},{7,0},{8,9},{9,10},{10,1... | collective-permute-start | bytes 786440 | tf_op jit(solution)/shard_map/ppermute | solution.py:312
  5.0 11.0 %collective-permute-start.3 = (bf16[1024,128]{1,0:T(8,128)(2,1)S(1)}, bf16[1024,128]{1,0:T(8,128)(2,1)S(1)}, u32[]{:S(2)}, u32[]{:S(2)}) collective-permute-start(bf16[1024,128]{1,0:T(8,128)(2,1)S(1)} %get-tuple-element.20), channel_id=1, source_target_pairs={{0,7},{1,0},{2,1},{3,2},{4,3},{5,4},{6,5},{7,6},{8,15},{9,8},{10,9... | collective-permute-start | bytes 786440 | tf_op jit(solution)/shard_map/ppermute | solution.py:312
  7.9 5.4 %collective-permute-start = (bf16[64,128]{1,0:T(8,128)(2,1)S(1)}, bf16[64,128]{1,0:T(8,128)(2,1)S(1)}, u32[]{:S(2)}, u32[]{:S(2)}) collective-permute-start(bf16[64,128]{1,0:T(8,128)(2,1)S(1)} %get-tuple-element.14.rest_0_.refs_0_), channel_id=1, source_target_pairs={{0,8},{8,0},{16,24},{24,16},{1,9},{9,1},{17,25},{25,17},{2,10},{10... | collective-permute-start | bytes 49160 | tf_op jit(solution)/shard_map/ppermute | solution.py:316
  13.3 5.7 %collective-permute-start.1 = (bf16[128,128]{1,0:T(8,128)(2,1)S(1)}, bf16[128,128]{1,0:T(8,128)(2,1)S(1)}, u32[]{:S(2)}, u32[]{:S(2)}) collective-permute-start(bf16[128,128]{1,0:T(8,128)(2,1)S(1)} %join.4.rest_1_.refs_0_), channel_id=1, source_target_pairs={{0,16},{8,24},{16,0},{24,8},{1,17},{9,25},{17,1},{25,9},{2,18},{10... | collective-permute-start | bytes 98312 | tf_op jit(solution)/shard_map/ppermute | solution.py:316
  18.4 12.1 %collective-permute-start.7 = (bf16[1152,128]{1,0:T(8,128)(2,1)S(1)}, bf16[1152,128]{1,0:T(8,128)(2,1)S(1)}, u32[]{:S(2)}, u32[]{:S(2)}) collective-permute-start(bf16[1152,128]{1,0:T(8,128)(2,1)S(1)} %get-tuple-element.21.rest_2_), channel_id=1, source_target_pairs={{0,8},{8,16},{16,24},{24,0},{1,9},{9,17},{17,25},{25,1},{2,10},{10... | collective-permute-start | bytes 884744 | tf_op jit(solution)/shard_map/ppermute | solution.py:312
  19.0 6.2 %collective-permute-start.4 = (bf16[256,128]{1,0:T(8,128)(2,1)S(1)}, bf16[256,128]{1,0:T(8,128)(2,1)S(1)}, u32[]{:S(2)}, u32[]{:S(2)}) collective-permute-start(bf16[256,128]{1,0:T(8,128)(2,1)S(1)} %join.5.rest_1_.refs_0_), channel_id=1, source_target_pairs={{0,2},{1,3},{2,0},{3,1},{4,6},{5,7},{6,4},{7,5},{8,10},{9,11},{10,... | collective-permute-start | bytes 196616 | tf_op jit(solution)/shard_map/ppermute | solution.py:316
  19.7 15.2 %collective-permute-start.8 = (bf16[1152,128]{1,0:T(8,128)(2,1)S(1)}, bf16[1152,128]{1,0:T(8,128)(2,1)S(1)}, u32[]{:S(2)}, u32[]{:S(2)}) collective-permute-start(bf16[1152,128]{1,0:T(8,128)(2,1)S(1)} %get-tuple-element.22), channel_id=1, source_target_pairs={{0,24},{8,0},{16,8},{24,16},{1,25},{9,1},{17,9},{25,17},{2,26},{10... | collective-permute-start | bytes 884744 | tf_op jit(solution)/shard_map/ppermute | solution.py:312
  25.3 5.0 %collective-permute-start.5 = (bf16[512,128]{1,0:T(8,128)(2,1)S(1)}, bf16[512,128]{1,0:T(8,128)(2,1)S(1)}, u32[]{:S(2)}, u32[]{:S(2)}) collective-permute-start(bf16[512,128]{1,0:T(8,128)(2,1)S(1)} %join.6.rest_1_.refs_0_), channel_id=1, source_target_pairs={{0,4},{1,5},{2,6},{3,7},{4,0},{5,1},{6,2},{7,3},{8,12},{9,13},{10,... | collective-permute-start | bytes 393224 | tf_op jit(solution)/shard_map/ppermute | solution.py:316
  30.4 10.0 %collective-permute-start.6 = (bf16[1024,128]{1,0:T(8,128)(2,1)S(1)}, bf16[1024,128]{1,0:T(8,128)(2,1)S(1)}, u32[]{:S(2)}, u32[]{:S(2)}) collective-permute-start(bf16[1024,128]{1,0:T(8,128)(2,1)S(1)} %join.7.rest_0_.refs_0_), channel_id=1, source_target_pairs={{0,1},{1,0},{2,3},{3,2},{4,5},{5,4},{6,7},{7,6},{8,9},{9,8},{10,11... | collective-permute-start | bytes 786440 | tf_op jit(solution)/shard_map/ppermute | solution.py:316
  36.9 3.5 %copy-start = (bf16[128,128]{1,0:T(8,128)(2,1)S(1)}, bf16[128,128]{1,0:T(8,128)(2,1)}, u32[]{:S(2)}) copy-start(bf16[128,128]{1,0:T(8,128)(2,1)} %refs_3_.1) | copy-start | bytes 98308
  37.0 3.5 %copy-start.1 = (bf16[128,128]{1,0:T(8,128)(2,1)S(1)}, bf16[128,128]{1,0:T(8,128)(2,1)}, u32[]{:S(2)}) copy-start(bf16[128,128]{1,0:T(8,128)(2,1)} %refs_4_.1) | copy-start | bytes 98308
  37.0 3.5 %copy-start.2 = (bf16[128,128]{1,0:T(8,128)(2,1)S(1)}, bf16[128,128]{1,0:T(8,128)(2,1)}, u32[]{:S(2)}) copy-start(bf16[128,128]{1,0:T(8,128)(2,1)} %refs_5_.1) | copy-start | bytes 98308
  37.0 3.5 %copy-start.3 = (bf16[128,128]{1,0:T(8,128)(2,1)S(1)}, bf16[128,128]{1,0:T(8,128)(2,1)}, u32[]{:S(2)}) copy-start(bf16[128,128]{1,0:T(8,128)(2,1)} %refs_6_.1) | copy-start | bytes 98308
  37.0 3.5 %copy-start.4 = (s32[32,8]{0,1:T(8,128)S(1)}, s32[32,8]{0,1:T(8,128)}, u32[]{:S(2)}) copy-start(s32[32,8]{0,1:T(8,128)} %param.13) | copy-start | bytes 3076

commit v5 on v4

--- a/solution.py
+++ b/solution.py
@@ -12,7 +12,7 @@
 F32 = jnp.float32
 S = 64
 DEPTH = 2
-CUTS = (4, 7, 10, 14)
+CUTS = (4, 7, 9, 12)
 IN_VMEM = pl.BlockSpec(memory_space=pltpu.VMEM)
 IN_HBM = pl.BlockSpec(memory_space=pltpu.HBM)
 
@@ -42,13 +42,16 @@
     return jnp.concatenate([ids[:half], ids[half:]], axis=1)
 
 
-def pool_kernel(tile, nx, ny, f_ref, pm_ref, tm_ref, wq_ref, wk_ref, fv_ref, pv_ref, mv_ref, m_ref, pooled_ref, left_ref, right_ref, tv, wq, wk, sems):
-    rows, span, chan = fv_ref.shape
+def opening_kernel(tile, nx, ny, f_ref, tm_ref, wq_ref, wk_ref, mv_ref, m_ref, left_ref, right_ref, tv, wq, wk, sems):
+    rows, span, chan = f_ref.shape
     cy = span // tile
-    small = [(tm_ref, tv), (wq_ref, wq), (wk_ref, wk), (pm_ref, pv_ref)]
-    first = [pltpu.make_async_copy(src, dst, sems.at[rows + i]) for i, (src, dst) in enumerate(small)]
-    beads_in = [pltpu.make_async_copy(f_ref.at[r], fv_ref.at[r], sems.at[r]) for r in range(rows)]
-    for copy in first + beads_in:
+    first = [pltpu.make_async_copy(src, dst, sems.at[i]) for i, (src, dst) in enumerate([(tm_ref, tv), (wq_ref, wq), (wk_ref, wk)])]
+    columns = []
+    for r in range(rows):
+        for k, (ref, lo) in enumerate(((left_ref, 0), (right_ref, span - tile))):
+            there = ref.at[pl.ds(tile * r, tile)]
+            columns.append(pltpu.make_async_copy(f_ref.at[r, pl.ds(lo, tile)], there, sems.at[3 + 2 * r + k]))
+    for copy in first + columns:
         copy.start()
     block = lax.broadcasted_iota(jnp.int32, (18, 12 * tile), 1) // tile
     which = lax.broadcasted_iota(jnp.int32, (18, 12 * tile), 0)
@@ -70,10 +73,45 @@
     even = lane % 2 == 0
     both = jnp.concatenate([jnp.where(even, mask, 0.0), jnp.where(even, 0.0, mask)], axis=0)
     mv_ref[...] = t_dot(both.astype(BF16), pick)
-
+    for copy in columns:
+        copy.wait()
+
+
+def opening(nx, ny, features, tile_mask, w_query, w_key):
+    cx, cy, tile, chan = features.shape
+    edge = pltpu.VMEM((cx * tile, chan), BF16)
+    return pl.pallas_call(
+        functools.partial(opening_kernel, tile, nx, ny),
+        in_specs=[IN_HBM] * 4,
+        out_specs=[IN_VMEM] * 4,
+        out_shape=[pltpu.VMEM((cx * cy, 12 * tile), F32), pltpu.VMEM((chan, chan), BF16), edge, edge],
+        scratch_shapes=[
+            pltpu.VMEM((9 * cx, cy), jnp.int32),
+            pltpu.VMEM((chan, chan), BF16),
+            pltpu.VMEM((chan, chan), BF16),
+            pltpu.SemaphoreType.DMA((3 + 2 * cx,)),
+        ],
+        compiler_params=params(8),
+        name="opening",
+    )(
+        in_hbm(features.reshape(cx, cy * tile, chan)),
+        in_hbm(jnp.transpose(tile_mask, (2, 0, 1)).reshape(9 * cx, cy)),
+        in_hbm(w_query),
+        in_hbm(w_key),
+    )
+
+
+def pool_kernel(tile, f_ref, pm_ref, tie, fv_ref, pv_ref, pooled_ref, sems):
+    rows, span, chan = fv_ref.shape
+    cy = span // tile
+    ids_in = pltpu.make_async_copy(pm_ref, pv_ref, sems.at[rows])
+    beads_in = [pltpu.make_async_copy(f_ref.at[r], fv_ref.at[r], sems.at[r]) for r in range(rows)]
+    for copy in [ids_in] + beads_in:
+        copy.start()
     node = lax.broadcasted_iota(jnp.int32, (S, 2 * tile), 0)
     order = [c for i in range(cy // 2) for c in (i, i + cy // 2)]
     total = jnp.zeros((S, chan), F32)
+    ids_in.wait()
     for r in range(rows):
         pairs = paired(pv_ref[r])
         onehot = jnp.concatenate(
@@ -82,43 +120,26 @@
         )
         beads_in[r].wait()
         total += dot(onehot, jnp.concatenate([fv_ref[r, tile * c : tile * (c + 1)] for c in order], axis=0))
-        left_ref[tile * r : tile * (r + 1)] = fv_ref[r, :tile]
-        right_ref[tile * r : tile * (r + 1)] = fv_ref[r, span - tile :]
     pooled_ref[...] = (total * math.sqrt(S / (rows * span))).astype(BF16)
 
 
-def pool(nx, ny, features, tile_mask, pool_map, w_query, w_key):
+def pool(features, pool_map, tie):
     cx, cy, tile, chan = features.shape
     span = cy * tile
-    edge = pltpu.VMEM((cx * tile, chan), BF16)
-    return pl.pallas_call(
-        functools.partial(pool_kernel, tile, nx, ny),
-        in_specs=[IN_HBM] * 5,
-        out_specs=[IN_VMEM] * 7,
+    return pl.pallas_call(
+        functools.partial(pool_kernel, tile),
+        in_specs=[IN_HBM] * 2 + [pl.BlockSpec(memory_space=pl.ANY)],
+        out_specs=[IN_VMEM] * 3,
         out_shape=[
             pltpu.VMEM((cx, span, chan), BF16),
             pltpu.VMEM((cx, cy, tile), jnp.int32),
-            pltpu.VMEM((cx * cy, 12 * tile), F32),
-            pltpu.VMEM((chan, chan), BF16),
             pltpu.VMEM((S, chan), BF16),
-            edge,
-            edge,
         ],
-        scratch_shapes=[
-            pltpu.VMEM((9 * cx, cy), jnp.int32),
-            pltpu.VMEM((chan, chan), BF16),
-            pltpu.VMEM((chan, chan), BF16),
-            pltpu.SemaphoreType.DMA((cx + 4,)),
-        ],
-        compiler_params=params(16),
+        scratch_shapes=[pltpu.SemaphoreType.DMA((cx + 1,))],
+        compiler_params=params(8),
+        cost_estimate=estimate(4),
         name="pool",
-    )(
-        in_hbm(features.reshape(cx, span, chan)),
-        in_hbm(pool_map),
-        in_hbm(jnp.transpose(tile_mask, (2, 0, 1)).reshape(9 * cx, cy)),
-        in_hbm(w_query),
-        in_hbm(w_key),
-    )
+    )(in_hbm(features.reshape(cx, span, chan)), in_hbm(pool_map), tie)
 
 
 def attend(tile, tasks):
@@ -361,22 +382,21 @@
 def per_device(features, tile_mask, pool_map, readers, w_query, w_key, w_value, w_cquery, w_ckey, w_cvalue):
     cx, cy, tile, chan = features.shape
     nx, ny = lax.axis_size("gx"), lax.axis_size("gy")
-    *base, pooled, left_edge, right_edge = pool(nx, ny, features, tile_mask, pool_map, w_query, w_key)
-    fv = base[0]
+    mv, m, left_edge, right_edge = opening(nx, ny, features, tile_mask, w_query, w_key)
+    left = shift(right_edge, "gy", 1)
+    right = shift(left_edge, "gy", -1)
+    fv, pv, pooled = pool(features, pool_map, right_edge)
+    base = (fv, pv, mv, m)
     cuts = [1] + [1 + (cx - 2) * part // 14 for part in CUTS] + [cx - 1]
     rows = [range(lo, hi) for lo, hi in zip(cuts, cuts[1:])]
     steps = [("gx", 1 << b) for b in range(nx.bit_length() - 1)]
     steps += [("gy", 1 << b) for b in range(1, ny.bit_length() - 1)] + [("gy", 1)]
-    left = shift(right_edge, "gy", 1)
-    right = shift(left_edge, "gy", -1)
-    out, first, ties = None, pooled, (pooled,)
+    up, down = edge_rows(tile, fv, left, right, (pooled,))
+    above = shift(up, "gx", 1)
+    below = shift(down, "gx", -1)
+    out, first, ties = None, pooled, (pooled, up)
     for step, (axis, bit) in enumerate(steps):
         second = swap(first, axis, bit)
-        if step == 1:
-            up, down = edge_rows(tile, fv, left, right, (out,))
-            above = shift(up, "gx", 1)
-            below = shift(down, "gx", -1)
-            ties += (up,)
         if step == len(steps) - 1:
             break
         if step < len(rows) - 1:

time: 44.8 us -> 50 us (1.12)
  waiting for transfers between devices: 4.81 us -> 10.3 us
  starting transfers between devices: 14.6 us -> 12.9 us
  Pallas kernels: 24.9 us -> 26.3 us
    ppermute x5, waiting for transfers between devices: 0.35 us -> 8.23 us  [swap(): lax.ppermute(array, axis, [(i, i ^ bits) for i in range(lax.axis_size(axi...]
    ppermute x4, waiting for transfers between devices: 4.46 us -> 2.06 us  [shift(): lax.ppermute(array, axis, [(i, (i + step) % count) for i in range(count)])]
    ppermute x5, starting transfers between devices: 7.21 us -> 5.81 us  [swap(): lax.ppermute(array, axis, [(i, i ^ bits) for i in range(lax.axis_size(axi...]
    pallas_call x1 -> x2, Pallas kernels: 4.48 us -> 5.66 us  [the longest x1 4.01 us: pool(): pl.pallas_call(functools.partial(pool_kernel, tile), in_specs=[IN_HBM] *...]
  transfers between devices with their start and end apart: 9 -> 9, of which waited for: 2 -> 5; matrix products, arithmetic and copies ran while one was open for 0% -> 0% of each run, Pallas kernels for 37% -> 41%
where the time goes in v5:
time: 50 us; the launch traced here: 49.9 us
  Pallas kernels  26.3 us (53%)
  starting transfers between devices  12.9 us (26%)
  waiting for transfers between devices  10.3 us (21%)
    pallas_call x6, Pallas kernels, piece(): pl.pallas_call(kernel, in_specs=[IN_VMEM] * (4 + len(done) + len(near)) +...  16.5 us
    ppermute x5, waiting for transfers between devices, swap(): lax.ppermute(array, axis, [(i, i ^ bits) for i in range(lax.axis_size(axi...  8.23 us
    ppermute x4, starting transfers between devices, shift(): lax.ppermute(array, axis, [(i, (i + step) % count) for i in range(count)])  7.05 us
    ppermute x5, starting transfers between devices, swap(): lax.ppermute(array, axis, [(i, i ^ bits) for i in range(lax.axis_size(axi...  5.81 us
    pallas_call x1, Pallas kernels, final(): pl.pallas_call(functools.partial(final_kernel, nx, ny, len(blocks)), in_s...  4.08 us
    pallas_call x1, Pallas kernels, pool(): pl.pallas_call(functools.partial(pool_kernel, tile), in_specs=[IN_HBM] *...  4.01 us
    ppermute x4, waiting for transfers between devices, shift(): lax.ppermute(array, axis, [(i, (i + step) % count) for i in range(count)])  2.06 us
    pallas_call x1, Pallas kernels, opening(): pl.pallas_call(functools.partial(opening_kernel, tile, nx, ny), in_specs=...  1.66 us
  transfers between devices with their start and end apart: 9, of which 5 were waited for; matrix products, arithmetic and copies ran while one was open for 0% of the time, Pallas kernels for 41%

profile of v5, /device:TPU:0, one launch (start us, length us, event | category | flops | bytes accessed | tf_op | source)
XLA Modules:
  0.0 49.9 jit_solution(4998032488640591869)
XLA Ops:
  0.0 1.7 %opening.1 = (f32[256,768]{1,0:T(8,128)S(1)}, bf16[128,128]{1,0:T(8,128)(2,1)S(1)}, bf16[1024,128]{1,0:T(8,128)(2,1)S(1)}, bf16[1024,128]{1,0:T(8,128)(2,1)S(1)}) custom-call(bf16[16,1024,128]{2,1,0:T(8,128)(2,1)} %bitcast.7, s32[144,16]{1,0:T(8,128)} %bitcast.9, bf16[128,128]{1,0:T(8,128)(2,1)} %wq_ref.1, bf16[128,128]{1,0:T(8,128)(2,1)} %wk_ref.1), custom_call_target="tpu_custom_call" | custom-call | tf_op jit(solution)/shard_map/opening/pallas_call | solution.py:83
  1.7 3.4 %collective-permute-start.2 = (bf16[1024,128]{1,0:T(8,128)(2,1)S(1)}, bf16[1024,128]{1,0:T(8,128)(2,1)S(1)}, u32[]{:S(2)}, u32[]{:S(2)}) collective-permute-start(bf16[1024,128]{1,0:T(8,128)(2,1)S(1)} %get-tuple-element.20), channel_id=1, source_target_pairs={{0,7},{1,0},{2,1},{3,2},{4,3},{5,4},{6,5},{7,6},{8,15},{9,8},{10,9... | collective-permute-start | bytes 786440 | tf_op jit(solution)/shard_map/ppermute | solution.py:333
  5.1 4.0 %pool.1 = (bf16[16,1024,128]{2,1,0:T(8,128)(2,1)S(1)}, s32[16,16,64]{2,1,0:T(8,128)S(1)}, bf16[64,128]{1,0:T(8,128)(2,1)S(1)}) custom-call(bf16[16,1024,128]{2,1,0:T(8,128)(2,1)} %bitcast.8, s32[16,16,64]{2,1,0:T(8,128)} %pm_ref.1, bf16[1024,128]{1,0:T(8,128)(2,1)S(1)} %get-tuple-element.14.tie), custom_call_target="tpu_custom_call" | custom-call | flops 1600000000 | bytes 1000000 | tf_op jit(solution)/shard_map/pool/pallas_call | solution.py:129
  9.1 1.6 %collective-permute-start = (bf16[64,128]{1,0:T(8,128)(2,1)S(1)}, bf16[64,128]{1,0:T(8,128)(2,1)S(1)}, u32[]{:S(2)}, u32[]{:S(2)}) collective-permute-start(bf16[64,128]{1,0:T(8,128)(2,1)S(1)} %get-tuple-element.15.rest_0_.refs_0_), channel_id=1, source_target_pairs={{0,8},{8,0},{16,24},{24,16},{1,9},{9,1},{17,25},{25,17},{2,10},{10... | collective-permute-start | bytes 49160 | tf_op jit(solution)/shard_map/ppermute | solution.py:337
  10.7 0.1 collective-permute-done.2.right_ref.right
  10.8 1.9 %collective-permute-done.1.left_ref.left = bf16[1024,128]{1,0:T(8,128)(2,1)S(1)} collective-permute-done((bf16[1024,128]{1,0:T(8,128)(2,1)S(1)}, bf16[1024,128]{1,0:T(8,128)(2,1)S(1)}, u32[]{:S(2)}, u32[]{:S(2)}) %collective-permute-start.1) | collective-permute-done | bytes 262176 | tf_op jit(solution)/shard_map/ppermute | solution.py:333
  12.8 3.7 %collective-permute-start.8 = (bf16[1152,128]{1,0:T(8,128)(2,1)S(1)}, bf16[1152,128]{1,0:T(8,128)(2,1)S(1)}, u32[]{:S(2)}, u32[]{:S(2)}) collective-permute-start(bf16[1152,128]{1,0:T(8,128)(2,1)S(1)} %get-tuple-element.22), channel_id=1, source_target_pairs={{0,24},{8,0},{16,8},{24,16},{1,25},{9,1},{17,9},{25,17},{2,26},{10... | collective-permute-start | bytes 884744 | tf_op jit(solution)/shard_map/ppermute | solution.py:333
  16.5 3.1 %inner_0.1.refs_2_.rest_0_ = bf16[16,1024,256]{2,1,0:T(8,128)(2,1)S(1)} custom-call(bf16[16,1024,128]{2,1,0:T(8,128)(2,1)S(1)} %get-tuple-element.16.fv_ref.fv, s32[16,16,64]{2,1,0:T(8,128)S(1)} %get-tuple-element.17.pv, f32[256,768]{1,0:T(8,128)S(1)} %get-tuple-element.18.mv, bf16[128,128]{1,0:T(8,128)(2,1)S(1)} %get-tuple-element.19.m, ...), custom_call_target="tpu_custom_call" | custom-call | flops 1600000000 | bytes 1000000 | tf_op jit(solution)/shard_map/inner_0/pallas_call | solution.py:268
  19.6 1.1 %collective-permute-start.3 = (bf16[128,128]{1,0:T(8,128)(2,1)S(1)}, bf16[128,128]{1,0:T(8,128)(2,1)S(1)}, u32[]{:S(2)}, u32[]{:S(2)}) collective-permute-start(bf16[128,128]{1,0:T(8,128)(2,1)S(1)} %join.4.rest_1_.refs_0_), channel_id=1, source_target_pairs={{0,16},{8,24},{16,0},{24,8},{1,17},{9,25},{17,1},{25,9},{2,18},{10... | collective-permute-start | bytes 98312 | tf_op jit(solution)/shard_map/ppermute | solution.py:337
  20.7 2.3 %inner_1.1.refs_2_.rest_0_ = bf16[16,1024,256]{2,1,0:T(8,128)(2,1)S(1)} custom-call(bf16[16,1024,128]{2,1,0:T(8,128)(2,1)S(1)} %get-tuple-element.16.fv_ref.fv, s32[16,16,64]{2,1,0:T(8,128)S(1)} %get-tuple-element.17.pv, f32[256,768]{1,0:T(8,128)S(1)} %get-tuple-element.18.mv, ...), custom_call_target="tpu_custom_call", output_to_operand_aliasing={{}: (4, {})} | custom-call | flops 1200000000 | bytes 1000000 | tf_op jit(solution)/shard_map/inner_1/pallas_call | solution.py:268
  23.0 5.3 %collective-permute-done.3.refs_1_ = bf16[128,128]{1,0:T(8,128)(2,1)S(1)} collective-permute-done((bf16[128,128]{1,0:T(8,128)(2,1)S(1)}, bf16[128,128]{1,0:T(8,128)(2,1)S(1)}, u32[]{:S(2)}, u32[]{:S(2)}) %collective-permute-start.3) | collective-permute-done | bytes 32800 | tf_op jit(solution)/shard_map/ppermute | solution.py:337
  28.3 1.9 %collective-permute-start.4 = (bf16[256,128]{1,0:T(8,128)(2,1)S(1)}, bf16[256,128]{1,0:T(8,128)(2,1)S(1)}, u32[]{:S(2)}, u32[]{:S(2)}) collective-permute-start(bf16[256,128]{1,0:T(8,128)(2,1)S(1)} %join.5.rest_1_.refs_0_), channel_id=1, source_target_pairs={{0,2},{1,3},{2,0},{3,1},{4,6},{5,7},{6,4},{7,5},{8,10},{9,11},{10,... | collective-permute-start | bytes 196616 | tf_op jit(solution)/shard_map/ppermute | solution.py:337
  30.2 1.6 %inner_2.1.refs_2_.rest_0_ = bf16[16,1024,256]{2,1,0:T(8,128)(2,1)S(1)} custom-call(bf16[16,1024,128]{2,1,0:T(8,128)(2,1)S(1)} %get-tuple-element.16.fv_ref.fv, s32[16,16,64]{2,1,0:T(8,128)S(1)} %get-tuple-element.17.pv, f32[256,768]{1,0:T(8,128)S(1)} %get-tuple-element.18.mv, ...), custom_call_target="tpu_custom_call", output_to_operand_aliasing={{}: (4, {})} | custom-call | flops 800000000 | bytes 1000000 | tf_op jit(solution)/shard_map/inner_2/pallas_call | solution.py:268
  31.8 1.1 %collective-permute-done.4.refs_1_ = bf16[256,128]{1,0:T(8,128)(2,1)S(1)} collective-permute-done((bf16[256,128]{1,0:T(8,128)(2,1)S(1)}, bf16[256,128]{1,0:T(8,128)(2,1)S(1)}, u32[]{:S(2)}, u32[]{:S(2)}) %collective-permute-start.4) | collective-permute-done | bytes 65568 | tf_op jit(solution)/shard_map/ppermute | solution.py:337
  33.0 1.1 %collective-permute-start.5 = (bf16[512,128]{1,0:T(8,128)(2,1)S(1)}, bf16[512,128]{1,0:T(8,128)(2,1)S(1)}, u32[]{:S(2)}, u32[]{:S(2)}) collective-permute-start(bf16[512,128]{1,0:T(8,128)(2,1)S(1)} %join.6.rest_1_.refs_0_), channel_id=1, source_target_pairs={{0,4},{1,5},{2,6},{3,7},{4,0},{5,1},{6,2},{7,3},{8,12},{9,13},{10,... | collective-permute-start | bytes 393224 | tf_op jit(solution)/shard_map/ppermute | solution.py:337
  34.1 2.3 %inner_3.1.refs_2_.out_in = bf16[16,1024,256]{2,1,0:T(8,128)(2,1)S(1)} custom-call(bf16[16,1024,128]{2,1,0:T(8,128)(2,1)S(1)} %get-tuple-element.16.fv_ref.fv, s32[16,16,64]{2,1,0:T(8,128)S(1)} %get-tuple-element.17.pv, f32[256,768]{1,0:T(8,128)S(1)} %get-tuple-element.18.mv, ...), custom_call_target="tpu_custom_call", output_to_operand_aliasing={{}: (4, {})} | custom-call | flops 1200000000 | bytes 1000000 | tf_op jit(solution)/shard_map/inner_3/pallas_call | solution.py:268
  36.5 1.8 %collective-permute-done.5.refs_1_ = bf16[512,128]{1,0:T(8,128)(2,1)S(1)} collective-permute-done((bf16[512,128]{1,0:T(8,128)(2,1)S(1)}, bf16[512,128]{1,0:T(8,128)(2,1)S(1)}, u32[]{:S(2)}, u32[]{:S(2)}) %collective-permute-start.5) | collective-permute-done | bytes 131104 | tf_op jit(solution)/shard_map/ppermute | solution.py:337
  38.3 0.1 collective-permute-start.6
  38.4 2.0 %ends.1.out_in = bf16[16,1024,256]{2,1,0:T(8,128)(2,1)S(1)} custom-call(bf16[16,1024,128]{2,1,0:T(8,128)(2,1)S(1)} %get-tuple-element.16.fv_ref.fv, s32[16,16,64]{2,1,0:T(8,128)S(1)} %get-tuple-element.17.pv, f32[256,768]{1,0:T(8,128)S(1)} %get-tuple-element.18.mv, bf16[128,128]{1,0:T(8,128)(2,1)S(1)} %get-tuple-element.19.m, ...), custom_call_target="tpu_custom_call", output_to_operand_aliasing={{}: (4, {})} | custom-call | flops 800000000 | bytes 1000000 | tf_op jit(solution)/shard_map/ends/pallas_call | solution.py:268
  40.4 0.0 copy-start
  40.4 0.0 copy-start.1
  40.5 0.0 copy-start.2
  40.5 5.0 %sides.1.refs_7_ = bf16[16,1024,256]{2,1,0:T(8,128)(2,1)S(1)} custom-call(bf16[16,1024,128]{2,1,0:T(8,128)(2,1)S(1)} %get-tuple-element.16.fv_ref.fv, s32[16,16,64]{2,1,0:T(8,128)S(1)} %get-tuple-element.17.pv, f32[256,768]{1,0:T(8,128)S(1)} %get-tuple-element.18.mv, bf16[128,128]{1,0:T(8,128)(2,1)S(1)} %get-tuple-element.19.m, ...), custom_call_target="tpu_custom_call", output_to_operand_aliasing={{}: (4, {})} | custom-call | flops 2200000000 | bytes 1000000 | tf_op jit(solution)/shard_map/sides/pallas_call | solution.py:268
  45.6 4.1 %final.1 = bf16[16,1024,128]{2,1,0:T(8,128)(2,1)} custom-call(bf16[1024,128]{1,0:T(8,128)(2,1)S(1)} %join.7.rest_0_.refs_0_, bf16[1024,128]{1,0:T(8,128)(2,1)S(1)} %collective-permute-done.6.refs_1_, s32[8,32]{1,0:T(8,128)S(1)} %bitcast.6, bf16[128,128]{1,0:T(8,128)(2,1)S(1)} %copy-done, bf16[128,128]{1,0:T(8,128)(2,1)S(1)} %copy-done.1, ...), custom_call_target="tpu_custom_call" | custom-call | tf_op jit(solution)/shard_map/final/pallas_call | solution.py:316
  (18 shorter events, 0.1 us)
Async XLA Ops:
  1.7 9.2 %collective-permute-start.2 = (bf16[1024,128]{1,0:T(8,128)(2,1)S(1)}, bf16[1024,128]{1,0:T(8,128)(2,1)S(1)}, u32[]{:S(2)}, u32[]{:S(2)}) collective-permute-start(bf16[1024,128]{1,0:T(8,128)(2,1)S(1)} %get-tuple-element.20), channel_id=1, source_target_pairs={{0,7},{1,0},{2,1},{3,2},{4,3},{5,4},{6,5},{7,6},{8,15},{9,8},{10,9... | collective-permute-start | bytes 786440 | tf_op jit(solution)/shard_map/ppermute | solution.py:333
  5.1 7.7 %collective-permute-start.1 = (bf16[1024,128]{1,0:T(8,128)(2,1)S(1)}, bf16[1024,128]{1,0:T(8,128)(2,1)S(1)}, u32[]{:S(2)}, u32[]{:S(2)}) collective-permute-start(bf16[1024,128]{1,0:T(8,128)(2,1)S(1)} %get-tuple-element.14.tie), channel_id=1, source_target_pairs={{0,1},{1,2},{2,3},{3,4},{4,5},{5,6},{6,7},{7,0},{8,9},{9,10},{10,1... | collective-permute-start | bytes 786440 | tf_op jit(solution)/shard_map/ppermute | solution.py:333
  9.1 10.5 %collective-permute-start = (bf16[64,128]{1,0:T(8,128)(2,1)S(1)}, bf16[64,128]{1,0:T(8,128)(2,1)S(1)}, u32[]{:S(2)}, u32[]{:S(2)}) collective-permute-start(bf16[64,128]{1,0:T(8,128)(2,1)S(1)} %get-tuple-element.15.rest_0_.refs_0_), channel_id=1, source_target_pairs={{0,8},{8,0},{16,24},{24,16},{1,9},{9,1},{17,25},{25,17},{2,10},{10... | collective-permute-start | bytes 49160 | tf_op jit(solution)/shard_map/ppermute | solution.py:337
  12.8 25.6 %collective-permute-start.8 = (bf16[1152,128]{1,0:T(8,128)(2,1)S(1)}, bf16[1152,128]{1,0:T(8,128)(2,1)S(1)}, u32[]{:S(2)}, u32[]{:S(2)}) collective-permute-start(bf16[1152,128]{1,0:T(8,128)(2,1)S(1)} %get-tuple-element.22), channel_id=1, source_target_pairs={{0,24},{8,0},{16,8},{24,16},{1,25},{9,1},{17,9},{25,17},{2,26},{10... | collective-permute-start | bytes 884744 | tf_op jit(solution)/shard_map/ppermute | solution.py:333
  16.5 21.9 %collective-permute-start.7 = (bf16[1152,128]{1,0:T(8,128)(2,1)S(1)}, bf16[1152,128]{1,0:T(8,128)(2,1)S(1)}, u32[]{:S(2)}, u32[]{:S(2)}) collective-permute-start(bf16[1152,128]{1,0:T(8,128)(2,1)S(1)} %get-tuple-element.21.rest_1_), channel_id=1, source_target_pairs={{0,8},{8,16},{16,24},{24,0},{1,9},{9,17},{17,25},{25,1},{2,10},{10... | collective-permute-start | bytes 884744 | tf_op jit(solution)/shard_map/ppermute | solution.py:333
  19.6 8.7 %collective-permute-start.3 = (bf16[128,128]{1,0:T(8,128)(2,1)S(1)}, bf16[128,128]{1,0:T(8,128)(2,1)S(1)}, u32[]{:S(2)}, u32[]{:S(2)}) collective-permute-start(bf16[128,128]{1,0:T(8,128)(2,1)S(1)} %join.4.rest_1_.refs_0_), channel_id=1, source_target_pairs={{0,16},{8,24},{16,0},{24,8},{1,17},{9,25},{17,1},{25,9},{2,18},{10... | collective-permute-start | bytes 98312 | tf_op jit(solution)/shard_map/ppermute | solution.py:337
  28.3 4.7 %collective-permute-start.4 = (bf16[256,128]{1,0:T(8,128)(2,1)S(1)}, bf16[256,128]{1,0:T(8,128)(2,1)S(1)}, u32[]{:S(2)}, u32[]{:S(2)}) collective-permute-start(bf16[256,128]{1,0:T(8,128)(2,1)S(1)} %join.5.rest_1_.refs_0_), channel_id=1, source_target_pairs={{0,2},{1,3},{2,0},{3,1},{4,6},{5,7},{6,4},{7,5},{8,10},{9,11},{10,... | collective-permute-start | bytes 196616 | tf_op jit(solution)/shard_map/ppermute | solution.py:337
  33.0 5.3 %collective-permute-start.5 = (bf16[512,128]{1,0:T(8,128)(2,1)S(1)}, bf16[512,128]{1,0:T(8,128)(2,1)S(1)}, u32[]{:S(2)}, u32[]{:S(2)}) collective-permute-start(bf16[512,128]{1,0:T(8,128)(2,1)S(1)} %join.6.rest_1_.refs_0_), channel_id=1, source_target_pairs={{0,4},{1,5},{2,6},{3,7},{4,0},{5,1},{6,2},{7,3},{8,12},{9,13},{10,... | collective-permute-start | bytes 393224 | tf_op jit(solution)/shard_map/ppermute | solution.py:337
  38.3 7.3 %collective-permute-start.6 = (bf16[1024,128]{1,0:T(8,128)(2,1)S(1)}, bf16[1024,128]{1,0:T(8,128)(2,1)S(1)}, u32[]{:S(2)}, u32[]{:S(2)}) collective-permute-start(bf16[1024,128]{1,0:T(8,128)(2,1)S(1)} %join.7.rest_0_.refs_0_), channel_id=1, source_target_pairs={{0,1},{1,0},{2,3},{3,2},{4,5},{5,4},{6,7},{7,6},{8,9},{9,8},{10,11... | collective-permute-start | bytes 786440 | tf_op jit(solution)/shard_map/ppermute | solution.py:337
  40.4 5.1 %copy-start = (bf16[128,128]{1,0:T(8,128)(2,1)S(1)}, bf16[128,128]{1,0:T(8,128)(2,1)}, u32[]{:S(2)}) copy-start(bf16[128,128]{1,0:T(8,128)(2,1)} %refs_3_.1) | copy-start | bytes 98308
  40.4 5.1 %copy-start.1 = (bf16[128,128]{1,0:T(8,128)(2,1)S(1)}, bf16[128,128]{1,0:T(8,128)(2,1)}, u32[]{:S(2)}) copy-start(bf16[128,128]{1,0:T(8,128)(2,1)} %refs_4_.1) | copy-start | bytes 98308
  40.5 5.1 %copy-start.2 = (bf16[128,128]{1,0:T(8,128)(2,1)S(1)}, bf16[128,128]{1,0:T(8,128)(2,1)}, u32[]{:S(2)}) copy-start(bf16[128,128]{1,0:T(8,128)(2,1)} %refs_5_.1) | copy-start | bytes 98308
  40.5 5.1 %copy-start.3 = (bf16[128,128]{1,0:T(8,128)(2,1)S(1)}, bf16[128,128]{1,0:T(8,128)(2,1)}, u32[]{:S(2)}) copy-start(bf16[128,128]{1,0:T(8,128)(2,1)} %refs_6_.1) | copy-start | bytes 98308
  40.5 5.1 %copy-start.4 = (s32[32,8]{0,1:T(8,128)S(1)}, s32[32,8]{0,1:T(8,128)}, u32[]{:S(2)}) copy-start(s32[32,8]{0,1:T(8,128)} %param.13) | copy-start | bytes 3076

commit v6 on v4

--- a/solution.py
+++ b/solution.py
@@ -12,7 +12,7 @@
 F32 = jnp.float32
 S = 64
 DEPTH = 2
-CUTS = (4, 7, 10, 14)
+CUTS = (4, 6, 9, 13)
 IN_VMEM = pl.BlockSpec(memory_space=pltpu.VMEM)
 IN_HBM = pl.BlockSpec(memory_space=pltpu.HBM)
 
@@ -219,11 +219,23 @@
     attend(tile, tasks)
 
 
-def ends_kernel(fv, pv, mv, m, out_in, left, right, above, below, *rest):
+def ends_kernel(fv, pv, mv, m, out_in, left, right, paired_row, other_row, *rest):
+    *_, o, above, below = rest
     cy, tile = pv.shape[1:]
     rows = fv.shape[0]
-    refs = (fv, pv, mv, m, rest[-1])
+    refs = (fv, pv, mv, m, o)
     near = side_window(fv, tile, left, right)
+    odd = lax.axis_index("gx") % 2 == 1
+
+    @pl.when(odd)
+    def _():
+        above[...] = paired_row[...]
+        below[...] = other_row[...]
+
+    @pl.when(jnp.logical_not(odd))
+    def _():
+        above[...] = other_row[...]
+        below[...] = paired_row[...]
 
     def window(r, j):
         if r in (-1, rows):
@@ -241,7 +253,7 @@
     return pl.CostEstimate(flops=int(rows * 400_000_000), bytes_accessed=1_000_000, transcendentals=0)
 
 
-def piece(kernel, rows_done, name, base, out, near=(), ties=()):
+def piece(kernel, rows_done, name, base, out, near=(), ties=(), scratch=()):
     cx, span, chan = base[0].shape
     done = [] if out is None else [out]
     return pl.pallas_call(
@@ -249,6 +261,7 @@
         in_specs=[IN_VMEM] * (4 + len(done) + len(near)) + [pl.BlockSpec(memory_space=pl.ANY)] * len(ties),
         out_specs=IN_VMEM,
         out_shape=pltpu.VMEM((cx, span, 2 * chan), BF16),
+        scratch_shapes=list(scratch),
         input_output_aliases={4: 0} if done else {},
         compiler_params=params(16),
         cost_estimate=estimate(rows_done),
@@ -337,12 +350,15 @@
 
 
 def edge_rows_kernel(tile, fv_ref, left_ref, right_ref, *rest):
-    up_ref, down_ref = rest[-2:]
+    to_refs = rest[-2:]
     rows, span, _ = fv_ref.shape
-    for ref, r in ((up_ref, rows - 1), (down_ref, 0)):
-        ref[:tile] = left_ref[tile * r : tile * (r + 1)]
+    odd = lax.axis_index("gx") % 2
+    for ref, low in ((to_refs[0], odd), (to_refs[1], 1 - odd)):
+        r = (1 - low) * (rows - 1)
+        corner = pl.ds(pl.multiple_of(tile * r, tile), tile)
+        ref[:tile] = left_ref[corner]
         ref[tile : tile + span] = fv_ref[r]
-        ref[tile + span :] = right_ref[tile * r : tile * (r + 1)]
+        ref[tile + span :] = right_ref[corner]
 
 
 def edge_rows(tile, fv, left, right, ties):
@@ -356,6 +372,16 @@
         compiler_params=params(4),
         name="edge_rows",
     )(fv, left, right, *ties)
+
+
+def swap_across(array, nx, ny):
+    moves = []
+    for x in range(nx):
+        for y in range(ny):
+            near = x + 1 if x % 2 else x - 1
+            there = near * ny + y if 0 <= near < nx else x * ny + (y ^ 1)
+            moves.append((x * ny + y, there))
+    return lax.ppermute(array, ("gx", "gy"), moves)
 
 
 def per_device(features, tile_mask, pool_map, readers, w_query, w_key, w_value, w_cquery, w_ckey, w_cvalue):
@@ -373,10 +399,10 @@
     for step, (axis, bit) in enumerate(steps):
         second = swap(first, axis, bit)
         if step == 1:
-            up, down = edge_rows(tile, fv, left, right, (out,))
-            above = shift(up, "gx", 1)
-            below = shift(down, "gx", -1)
-            ties += (up,)
+            inward, outward = edge_rows(tile, fv, left, right, (out,))
+            paired_row = swap(inward, "gx", 1)
+            other_row = swap_across(outward, nx, ny)
+            ties += (inward,)
         if step == len(steps) - 1:
             break
         if step < len(rows) - 1:
@@ -384,7 +410,7 @@
             out = piece(kernel, len(rows[step]), f"inner_{step}", base, out, (), ties)
         first = join((first, second), (out,))
         ties = (first,)
-    out = piece(ends_kernel, 2, "ends", base, out, (left, right, above, below), ties)
+    out = piece(ends_kernel, 2, "ends", base, out, (left, right, paired_row, other_row), ties, [pltpu.VMEM(inward.shape, BF16)] * 2)
     out = piece(functools.partial(sides_kernel, rows[-1]), len(rows[-1]) + 3.5, "sides", base, out, (left, right))
     update = final(nx, ny, (first, second), readers, w_cquery, w_ckey, w_cvalue, w_value, out)
     return update.reshape(features.shape)

time: 44.8 us -> 39.3 us (0.88)
  waiting for transfers between devices: 4.81 us -> 1.23 us
  starting transfers between devices: 14.6 us -> 12.1 us
    ppermute x4 -> x2, waiting for transfers between devices: 4.46 us -> 0.01 us  [shift(): lax.ppermute(array, axis, [(i, (i + step) % count) for i in range(count)])]
    ppermute x4 -> x2, starting transfers between devices: 7.36 us -> 3.45 us  [shift(): lax.ppermute(array, axis, [(i, (i + step) % count) for i in range(count)])]
    ppermute x5 -> x6, starting transfers between devices: 7.21 us -> 8.5 us  [swap(): lax.ppermute(array, axis, [(i, i ^ bits) for i in range(lax.axis_size(axi...]
    ppermute x5 -> x6, waiting for transfers between devices: 0.35 us -> 1.22 us  [swap(): lax.ppermute(array, axis, [(i, i ^ bits) for i in range(lax.axis_size(axi...]
  transfers between devices with their start and end apart: 9 -> 9, of which waited for: 2 -> 3; matrix products, arithmetic and copies ran while one was open for 0% -> 0% of each run, Pallas kernels for 37% -> 43%
where the time goes in v6:
time: 39.3 us; the launch traced here: 38.8 us
  Pallas kernels  25.1 us (64%)
  starting transfers between devices  12.1 us (31%)
  waiting for transfers between devices  1.23 us (3%)
    pallas_call x6, Pallas kernels, piece(): pl.pallas_call(kernel, in_specs=[IN_VMEM] * (4 + len(done) + len(near)) +...  16.5 us
    ppermute x6, starting transfers between devices, swap(): lax.ppermute(array, axis, [(i, i ^ bits) for i in range(lax.axis_size(axi...  8.5 us
    pallas_call x1, Pallas kernels, pool(): pl.pallas_call(functools.partial(pool_kernel, tile, nx, ny), in_specs=[IN...  4.48 us
    pallas_call x1, Pallas kernels, final(): pl.pallas_call(functools.partial(final_kernel, nx, ny, len(blocks)), in_s...  4.07 us
    ppermute x2, starting transfers between devices, shift(): lax.ppermute(array, axis, [(i, (i + step) % count) for i in range(count)])  3.45 us
    ppermute x6, waiting for transfers between devices, swap(): lax.ppermute(array, axis, [(i, i ^ bits) for i in range(lax.axis_size(axi...  1.22 us
  transfers between devices with their start and end apart: 9, of which 3 were waited for; matrix products, arithmetic and copies ran while one was open for 0% of the time, Pallas kernels for 43%

profile of v6, /device:TPU:0, one launch (start us, length us, event | category | flops | bytes accessed | tf_op | source)
XLA Modules:
  0.0 38.8 jit_solution(1892806412166608288)
XLA Ops:
  0.0 4.5 %pool.1 = (bf16[16,1024,128]{2,1,0:T(8,128)(2,1)S(1)}, s32[16,16,64]{2,1,0:T(8,128)S(1)}, f32[256,768]{1,0:T(8,128)S(1)}, bf16[128,128]{1,0:T(8,128)(2,1)S(1)}, ...) custom-call(bf16[16,1024,128]{2,1,0:T(8,128)(2,1)} %bitcast.7, ...), custom_call_target="tpu_custom_call" | custom-call | tf_op jit(solution)/shard_map/pool/pallas_call | solution.py:94
  4.5 0.5 %collective-permute-start.2 = (bf16[1024,128]{1,0:T(8,128)(2,1)S(1)}, bf16[1024,128]{1,0:T(8,128)(2,1)S(1)}, u32[]{:S(2)}, u32[]{:S(2)}) collective-permute-start(bf16[1024,128]{1,0:T(8,128)(2,1)S(1)} %get-tuple-element.19), channel_id=1, source_target_pairs={{0,1},{1,2},{2,3},{3,4},{4,5},{5,6},{6,7},{7,0},{8,9},{9,10},{10,1... | collective-permute-start | bytes 786440 | tf_op jit(solution)/shard_map/ppermute | solution.py:325
  5.0 2.9 %collective-permute-start.3 = (bf16[1024,128]{1,0:T(8,128)(2,1)S(1)}, bf16[1024,128]{1,0:T(8,128)(2,1)S(1)}, u32[]{:S(2)}, u32[]{:S(2)}) collective-permute-start(bf16[1024,128]{1,0:T(8,128)(2,1)S(1)} %get-tuple-element.20), channel_id=1, source_target_pairs={{0,7},{1,0},{2,1},{3,2},{4,3},{5,4},{6,5},{7,6},{8,15},{9,8},{10,9... | collective-permute-start | bytes 786440 | tf_op jit(solution)/shard_map/ppermute | solution.py:325
  7.9 2.3 %collective-permute-start = (bf16[64,128]{1,0:T(8,128)(2,1)S(1)}, bf16[64,128]{1,0:T(8,128)(2,1)S(1)}, u32[]{:S(2)}, u32[]{:S(2)}) collective-permute-start(bf16[64,128]{1,0:T(8,128)(2,1)S(1)} %get-tuple-element.14.rest_0_.refs_0_), channel_id=1, source_target_pairs={{0,8},{8,0},{16,24},{24,16},{1,9},{9,1},{17,25},{25,17},{2,10},{10... | collective-permute-start | bytes 49160 | tf_op jit(solution)/shard_map/ppermute | solution.py:329
  10.2 3.1 %inner_0.1.refs_2_.rest_0_ = bf16[16,1024,256]{2,1,0:T(8,128)(2,1)S(1)} custom-call(bf16[16,1024,128]{2,1,0:T(8,128)(2,1)S(1)} %get-tuple-element.15.fv.fv_ref, s32[16,16,64]{2,1,0:T(8,128)S(1)} %get-tuple-element.16.pv, f32[256,768]{1,0:T(8,128)S(1)} %get-tuple-element.17.mv, bf16[128,128]{1,0:T(8,128)(2,1)S(1)} %get-tuple-element.18.m, ...), custom_call_target="tpu_custom_call" | custom-call | flops 1600000000 | bytes 1000000 | tf_op jit(solution)/shard_map/inner_0/pallas_call | solution.py:259
  13.3 2.7 %collective-permute-start.1 = (bf16[128,128]{1,0:T(8,128)(2,1)S(1)}, bf16[128,128]{1,0:T(8,128)(2,1)S(1)}, u32[]{:S(2)}, u32[]{:S(2)}) collective-permute-start(bf16[128,128]{1,0:T(8,128)(2,1)S(1)} %join.4.rest_1_.refs_0_), channel_id=1, source_target_pairs={{0,16},{8,24},{16,0},{24,8},{1,17},{9,25},{17,1},{25,9},{2,18},{10... | collective-permute-start | bytes 98312 | tf_op jit(solution)/shard_map/ppermute | solution.py:329
  16.0 0.6 %collective-permute-start.7 = (bf16[1152,128]{1,0:T(8,128)(2,1)S(1)}, bf16[1152,128]{1,0:T(8,128)(2,1)S(1)}, u32[]{:S(2)}, u32[]{:S(2)}) collective-permute-start(bf16[1152,128]{1,0:T(8,128)(2,1)S(1)} %get-tuple-element.21.rest_2_), channel_id=1, source_target_pairs={{0,8},{8,0},{16,24},{24,16},{1,9},{9,1},{17,25},{25,17},{2,10},{10... | collective-permute-start | bytes 884744 | tf_op jit(solution)/shard_map/ppermute | solution.py:329
  16.7 0.1 collective-permute-start.8
  16.8 1.6 %inner_1.1.refs_2_.rest_0_ = bf16[16,1024,256]{2,1,0:T(8,128)(2,1)S(1)} custom-call(bf16[16,1024,128]{2,1,0:T(8,128)(2,1)S(1)} %get-tuple-element.15.fv.fv_ref, s32[16,16,64]{2,1,0:T(8,128)S(1)} %get-tuple-element.16.pv, f32[256,768]{1,0:T(8,128)S(1)} %get-tuple-element.17.mv, ...), custom_call_target="tpu_custom_call", output_to_operand_aliasing={{}: (4, {})} | custom-call | flops 800000000 | bytes 1000000 | tf_op jit(solution)/shard_map/inner_1/pallas_call | solution.py:259
  18.4 0.2 collective-permute-done.1.refs_1_
  18.7 1.3 %collective-permute-start.4 = (bf16[256,128]{1,0:T(8,128)(2,1)S(1)}, bf16[256,128]{1,0:T(8,128)(2,1)S(1)}, u32[]{:S(2)}, u32[]{:S(2)}) collective-permute-start(bf16[256,128]{1,0:T(8,128)(2,1)S(1)} %join.5.rest_1_.refs_0_), channel_id=1, source_target_pairs={{0,2},{1,3},{2,0},{3,1},{4,6},{5,7},{6,4},{7,5},{8,10},{9,11},{10,... | collective-permute-start | bytes 196616 | tf_op jit(solution)/shard_map/ppermute | solution.py:329
  20.0 2.3 %inner_2.1.refs_2_.rest_0_ = bf16[16,1024,256]{2,1,0:T(8,128)(2,1)S(1)} custom-call(bf16[16,1024,128]{2,1,0:T(8,128)(2,1)S(1)} %get-tuple-element.15.fv.fv_ref, s32[16,16,64]{2,1,0:T(8,128)S(1)} %get-tuple-element.16.pv, f32[256,768]{1,0:T(8,128)S(1)} %get-tuple-element.17.mv, ...), custom_call_target="tpu_custom_call", output_to_operand_aliasing={{}: (4, {})} | custom-call | flops 1200000000 | bytes 1000000 | tf_op jit(solution)/shard_map/inner_2/pallas_call | solution.py:259
  22.3 0.6 %collective-permute-done.4.refs_1_ = bf16[256,128]{1,0:T(8,128)(2,1)S(1)} collective-permute-done((bf16[256,128]{1,0:T(8,128)(2,1)S(1)}, bf16[256,128]{1,0:T(8,128)(2,1)S(1)}, u32[]{:S(2)}, u32[]{:S(2)}) %collective-permute-start.4) | collective-permute-done | bytes 65568 | tf_op jit(solution)/shard_map/ppermute | solution.py:329
  22.9 1.6 %collective-permute-start.5 = (bf16[512,128]{1,0:T(8,128)(2,1)S(1)}, bf16[512,128]{1,0:T(8,128)(2,1)S(1)}, u32[]{:S(2)}, u32[]{:S(2)}) collective-permute-start(bf16[512,128]{1,0:T(8,128)(2,1)S(1)} %join.6.rest_1_.refs_0_), channel_id=1, source_target_pairs={{0,4},{1,5},{2,6},{3,7},{4,0},{5,1},{6,2},{7,3},{8,12},{9,13},{10,... | collective-permute-start | bytes 393224 | tf_op jit(solution)/shard_map/ppermute | solution.py:329
  24.5 3.1 %inner_3.1.refs_2_.out_in = bf16[16,1024,256]{2,1,0:T(8,128)(2,1)S(1)} custom-call(bf16[16,1024,128]{2,1,0:T(8,128)(2,1)S(1)} %get-tuple-element.15.fv.fv_ref, s32[16,16,64]{2,1,0:T(8,128)S(1)} %get-tuple-element.16.pv, f32[256,768]{1,0:T(8,128)S(1)} %get-tuple-element.17.mv, ...), custom_call_target="tpu_custom_call", output_to_operand_aliasing={{}: (4, {})} | custom-call | flops 1600000000 | bytes 1000000 | tf_op jit(solution)/shard_map/inner_3/pallas_call | solution.py:259
  27.6 0.3 collective-permute-done.5.refs_1_
  28.0 0.1 collective-permute-start.6
  28.1 2.3 %ends.1.out_in = bf16[16,1024,256]{2,1,0:T(8,128)(2,1)S(1)} custom-call(bf16[16,1024,128]{2,1,0:T(8,128)(2,1)S(1)} %get-tuple-element.15.fv.fv_ref, s32[16,16,64]{2,1,0:T(8,128)S(1)} %get-tuple-element.16.pv, f32[256,768]{1,0:T(8,128)S(1)} %get-tuple-element.17.mv, bf16[128,128]{1,0:T(8,128)(2,1)S(1)} %get-tuple-element.18.m, ...), custom_call_target="tpu_custom_call", output_to_operand_aliasing={{}: (4, {})} | custom-call | flops 800000000 | bytes 1000000 | tf_op jit(solution)/shard_map/ends/pallas_call | solution.py:259
  30.4 0.0 copy-start
  30.4 0.0 copy-start.1
  30.4 0.0 copy-start.2
  30.4 0.0 copy-start.4
  30.4 4.1 %sides.1.refs_7_ = bf16[16,1024,256]{2,1,0:T(8,128)(2,1)S(1)} custom-call(bf16[16,1024,128]{2,1,0:T(8,128)(2,1)S(1)} %get-tuple-element.15.fv.fv_ref, s32[16,16,64]{2,1,0:T(8,128)S(1)} %get-tuple-element.16.pv, f32[256,768]{1,0:T(8,128)S(1)} %get-tuple-element.17.mv, bf16[128,128]{1,0:T(8,128)(2,1)S(1)} %get-tuple-element.18.m, ...), custom_call_target="tpu_custom_call", output_to_operand_aliasing={{}: (4, {})} | custom-call | flops 1800000000 | bytes 1000000 | tf_op jit(solution)/shard_map/sides/pallas_call | solution.py:259
  34.6 4.1 %final.1 = bf16[16,1024,128]{2,1,0:T(8,128)(2,1)} custom-call(bf16[1024,128]{1,0:T(8,128)(2,1)S(1)} %join.7.rest_0_.refs_0_, bf16[1024,128]{1,0:T(8,128)(2,1)S(1)} %collective-permute-done.6.refs_1_, s32[8,32]{1,0:T(8,128)S(1)} %bitcast.6, bf16[128,128]{1,0:T(8,128)(2,1)S(1)} %copy-done, bf16[128,128]{1,0:T(8,128)(2,1)S(1)} %copy-done.1, ...), custom_call_target="tpu_custom_call" | custom-call | tf_op jit(solution)/shard_map/final/pallas_call | solution.py:308
  (17 shorter events, 0.1 us)
Async XLA Ops:
  4.5 11.5 %collective-permute-start.2 = (bf16[1024,128]{1,0:T(8,128)(2,1)S(1)}, bf16[1024,128]{1,0:T(8,128)(2,1)S(1)}, u32[]{:S(2)}, u32[]{:S(2)}) collective-permute-start(bf16[1024,128]{1,0:T(8,128)(2,1)S(1)} %get-tuple-element.19), channel_id=1, source_target_pairs={{0,1},{1,2},{2,3},{3,4},{4,5},{5,6},{6,7},{7,0},{8,9},{9,10},{10,1... | collective-permute-start | bytes 786440 | tf_op jit(solution)/shard_map/ppermute | solution.py:325
  5.0 11.0 %collective-permute-start.3 = (bf16[1024,128]{1,0:T(8,128)(2,1)S(1)}, bf16[1024,128]{1,0:T(8,128)(2,1)S(1)}, u32[]{:S(2)}, u32[]{:S(2)}) collective-permute-start(bf16[1024,128]{1,0:T(8,128)(2,1)S(1)} %get-tuple-element.20), channel_id=1, source_target_pairs={{0,7},{1,0},{2,1},{3,2},{4,3},{5,4},{6,5},{7,6},{8,15},{9,8},{10,9... | collective-permute-start | bytes 786440 | tf_op jit(solution)/shard_map/ppermute | solution.py:325
  7.9 5.4 %collective-permute-start = (bf16[64,128]{1,0:T(8,128)(2,1)S(1)}, bf16[64,128]{1,0:T(8,128)(2,1)S(1)}, u32[]{:S(2)}, u32[]{:S(2)}) collective-permute-start(bf16[64,128]{1,0:T(8,128)(2,1)S(1)} %get-tuple-element.14.rest_0_.refs_0_), channel_id=1, source_target_pairs={{0,8},{8,0},{16,24},{24,16},{1,9},{9,1},{17,25},{25,17},{2,10},{10... | collective-permute-start | bytes 49160 | tf_op jit(solution)/shard_map/ppermute | solution.py:329
  13.3 5.3 %collective-permute-start.1 = (bf16[128,128]{1,0:T(8,128)(2,1)S(1)}, bf16[128,128]{1,0:T(8,128)(2,1)S(1)}, u32[]{:S(2)}, u32[]{:S(2)}) collective-permute-start(bf16[128,128]{1,0:T(8,128)(2,1)S(1)} %join.4.rest_1_.refs_0_), channel_id=1, source_target_pairs={{0,16},{8,24},{16,0},{24,8},{1,17},{9,25},{17,1},{25,9},{2,18},{10... | collective-permute-start | bytes 98312 | tf_op jit(solution)/shard_map/ppermute | solution.py:329
  16.0 12.0 %collective-permute-start.7 = (bf16[1152,128]{1,0:T(8,128)(2,1)S(1)}, bf16[1152,128]{1,0:T(8,128)(2,1)S(1)}, u32[]{:S(2)}, u32[]{:S(2)}) collective-permute-start(bf16[1152,128]{1,0:T(8,128)(2,1)S(1)} %get-tuple-element.21.rest_2_), channel_id=1, source_target_pairs={{0,8},{8,0},{16,24},{24,16},{1,9},{9,1},{17,25},{25,17},{2,10},{10... | collective-permute-start | bytes 884744 | tf_op jit(solution)/shard_map/ppermute | solution.py:329
  16.7 11.4 %collective-permute-start.8 = (bf16[1152,128]{1,0:T(8,128)(2,1)S(1)}, bf16[1152,128]{1,0:T(8,128)(2,1)S(1)}, u32[]{:S(2)}, u32[]{:S(2)}) collective-permute-start(bf16[1152,128]{1,0:T(8,128)(2,1)S(1)} %get-tuple-element.22), channel_id=1, source_target_pairs={{0,1},{1,0},{2,3},{3,2},{4,5},{5,4},{6,7},{7,6},{8,16},{9,17},{10,... | collective-permute-start | bytes 884744 | tf_op jit(solution)/shard_map/ppermute | solution.py:384
  18.7 4.3 %collective-permute-start.4 = (bf16[256,128]{1,0:T(8,128)(2,1)S(1)}, bf16[256,128]{1,0:T(8,128)(2,1)S(1)}, u32[]{:S(2)}, u32[]{:S(2)}) collective-permute-start(bf16[256,128]{1,0:T(8,128)(2,1)S(1)} %join.5.rest_1_.refs_0_), channel_id=1, source_target_pairs={{0,2},{1,3},{2,0},{3,1},{4,6},{5,7},{6,4},{7,5},{8,10},{9,11},{10,... | collective-permute-start | bytes 196616 | tf_op jit(solution)/shard_map/ppermute | solution.py:329
  22.9 5.0 %collective-permute-start.5 = (bf16[512,128]{1,0:T(8,128)(2,1)S(1)}, bf16[512,128]{1,0:T(8,128)(2,1)S(1)}, u32[]{:S(2)}, u32[]{:S(2)}) collective-permute-start(bf16[512,128]{1,0:T(8,128)(2,1)S(1)} %join.6.rest_1_.refs_0_), channel_id=1, source_target_pairs={{0,4},{1,5},{2,6},{3,7},{4,0},{5,1},{6,2},{7,3},{8,12},{9,13},{10,... | collective-permute-start | bytes 393224 | tf_op jit(solution)/shard_map/ppermute | solution.py:329
  28.0 6.5 %collective-permute-start.6 = (bf16[1024,128]{1,0:T(8,128)(2,1)S(1)}, bf16[1024,128]{1,0:T(8,128)(2,1)S(1)}, u32[]{:S(2)}, u32[]{:S(2)}) collective-permute-start(bf16[1024,128]{1,0:T(8,128)(2,1)S(1)} %join.7.rest_0_.refs_0_), channel_id=1, source_target_pairs={{0,1},{1,0},{2,3},{3,2},{4,5},{5,4},{6,7},{7,6},{8,9},{9,8},{10,11... | collective-permute-start | bytes 786440 | tf_op jit(solution)/shard_map/ppermute | solution.py:329
  30.4 4.1 %copy-start = (bf16[128,128]{1,0:T(8,128)(2,1)S(1)}, bf16[128,128]{1,0:T(8,128)(2,1)}, u32[]{:S(2)}) copy-start(bf16[128,128]{1,0:T(8,128)(2,1)} %refs_3_.1) | copy-start | bytes 98308
  30.4 4.1 %copy-start.1 = (bf16[128,128]{1,0:T(8,128)(2,1)S(1)}, bf16[128,128]{1,0:T(8,128)(2,1)}, u32[]{:S(2)}) copy-start(bf16[128,128]{1,0:T(8,128)(2,1)} %refs_4_.1) | copy-start | bytes 98308
  30.4 4.1 %copy-start.2 = (bf16[128,128]{1,0:T(8,128)(2,1)S(1)}, bf16[128,128]{1,0:T(8,128)(2,1)}, u32[]{:S(2)}) copy-start(bf16[128,128]{1,0:T(8,128)(2,1)} %refs_5_.1) | copy-start | bytes 98308
  30.4 4.1 %copy-start.3 = (bf16[128,128]{1,0:T(8,128)(2,1)S(1)}, bf16[128,128]{1,0:T(8,128)(2,1)}, u32[]{:S(2)}) copy-start(bf16[128,128]{1,0:T(8,128)(2,1)} %refs_6_.1) | copy-start | bytes 98308
  30.4 4.1 %copy-start.4 = (s32[32,8]{0,1:T(8,128)S(1)}, s32[32,8]{0,1:T(8,128)}, u32[]{:S(2)}) copy-start(s32[32,8]{0,1:T(8,128)} %param.13) | copy-start | bytes 3076

commit v7 on v6

--- a/solution.py
+++ b/solution.py
@@ -42,7 +42,7 @@
     return jnp.concatenate([ids[:half], ids[half:]], axis=1)
 
 
-def pool_kernel(tile, nx, ny, f_ref, pm_ref, tm_ref, wq_ref, wk_ref, fv_ref, pv_ref, mv_ref, m_ref, pooled_ref, left_ref, right_ref, tv, wq, wk, sems):
+def pool_kernel(tile, nx, ny, f_ref, pm_ref, tm_ref, wq_ref, wk_ref, fv_ref, pv_ref, mv_ref, m_ref, pooled_ref, inward_ref, outward_ref, tv, wq, wk, sems):
     rows, span, chan = fv_ref.shape
     cy = span // tile
     small = [(tm_ref, tv), (wq_ref, wq), (wk_ref, wk), (pm_ref, pv_ref)]
@@ -82,8 +82,9 @@
         )
         beads_in[r].wait()
         total += dot(onehot, jnp.concatenate([fv_ref[r, tile * c : tile * (c + 1)] for c in order], axis=0))
-        left_ref[tile * r : tile * (r + 1)] = fv_ref[r, :tile]
-        right_ref[tile * r : tile * (r + 1)] = fv_ref[r, span - tile :]
+        for ref, low in ((inward_ref, my % 2), (outward_ref, 1 - my % 2)):
+            column = pl.ds(pl.multiple_of((1 - low) * (span - tile), tile), tile)
+            ref[tile * r : tile * (r + 1)] = fv_ref[r, column]
     pooled_ref[...] = (total * math.sqrt(S / (rows * span))).astype(BF16)
 
 
@@ -320,11 +321,6 @@
     )(*blocks, readers.T, w_cquery, w_ckey, w_cvalue, w_value, out)
 
 
-def shift(array, axis, step):
-    count = lax.axis_size(axis)
-    return lax.ppermute(array, axis, [(i, (i + step) % count) for i in range(count)])
-
-
 def swap(array, axis, bits):
     return lax.ppermute(array, axis, [(i, i ^ bits) for i in range(lax.axis_size(axis))])
 
@@ -349,11 +345,22 @@
     )(*parts, *ties)
 
 
-def edge_rows_kernel(tile, fv_ref, left_ref, right_ref, *rest):
-    to_refs = rest[-2:]
+def edge_rows_kernel(tile, fv_ref, paired_ref, other_ref, *rest):
+    left_ref, right_ref, inward_ref, outward_ref = rest[-4:]
     rows, span, _ = fv_ref.shape
+
+    @pl.when(lax.axis_index("gy") % 2 == 1)
+    def _():
+        left_ref[...] = paired_ref[...]
+        right_ref[...] = other_ref[...]
+
+    @pl.when(lax.axis_index("gy") % 2 == 0)
+    def _():
+        left_ref[...] = other_ref[...]
+        right_ref[...] = paired_ref[...]
+
     odd = lax.axis_index("gx") % 2
-    for ref, low in ((to_refs[0], odd), (to_refs[1], 1 - odd)):
+    for ref, low in ((inward_ref, odd), (outward_ref, 1 - odd)):
         r = (1 - low) * (rows - 1)
         corner = pl.ds(pl.multiple_of(tile * r, tile), tile)
         ref[:tile] = left_ref[corner]
@@ -361,25 +368,30 @@
         ref[tile + span :] = right_ref[corner]
 
 
-def edge_rows(tile, fv, left, right, ties):
-    _, span, chan = fv.shape
+def edge_rows(tile, fv, paired_column, other_column, ties):
+    rows, span, chan = fv.shape
+    column = pltpu.VMEM((rows * tile, chan), BF16)
     edge = pltpu.VMEM((span + 2 * tile, chan), BF16)
     return pl.pallas_call(
         functools.partial(edge_rows_kernel, tile),
         in_specs=[IN_VMEM] * 3 + [pl.BlockSpec(memory_space=pl.ANY)] * len(ties),
-        out_specs=[IN_VMEM] * 2,
-        out_shape=[edge, edge],
+        out_specs=[IN_VMEM] * 4,
+        out_shape=[column, column, edge, edge],
         compiler_params=params(4),
         name="edge_rows",
-    )(fv, left, right, *ties)
-
-
-def swap_across(array, nx, ny):
+    )(fv, paired_column, other_column, *ties)
+
+
+def swap_across(array, axis, nx, ny):
     moves = []
     for x in range(nx):
         for y in range(ny):
-            near = x + 1 if x % 2 else x - 1
-            there = near * ny + y if 0 <= near < nx else x * ny + (y ^ 1)
+            if axis == "gx":
+                near = x + 1 if x % 2 else x - 1
+                there = near * ny + y if 0 <= near < nx else x * ny + (y ^ 1)
+            else:
+                near = y + 1 if y % 2 else y - 1
+                there = x * ny + near if 0 <= near < ny else (x ^ 1) * ny + y
             moves.append((x * ny + y, there))
     return lax.ppermute(array, ("gx", "gy"), moves)
 
@@ -387,21 +399,21 @@
 def per_device(features, tile_mask, pool_map, readers, w_query, w_key, w_value, w_cquery, w_ckey, w_cvalue):
     cx, cy, tile, chan = features.shape
     nx, ny = lax.axis_size("gx"), lax.axis_size("gy")
-    *base, pooled, left_edge, right_edge = pool(nx, ny, features, tile_mask, pool_map, w_query, w_key)
+    *base, pooled, inward, outward = pool(nx, ny, features, tile_mask, pool_map, w_query, w_key)
     fv = base[0]
     cuts = [1] + [1 + (cx - 2) * part // 14 for part in CUTS] + [cx - 1]
     rows = [range(lo, hi) for lo, hi in zip(cuts, cuts[1:])]
     steps = [("gx", 1 << b) for b in range(nx.bit_length() - 1)]
     steps += [("gy", 1 << b) for b in range(1, ny.bit_length() - 1)] + [("gy", 1)]
-    left = shift(right_edge, "gy", 1)
-    right = shift(left_edge, "gy", -1)
+    paired_column = swap(inward, "gy", 1)
+    other_column = swap_across(outward, "gy", nx, ny)
     out, first, ties = None, pooled, (pooled,)
     for step, (axis, bit) in enumerate(steps):
         second = swap(first, axis, bit)
-        if step == 1:
-            inward, outward = edge_rows(tile, fv, left, right, (out,))
+        if step == 2:
+            left, right, inward, outward = edge_rows(tile, fv, paired_column, other_column, (out, first))
             paired_row = swap(inward, "gx", 1)
-            other_row = swap_across(outward, nx, ny)
+            other_row = swap_across(outward, "gx", nx, ny)
             ties += (inward,)
         if step == len(steps) - 1:
             break
@@ -410,8 +422,8 @@
             out = piece(kernel, len(rows[step]), f"inner_{step}", base, out, (), ties)
         first = join((first, second), (out,))
         ties = (first,)
-    out = piece(ends_kernel, 2, "ends", base, out, (left, right, paired_row, other_row), ties, [pltpu.VMEM(inward.shape, BF16)] * 2)
-    out = piece(functools.partial(sides_kernel, rows[-1]), len(rows[-1]) + 3.5, "sides", base, out, (left, right))
+    out = piece(functools.partial(sides_kernel, rows[-1]), len(rows[-1]) + 3.5, "sides", base, out, (left, right), ties)
+    out = piece(ends_kernel, 2, "ends", base, out, (left, right, paired_row, other_row), (), [pltpu.VMEM(inward.shape, BF16)] * 2)
     update = final(nx, ny, (first, second), readers, w_cquery, w_ckey, w_cvalue, w_value, out)
     return update.reshape(features.shape)
 

time: 39.3 us -> 38.2 us (0.972)
  starting transfers between devices: 12.1 us -> 9.75 us
  waiting for transfers between devices: 1.23 us -> 2.36 us
    ppermute x2 -> x0, starting transfers between devices: 3.45 us -> none  [shift(): lax.ppermute(array, axis, [(i, (i + step) % count) for i in range(count)])]
    ppermute x1 -> x2, starting transfers between devices: 0.15 us -> 2.65 us  [swap_across(): return lax.ppermute(array, ('gx', 'gy'), moves)]
    ppermute x6 -> x7, starting transfers between devices: 8.5 us -> 7.1 us  [swap(): lax.ppermute(array, axis, [(i, i ^ bits) for i in range(lax.axis_size(axi...]
    ppermute x6 -> x7, waiting for transfers between devices: 1.22 us -> 2.36 us  [swap(): lax.ppermute(array, axis, [(i, i ^ bits) for i in range(lax.axis_size(axi...]
  transfers between devices with their start and end apart: 9 -> 9, of which waited for: 3 -> 3; matrix products, arithmetic and copies ran while one was open for 0% -> 0% of each run, Pallas kernels for 43% -> 44%
where the time goes in v7:
time: 38.2 us; the launch traced here: 37.9 us
  Pallas kernels  25.4 us (66%)
  starting transfers between devices  9.75 us (26%)
  waiting for transfers between devices  2.36 us (6%)
    pallas_call x6, Pallas kernels, piece(): pl.pallas_call(kernel, in_specs=[IN_VMEM] * (4 + len(done) + len(near)) +...  16.5 us
    ppermute x7, starting transfers between devices, swap(): lax.ppermute(array, axis, [(i, i ^ bits) for i in range(lax.axis_size(axi...  7.1 us
    pallas_call x1, Pallas kernels, pool(): pl.pallas_call(functools.partial(pool_kernel, tile, nx, ny), in_specs=[IN...  4.46 us
    pallas_call x1, Pallas kernels, final(): pl.pallas_call(functools.partial(final_kernel, nx, ny, len(blocks)), in_s...  4.08 us
    ppermute x2, starting transfers between devices, swap_across(): return lax.ppermute(array, ('gx', 'gy'), moves)  2.65 us
    ppermute x7, waiting for transfers between devices, swap(): lax.ppermute(array, axis, [(i, i ^ bits) for i in range(lax.axis_size(axi...  2.36 us
  transfers between devices with their start and end apart: 9, of which 3 were waited for; matrix products, arithmetic and copies ran while one was open for 0% of the time, Pallas kernels for 44%

profile of v7, /device:TPU:0, one launch (start us, length us, event | category | flops | bytes accessed | tf_op | source)
XLA Modules:
  0.0 37.9 jit_solution(16125438777573702988)
XLA Ops:
  0.0 4.5 %pool.1 = (bf16[16,1024,128]{2,1,0:T(8,128)(2,1)S(1)}, s32[16,16,64]{2,1,0:T(8,128)S(1)}, f32[256,768]{1,0:T(8,128)S(1)}, bf16[128,128]{1,0:T(8,128)(2,1)S(1)}, ...) custom-call(bf16[16,1024,128]{2,1,0:T(8,128)(2,1)} %bitcast.7, ...), custom_call_target="tpu_custom_call" | custom-call | tf_op jit(solution)/shard_map/pool/pallas_call | solution.py:95
  4.5 0.5 %collective-permute-start.3 = (bf16[1024,128]{1,0:T(8,128)(2,1)S(1)}, bf16[1024,128]{1,0:T(8,128)(2,1)S(1)}, u32[]{:S(2)}, u32[]{:S(2)}) collective-permute-start(bf16[1024,128]{1,0:T(8,128)(2,1)S(1)} %get-tuple-element.21), channel_id=1, source_target_pairs={{0,1},{1,0},{2,3},{3,2},{4,5},{5,4},{6,7},{7,6},{8,9},{9,8},{10,11... | collective-permute-start | bytes 786440 | tf_op jit(solution)/shard_map/ppermute | solution.py:325
  5.0 2.6 %collective-permute-start.4 = (bf16[1024,128]{1,0:T(8,128)(2,1)S(1)}, bf16[1024,128]{1,0:T(8,128)(2,1)S(1)}, u32[]{:S(2)}, u32[]{:S(2)}) collective-permute-start(bf16[1024,128]{1,0:T(8,128)(2,1)S(1)} %get-tuple-element.22), channel_id=1, source_target_pairs={{0,8},{1,2},{2,1},{3,4},{4,3},{5,6},{6,5},{7,15},{8,0},{9,10},{10,... | collective-permute-start | bytes 786440 | tf_op jit(solution)/shard_map/ppermute | solution.py:396
  7.6 0.1 collective-permute-start
  7.7 3.1 %inner_0.1.refs_2_.rest_0_ = bf16[16,1024,256]{2,1,0:T(8,128)(2,1)S(1)} custom-call(bf16[16,1024,128]{2,1,0:T(8,128)(2,1)S(1)} %get-tuple-element.17.fv.fv_ref, s32[16,16,64]{2,1,0:T(8,128)S(1)} %get-tuple-element.18.pv, f32[256,768]{1,0:T(8,128)S(1)} %get-tuple-element.19.mv, bf16[128,128]{1,0:T(8,128)(2,1)S(1)} %get-tuple-element.20.m, ...), custom_call_target="tpu_custom_call" | custom-call | flops 1600000000 | bytes 1000000 | tf_op jit(solution)/shard_map/inner_0/pallas_call | solution.py:260
  10.8 1.5 %collective-permute-done.refs_1_ = bf16[64,128]{1,0:T(8,128)(2,1)S(1)} collective-permute-done((bf16[64,128]{1,0:T(8,128)(2,1)S(1)}, bf16[64,128]{1,0:T(8,128)(2,1)S(1)}, u32[]{:S(2)}, u32[]{:S(2)}) %collective-permute-start) | collective-permute-done | bytes 16416 | tf_op jit(solution)/shard_map/ppermute | solution.py:325
  12.3 3.0 %collective-permute-start.1 = (bf16[128,128]{1,0:T(8,128)(2,1)S(1)}, bf16[128,128]{1,0:T(8,128)(2,1)S(1)}, u32[]{:S(2)}, u32[]{:S(2)}) collective-permute-start(bf16[128,128]{1,0:T(8,128)(2,1)S(1)} %join.4.rest_1_.refs_0_), channel_id=1, source_target_pairs={{0,16},{8,24},{16,0},{24,8},{1,17},{9,25},{17,1},{25,9},{2,18},{10... | collective-permute-start | bytes 98312 | tf_op jit(solution)/shard_map/ppermute | solution.py:325
  15.4 1.6 %inner_1.1.refs_2_.rest_0_ = bf16[16,1024,256]{2,1,0:T(8,128)(2,1)S(1)} custom-call(bf16[16,1024,128]{2,1,0:T(8,128)(2,1)S(1)} %get-tuple-element.17.fv.fv_ref, s32[16,16,64]{2,1,0:T(8,128)S(1)} %get-tuple-element.18.pv, f32[256,768]{1,0:T(8,128)S(1)} %get-tuple-element.19.mv, ...), custom_call_target="tpu_custom_call", output_to_operand_aliasing={{}: (4, {})} | custom-call | flops 800000000 | bytes 1000000 | tf_op jit(solution)/shard_map/inner_1/pallas_call | solution.py:260
  17.0 0.3 collective-permute-done.1.refs_1_
  17.3 1.2 %collective-permute-start.2 = (bf16[256,128]{1,0:T(8,128)(2,1)S(1)}, bf16[256,128]{1,0:T(8,128)(2,1)S(1)}, u32[]{:S(2)}, u32[]{:S(2)}) collective-permute-start(bf16[256,128]{1,0:T(8,128)(2,1)S(1)} %join.5.rest_1_.refs_0_), channel_id=1, source_target_pairs={{0,2},{1,3},{2,0},{3,1},{4,6},{5,7},{6,4},{7,5},{8,10},{9,11},{10,... | collective-permute-start | bytes 196616 | tf_op jit(solution)/shard_map/ppermute | solution.py:325
  18.4 0.3 edge_rows.1
  18.7 0.9 %collective-permute-start.7 = (bf16[1152,128]{1,0:T(8,128)(2,1)S(1)}, bf16[1152,128]{1,0:T(8,128)(2,1)S(1)}, u32[]{:S(2)}, u32[]{:S(2)}) collective-permute-start(bf16[1152,128]{1,0:T(8,128)(2,1)S(1)} %get-tuple-element.23.rest_2_), channel_id=1, source_target_pairs={{0,8},{8,0},{16,24},{24,16},{1,9},{9,1},{17,25},{25,17},{2,10},{10... | collective-permute-start | bytes 884744 | tf_op jit(solution)/shard_map/ppermute | solution.py:325
  19.6 2.3 %inner_2.1.refs_2_.rest_0_ = bf16[16,1024,256]{2,1,0:T(8,128)(2,1)S(1)} custom-call(bf16[16,1024,128]{2,1,0:T(8,128)(2,1)S(1)} %get-tuple-element.17.fv.fv_ref, s32[16,16,64]{2,1,0:T(8,128)S(1)} %get-tuple-element.18.pv, f32[256,768]{1,0:T(8,128)S(1)} %get-tuple-element.19.mv, ...), custom_call_target="tpu_custom_call", output_to_operand_aliasing={{}: (4, {})} | custom-call | flops 1200000000 | bytes 1000000 | tf_op jit(solution)/shard_map/inner_2/pallas_call | solution.py:260
  21.9 1.4 %collective-permute-start.5 = (bf16[512,128]{1,0:T(8,128)(2,1)S(1)}, bf16[512,128]{1,0:T(8,128)(2,1)S(1)}, u32[]{:S(2)}, u32[]{:S(2)}) collective-permute-start(bf16[512,128]{1,0:T(8,128)(2,1)S(1)} %join.6.rest_1_.refs_0_), channel_id=1, source_target_pairs={{0,4},{1,5},{2,6},{3,7},{4,0},{5,1},{6,2},{7,3},{8,12},{9,13},{10,... | collective-permute-start | bytes 393224 | tf_op jit(solution)/shard_map/ppermute | solution.py:325
  23.3 3.1 %inner_3.1.refs_2_.out_in = bf16[16,1024,256]{2,1,0:T(8,128)(2,1)S(1)} custom-call(bf16[16,1024,128]{2,1,0:T(8,128)(2,1)S(1)} %get-tuple-element.17.fv.fv_ref, s32[16,16,64]{2,1,0:T(8,128)S(1)} %get-tuple-element.18.pv, f32[256,768]{1,0:T(8,128)S(1)} %get-tuple-element.19.mv, ...), custom_call_target="tpu_custom_call", output_to_operand_aliasing={{}: (4, {})} | custom-call | flops 1600000000 | bytes 1000000 | tf_op jit(solution)/shard_map/inner_3/pallas_call | solution.py:260
  26.4 0.5 %collective-permute-done.5.refs_1_ = bf16[512,128]{1,0:T(8,128)(2,1)S(1)} collective-permute-done((bf16[512,128]{1,0:T(8,128)(2,1)S(1)}, bf16[512,128]{1,0:T(8,128)(2,1)S(1)}, u32[]{:S(2)}, u32[]{:S(2)}) %collective-permute-start.5) | collective-permute-done | bytes 131104 | tf_op jit(solution)/shard_map/ppermute | solution.py:325
  27.0 0.1 collective-permute-start.6
  27.1 4.1 %sides.1.out_in = bf16[16,1024,256]{2,1,0:T(8,128)(2,1)S(1)} custom-call(bf16[16,1024,128]{2,1,0:T(8,128)(2,1)S(1)} %get-tuple-element.17.fv.fv_ref, s32[16,16,64]{2,1,0:T(8,128)S(1)} %get-tuple-element.18.pv, f32[256,768]{1,0:T(8,128)S(1)} %get-tuple-element.19.mv, bf16[128,128]{1,0:T(8,128)(2,1)S(1)} %get-tuple-element.20.m, ...), custom_call_target="tpu_custom_call", output_to_operand_aliasing={{}: (4, {})} | custom-call | flops 1800000000 | bytes 1000000 | tf_op jit(solution)/shard_map/sides/pallas_call | solution.py:260
  31.2 0.0 copy-start
  31.2 0.0 copy-start.1
  31.2 0.0 copy-start.3
  31.2 0.0 copy-start.4
  31.2 2.3 %ends.1.refs_7_ = bf16[16,1024,256]{2,1,0:T(8,128)(2,1)S(1)} custom-call(bf16[16,1024,128]{2,1,0:T(8,128)(2,1)S(1)} %get-tuple-element.17.fv.fv_ref, s32[16,16,64]{2,1,0:T(8,128)S(1)} %get-tuple-element.18.pv, f32[256,768]{1,0:T(8,128)S(1)} %get-tuple-element.19.mv, bf16[128,128]{1,0:T(8,128)(2,1)S(1)} %get-tuple-element.20.m, ...), custom_call_target="tpu_custom_call", output_to_operand_aliasing={{}: (4, {})} | custom-call | flops 800000000 | bytes 1000000 | tf_op jit(solution)/shard_map/ends/pallas_call | solution.py:260
  33.6 4.1 %final.1 = bf16[16,1024,128]{2,1,0:T(8,128)(2,1)} custom-call(bf16[1024,128]{1,0:T(8,128)(2,1)S(1)} %join.7.rest_0_.refs_0_, bf16[1024,128]{1,0:T(8,128)(2,1)S(1)} %collective-permute-done.6.refs_1_, s32[8,32]{1,0:T(8,128)S(1)} %bitcast.6, bf16[128,128]{1,0:T(8,128)(2,1)S(1)} %copy-done, bf16[128,128]{1,0:T(8,128)(2,1)S(1)} %copy-done.1, ...), custom_call_target="tpu_custom_call" | custom-call | tf_op jit(solution)/shard_map/final/pallas_call | solution.py:309
  (17 shorter events, 0.1 us)
Async XLA Ops:
  4.5 14.0 %collective-permute-start.3 = (bf16[1024,128]{1,0:T(8,128)(2,1)S(1)}, bf16[1024,128]{1,0:T(8,128)(2,1)S(1)}, u32[]{:S(2)}, u32[]{:S(2)}) collective-permute-start(bf16[1024,128]{1,0:T(8,128)(2,1)S(1)} %get-tuple-element.21), channel_id=1, source_target_pairs={{0,1},{1,0},{2,3},{3,2},{4,5},{5,4},{6,7},{7,6},{8,9},{9,8},{10,11... | collective-permute-start | bytes 786440 | tf_op jit(solution)/shard_map/ppermute | solution.py:325
  5.0 13.5 %collective-permute-start.4 = (bf16[1024,128]{1,0:T(8,128)(2,1)S(1)}, bf16[1024,128]{1,0:T(8,128)(2,1)S(1)}, u32[]{:S(2)}, u32[]{:S(2)}) collective-permute-start(bf16[1024,128]{1,0:T(8,128)(2,1)S(1)} %get-tuple-element.22), channel_id=1, source_target_pairs={{0,8},{1,2},{2,1},{3,4},{4,3},{5,6},{6,5},{7,15},{8,0},{9,10},{10,... | collective-permute-start | bytes 786440 | tf_op jit(solution)/shard_map/ppermute | solution.py:396
  7.6 4.7 %collective-permute-start = (bf16[64,128]{1,0:T(8,128)(2,1)S(1)}, bf16[64,128]{1,0:T(8,128)(2,1)S(1)}, u32[]{:S(2)}, u32[]{:S(2)}) collective-permute-start(bf16[64,128]{1,0:T(8,128)(2,1)S(1)} %get-tuple-element.16.rest_0_.refs_0_), channel_id=1, source_target_pairs={{0,8},{8,0},{16,24},{24,16},{1,9},{9,1},{17,25},{25,17},{2,10},{10... | collective-permute-start | bytes 49160 | tf_op jit(solution)/shard_map/ppermute | solution.py:325
  12.3 4.9 %collective-permute-start.1 = (bf16[128,128]{1,0:T(8,128)(2,1)S(1)}, bf16[128,128]{1,0:T(8,128)(2,1)S(1)}, u32[]{:S(2)}, u32[]{:S(2)}) collective-permute-start(bf16[128,128]{1,0:T(8,128)(2,1)S(1)} %join.4.rest_1_.refs_0_), channel_id=1, source_target_pairs={{0,16},{8,24},{16,0},{24,8},{1,17},{9,25},{17,1},{25,9},{2,18},{10... | collective-permute-start | bytes 98312 | tf_op jit(solution)/shard_map/ppermute | solution.py:325
  17.3 4.6 %collective-permute-start.2 = (bf16[256,128]{1,0:T(8,128)(2,1)S(1)}, bf16[256,128]{1,0:T(8,128)(2,1)S(1)}, u32[]{:S(2)}, u32[]{:S(2)}) collective-permute-start(bf16[256,128]{1,0:T(8,128)(2,1)S(1)} %join.5.rest_1_.refs_0_), channel_id=1, source_target_pairs={{0,2},{1,3},{2,0},{3,1},{4,6},{5,7},{6,4},{7,5},{8,10},{9,11},{10,... | collective-permute-start | bytes 196616 | tf_op jit(solution)/shard_map/ppermute | solution.py:325
  18.7 12.5 %collective-permute-start.7 = (bf16[1152,128]{1,0:T(8,128)(2,1)S(1)}, bf16[1152,128]{1,0:T(8,128)(2,1)S(1)}, u32[]{:S(2)}, u32[]{:S(2)}) collective-permute-start(bf16[1152,128]{1,0:T(8,128)(2,1)S(1)} %get-tuple-element.23.rest_2_), channel_id=1, source_target_pairs={{0,8},{8,0},{16,24},{24,16},{1,9},{9,1},{17,25},{25,17},{2,10},{10... | collective-permute-start | bytes 884744 | tf_op jit(solution)/shard_map/ppermute | solution.py:325
  21.9 5.0 %collective-permute-start.5 = (bf16[512,128]{1,0:T(8,128)(2,1)S(1)}, bf16[512,128]{1,0:T(8,128)(2,1)S(1)}, u32[]{:S(2)}, u32[]{:S(2)}) collective-permute-start(bf16[512,128]{1,0:T(8,128)(2,1)S(1)} %join.6.rest_1_.refs_0_), channel_id=1, source_target_pairs={{0,4},{1,5},{2,6},{3,7},{4,0},{5,1},{6,2},{7,3},{8,12},{9,13},{10,... | collective-permute-start | bytes 393224 | tf_op jit(solution)/shard_map/ppermute | solution.py:325
  23.3 7.9 %collective-permute-start.8 = (bf16[1152,128]{1,0:T(8,128)(2,1)S(1)}, bf16[1152,128]{1,0:T(8,128)(2,1)S(1)}, u32[]{:S(2)}, u32[]{:S(2)}) collective-permute-start(bf16[1152,128]{1,0:T(8,128)(2,1)S(1)} %get-tuple-element.26), channel_id=1, source_target_pairs={{0,1},{1,0},{2,3},{3,2},{4,5},{5,4},{6,7},{7,6},{8,16},{9,17},{10,... | collective-permute-start | bytes 884744 | tf_op jit(solution)/shard_map/ppermute | solution.py:396
  27.0 6.6 %collective-permute-start.6 = (bf16[1024,128]{1,0:T(8,128)(2,1)S(1)}, bf16[1024,128]{1,0:T(8,128)(2,1)S(1)}, u32[]{:S(2)}, u32[]{:S(2)}) collective-permute-start(bf16[1024,128]{1,0:T(8,128)(2,1)S(1)} %join.7.rest_0_.refs_0_), channel_id=1, source_target_pairs={{0,1},{1,0},{2,3},{3,2},{4,5},{5,4},{6,7},{7,6},{8,9},{9,8},{10,11... | collective-permute-start | bytes 786440 | tf_op jit(solution)/shard_map/ppermute | solution.py:325
  31.2 2.4 %copy-start = (bf16[128,128]{1,0:T(8,128)(2,1)S(1)}, bf16[128,128]{1,0:T(8,128)(2,1)}, u32[]{:S(2)}) copy-start(bf16[128,128]{1,0:T(8,128)(2,1)} %refs_3_.1) | copy-start | bytes 98308
  31.2 2.4 %copy-start.1 = (bf16[128,128]{1,0:T(8,128)(2,1)S(1)}, bf16[128,128]{1,0:T(8,128)(2,1)}, u32[]{:S(2)}) copy-start(bf16[128,128]{1,0:T(8,128)(2,1)} %refs_4_.1) | copy-start | bytes 98308
  31.2 2.4 %copy-start.2 = (bf16[128,128]{1,0:T(8,128)(2,1)S(1)}, bf16[128,128]{1,0:T(8,128)(2,1)}, u32[]{:S(2)}) copy-start(bf16[128,128]{1,0:T(8,128)(2,1)} %refs_5_.1) | copy-start | bytes 98308
  31.2 2.4 %copy-start.3 = (bf16[128,128]{1,0:T(8,128)(2,1)S(1)}, bf16[128,128]{1,0:T(8,128)(2,1)}, u32[]{:S(2)}) copy-start(bf16[128,128]{1,0:T(8,128)(2,1)} %refs_6_.1) | copy-start | bytes 98308
  31.2 2.4 %copy-start.4 = (s32[32,8]{0,1:T(8,128)S(1)}, s32[32,8]{0,1:T(8,128)}, u32[]{:S(2)}) copy-start(s32[32,8]{0,1:T(8,128)} %param.13) | copy-start | bytes 3076

commit v8 on v7

--- a/solution.py
+++ b/solution.py
@@ -12,7 +12,7 @@
 F32 = jnp.float32
 S = 64
 DEPTH = 2
-CUTS = (4, 6, 9, 13)
+CUTS = (4, 7, 10, 14)
 IN_VMEM = pl.BlockSpec(memory_space=pltpu.VMEM)
 IN_HBM = pl.BlockSpec(memory_space=pltpu.HBM)
 
@@ -74,17 +74,23 @@
     node = lax.broadcasted_iota(jnp.int32, (S, 2 * tile), 0)
     order = [c for i in range(cy // 2) for c in (i, i + cy // 2)]
     total = jnp.zeros((S, chan), F32)
-    for r in range(rows):
-        pairs = paired(pv_ref[r])
-        onehot = jnp.concatenate(
-            [(jnp.broadcast_to(pairs[i : i + 1], node.shape) == node).astype(F32).astype(BF16) for i in range(cy // 2)],
-            axis=1,
-        )
-        beads_in[r].wait()
-        total += dot(onehot, jnp.concatenate([fv_ref[r, tile * c : tile * (c + 1)] for c in order], axis=0))
-        for ref, low in ((inward_ref, my % 2), (outward_ref, 1 - my % 2)):
-            column = pl.ds(pl.multiple_of((1 - low) * (span - tile), tile), tile)
-            ref[tile * r : tile * (r + 1)] = fv_ref[r, column]
+    for low in range(0, rows, 8):
+        group = range(low, min(low + 8, rows))
+        hot, beads = [], []
+        for r in group:
+            pairs = paired(pv_ref[r])
+            hot += [
+                (jnp.broadcast_to(pairs[i : i + 1], node.shape) == node).astype(F32).astype(BF16) for i in range(cy // 2)
+            ]
+        for r in group:
+            beads_in[r].wait()
+        for r in group:
+            beads += [fv_ref[r, tile * c : tile * (c + 1)] for c in order]
+        total += dot(jnp.concatenate(hot, axis=1), jnp.concatenate(beads, axis=0))
+        for r in group:
+            for ref, low_side in ((inward_ref, my % 2), (outward_ref, 1 - my % 2)):
+                column = pl.ds(pl.multiple_of((1 - low_side) * (span - tile), tile), tile)
+                ref[tile * r : tile * (r + 1)] = fv_ref[r, column]
     pooled_ref[...] = (total * math.sqrt(S / (rows * span))).astype(BF16)
 
 

time: 38.2 us -> 36 us (0.942)
  waiting for transfers between devices: 2.36 us -> 0.45 us
  Pallas kernels: 25.4 us -> 24.2 us
  starting transfers between devices: 9.75 us -> 10.8 us
    ppermute x7, starting transfers between devices: 7.1 us -> 10.6 us  [swap(): lax.ppermute(array, axis, [(i, i ^ bits) for i in range(lax.axis_size(axi...]
    ppermute x2, starting transfers between devices: 2.65 us -> 0.16 us  [swap_across(): return lax.ppermute(array, ('gx', 'gy'), moves)]
    ppermute x7, waiting for transfers between devices: 2.36 us -> 0.44 us  [swap(): lax.ppermute(array, axis, [(i, i ^ bits) for i in range(lax.axis_size(axi...]
    pallas_call x1, Pallas kernels: 4.46 us -> 3.23 us  [pool(): pl.pallas_call(functools.partial(pool_kernel, tile, nx, ny), in_specs=[IN...]
  transfers between devices with their start and end apart: 9 -> 9, of which waited for: 3 -> 2; matrix products, arithmetic and copies ran while one was open for 0% -> 0% of each run, Pallas kernels for 44% -> 47%
where the time goes in v8:
time: 36 us; the launch traced here: 35.8 us
  Pallas kernels  24.2 us (67%)
  starting transfers between devices  10.8 us (30%)
  waiting for transfers between devices  0.45 us (1%)
  between operations  0.37 us (1%)
    pallas_call x6, Pallas kernels, piece(): pl.pallas_call(kernel, in_specs=[IN_VMEM] * (4 + len(done) + len(near)) +...  16.6 us
    ppermute x7, starting transfers between devices, swap(): lax.ppermute(array, axis, [(i, i ^ bits) for i in range(lax.axis_size(axi...  10.6 us
    pallas_call x1, Pallas kernels, final(): pl.pallas_call(functools.partial(final_kernel, nx, ny, len(blocks)), in_s...  4.08 us
    pallas_call x1, Pallas kernels, pool(): pl.pallas_call(functools.partial(pool_kernel, tile, nx, ny), in_specs=[IN...  3.23 us
  transfers between devices with their start and end apart: 9, of which 2 were waited for; matrix products, arithmetic and copies ran while one was open for 0% of the time, Pallas kernels for 47%

profile of v8, /device:TPU:0, one launch (start us, length us, event | category | flops | bytes accessed | tf_op | source)
XLA Modules:
  0.0 35.8 jit_solution(8952217103293253025)
XLA Ops:
  0.0 3.2 %pool.1 = (bf16[16,1024,128]{2,1,0:T(8,128)(2,1)S(1)}, s32[16,16,64]{2,1,0:T(8,128)S(1)}, f32[256,768]{1,0:T(8,128)S(1)}, bf16[128,128]{1,0:T(8,128)(2,1)S(1)}, ...) custom-call(bf16[16,1024,128]{2,1,0:T(8,128)(2,1)} %bitcast.7, ...), custom_call_target="tpu_custom_call" | custom-call | tf_op jit(solution)/shard_map/pool/pallas_call | solution.py:101
  3.2 3.1 %collective-permute-start = (bf16[64,128]{1,0:T(8,128)(2,1)S(1)}, bf16[64,128]{1,0:T(8,128)(2,1)S(1)}, u32[]{:S(2)}, u32[]{:S(2)}) collective-permute-start(bf16[64,128]{1,0:T(8,128)(2,1)S(1)} %get-tuple-element.16.rest_0_.refs_0_), channel_id=1, source_target_pairs={{0,8},{8,0},{16,24},{24,16},{1,9},{9,1},{17,25},{25,17},{2,10},{10... | collective-permute-start | bytes 49160 | tf_op jit(solution)/shard_map/ppermute | solution.py:331
  6.3 0.0 collective-permute-start.3
  6.3 0.2 collective-permute-start.4
  6.5 3.1 %inner_0.1.refs_2_.rest_0_ = bf16[16,1024,256]{2,1,0:T(8,128)(2,1)S(1)} custom-call(bf16[16,1024,128]{2,1,0:T(8,128)(2,1)S(1)} %get-tuple-element.17.fv.fv_ref, s32[16,16,64]{2,1,0:T(8,128)S(1)} %get-tuple-element.18.pv, f32[256,768]{1,0:T(8,128)S(1)} %get-tuple-element.19.mv, bf16[128,128]{1,0:T(8,128)(2,1)S(1)} %get-tuple-element.20.m, ...), custom_call_target="tpu_custom_call" | custom-call | flops 1600000000 | bytes 1000000 | tf_op jit(solution)/shard_map/inner_0/pallas_call | solution.py:266
  9.6 2.9 %collective-permute-start.1 = (bf16[128,128]{1,0:T(8,128)(2,1)S(1)}, bf16[128,128]{1,0:T(8,128)(2,1)S(1)}, u32[]{:S(2)}, u32[]{:S(2)}) collective-permute-start(bf16[128,128]{1,0:T(8,128)(2,1)S(1)} %join.4.rest_1_.refs_0_), channel_id=1, source_target_pairs={{0,16},{8,24},{16,0},{24,8},{1,17},{9,25},{17,1},{25,9},{2,18},{10... | collective-permute-start | bytes 98312 | tf_op jit(solution)/shard_map/ppermute | solution.py:331
  12.6 2.3 %inner_1.1.refs_2_.rest_0_ = bf16[16,1024,256]{2,1,0:T(8,128)(2,1)S(1)} custom-call(bf16[16,1024,128]{2,1,0:T(8,128)(2,1)S(1)} %get-tuple-element.17.fv.fv_ref, s32[16,16,64]{2,1,0:T(8,128)S(1)} %get-tuple-element.18.pv, f32[256,768]{1,0:T(8,128)S(1)} %get-tuple-element.19.mv, ...), custom_call_target="tpu_custom_call", output_to_operand_aliasing={{}: (4, {})} | custom-call | flops 1200000000 | bytes 1000000 | tf_op jit(solution)/shard_map/inner_1/pallas_call | solution.py:266
  14.9 2.2 %collective-permute-start.2 = (bf16[256,128]{1,0:T(8,128)(2,1)S(1)}, bf16[256,128]{1,0:T(8,128)(2,1)S(1)}, u32[]{:S(2)}, u32[]{:S(2)}) collective-permute-start(bf16[256,128]{1,0:T(8,128)(2,1)S(1)} %join.5.rest_1_.refs_0_), channel_id=1, source_target_pairs={{0,2},{1,3},{2,0},{3,1},{4,6},{5,7},{6,4},{7,5},{8,10},{9,11},{10,... | collective-permute-start | bytes 196616 | tf_op jit(solution)/shard_map/ppermute | solution.py:331
  17.1 0.3 edge_rows.1
  17.4 0.1 collective-permute-start.7
  17.5 2.3 %inner_2.1.refs_2_.rest_0_ = bf16[16,1024,256]{2,1,0:T(8,128)(2,1)S(1)} custom-call(bf16[16,1024,128]{2,1,0:T(8,128)(2,1)S(1)} %get-tuple-element.17.fv.fv_ref, s32[16,16,64]{2,1,0:T(8,128)S(1)} %get-tuple-element.18.pv, f32[256,768]{1,0:T(8,128)S(1)} %get-tuple-element.19.mv, ...), custom_call_target="tpu_custom_call", output_to_operand_aliasing={{}: (4, {})} | custom-call | flops 1200000000 | bytes 1000000 | tf_op jit(solution)/shard_map/inner_2/pallas_call | solution.py:266
  19.8 0.1 collective-permute-done.2.refs_1_
  19.9 2.1 %collective-permute-start.5 = (bf16[512,128]{1,0:T(8,128)(2,1)S(1)}, bf16[512,128]{1,0:T(8,128)(2,1)S(1)}, u32[]{:S(2)}, u32[]{:S(2)}) collective-permute-start(bf16[512,128]{1,0:T(8,128)(2,1)S(1)} %join.6.rest_1_.refs_0_), channel_id=1, source_target_pairs={{0,4},{1,5},{2,6},{3,7},{4,0},{5,1},{6,2},{7,3},{8,12},{9,13},{10,... | collective-permute-start | bytes 393224 | tf_op jit(solution)/shard_map/ppermute | solution.py:331
  22.0 3.1 %inner_3.1.refs_2_.out_in = bf16[16,1024,256]{2,1,0:T(8,128)(2,1)S(1)} custom-call(bf16[16,1024,128]{2,1,0:T(8,128)(2,1)S(1)} %get-tuple-element.17.fv.fv_ref, s32[16,16,64]{2,1,0:T(8,128)S(1)} %get-tuple-element.18.pv, f32[256,768]{1,0:T(8,128)S(1)} %get-tuple-element.19.mv, ...), custom_call_target="tpu_custom_call", output_to_operand_aliasing={{}: (4, {})} | custom-call | flops 1600000000 | bytes 1000000 | tf_op jit(solution)/shard_map/inner_3/pallas_call | solution.py:266
  25.1 0.4 %collective-permute-done.5.refs_1_ = bf16[512,128]{1,0:T(8,128)(2,1)S(1)} collective-permute-done((bf16[512,128]{1,0:T(8,128)(2,1)S(1)}, bf16[512,128]{1,0:T(8,128)(2,1)S(1)}, u32[]{:S(2)}, u32[]{:S(2)}) %collective-permute-start.5) | collective-permute-done | bytes 131104 | tf_op jit(solution)/shard_map/ppermute | solution.py:331
  25.5 0.2 collective-permute-start.6
  25.7 3.4 %sides.1.out_in = bf16[16,1024,256]{2,1,0:T(8,128)(2,1)S(1)} custom-call(bf16[16,1024,128]{2,1,0:T(8,128)(2,1)S(1)} %get-tuple-element.17.fv.fv_ref, s32[16,16,64]{2,1,0:T(8,128)S(1)} %get-tuple-element.18.pv, f32[256,768]{1,0:T(8,128)S(1)} %get-tuple-element.19.mv, bf16[128,128]{1,0:T(8,128)(2,1)S(1)} %get-tuple-element.20.m, ...), custom_call_target="tpu_custom_call", output_to_operand_aliasing={{}: (4, {})} | custom-call | flops 1400000000 | bytes 1000000 | tf_op jit(solution)/shard_map/sides/pallas_call | solution.py:266
  29.1 0.0 copy-start
  29.1 0.0 copy-start.1
  29.1 0.0 copy-start.2
  29.1 0.0 copy-start.3
  29.1 0.0 copy-start.4
  29.2 2.3 %ends.1.refs_7_ = bf16[16,1024,256]{2,1,0:T(8,128)(2,1)S(1)} custom-call(bf16[16,1024,128]{2,1,0:T(8,128)(2,1)S(1)} %get-tuple-element.17.fv.fv_ref, s32[16,16,64]{2,1,0:T(8,128)S(1)} %get-tuple-element.18.pv, f32[256,768]{1,0:T(8,128)S(1)} %get-tuple-element.19.mv, bf16[128,128]{1,0:T(8,128)(2,1)S(1)} %get-tuple-element.20.m, ...), custom_call_target="tpu_custom_call", output_to_operand_aliasing={{}: (4, {})} | custom-call | flops 800000000 | bytes 1000000 | tf_op jit(solution)/shard_map/ends/pallas_call | solution.py:266
  31.5 4.1 %final.1 = bf16[16,1024,128]{2,1,0:T(8,128)(2,1)} custom-call(bf16[1024,128]{1,0:T(8,128)(2,1)S(1)} %join.7.rest_0_.refs_0_, bf16[1024,128]{1,0:T(8,128)(2,1)S(1)} %collective-permute-done.6.refs_1_, s32[8,32]{1,0:T(8,128)S(1)} %bitcast.6, bf16[128,128]{1,0:T(8,128)(2,1)S(1)} %copy-done, bf16[128,128]{1,0:T(8,128)(2,1)S(1)} %copy-done.1, ...), custom_call_target="tpu_custom_call" | custom-call | tf_op jit(solution)/shard_map/final/pallas_call | solution.py:315
  (17 shorter events, 0.1 us)
Async XLA Ops:
  3.2 6.4 %collective-permute-start = (bf16[64,128]{1,0:T(8,128)(2,1)S(1)}, bf16[64,128]{1,0:T(8,128)(2,1)S(1)}, u32[]{:S(2)}, u32[]{:S(2)}) collective-permute-start(bf16[64,128]{1,0:T(8,128)(2,1)S(1)} %get-tuple-element.16.rest_0_.refs_0_), channel_id=1, source_target_pairs={{0,8},{8,0},{16,24},{24,16},{1,9},{9,1},{17,25},{25,17},{2,10},{10... | collective-permute-start | bytes 49160 | tf_op jit(solution)/shard_map/ppermute | solution.py:331
  6.3 10.8 %collective-permute-start.3 = (bf16[1024,128]{1,0:T(8,128)(2,1)S(1)}, bf16[1024,128]{1,0:T(8,128)(2,1)S(1)}, u32[]{:S(2)}, u32[]{:S(2)}) collective-permute-start(bf16[1024,128]{1,0:T(8,128)(2,1)S(1)} %get-tuple-element.21), channel_id=1, source_target_pairs={{0,1},{1,0},{2,3},{3,2},{4,5},{5,4},{6,7},{7,6},{8,9},{9,8},{10,11... | collective-permute-start | bytes 786440 | tf_op jit(solution)/shard_map/ppermute | solution.py:331
  6.3 10.8 %collective-permute-start.4 = (bf16[1024,128]{1,0:T(8,128)(2,1)S(1)}, bf16[1024,128]{1,0:T(8,128)(2,1)S(1)}, u32[]{:S(2)}, u32[]{:S(2)}) collective-permute-start(bf16[1024,128]{1,0:T(8,128)(2,1)S(1)} %get-tuple-element.22), channel_id=1, source_target_pairs={{0,8},{1,2},{2,1},{3,4},{4,3},{5,6},{6,5},{7,15},{8,0},{9,10},{10,... | collective-permute-start | bytes 786440 | tf_op jit(solution)/shard_map/ppermute | solution.py:402
  9.6 5.3 %collective-permute-start.1 = (bf16[128,128]{1,0:T(8,128)(2,1)S(1)}, bf16[128,128]{1,0:T(8,128)(2,1)S(1)}, u32[]{:S(2)}, u32[]{:S(2)}) collective-permute-start(bf16[128,128]{1,0:T(8,128)(2,1)S(1)} %join.4.rest_1_.refs_0_), channel_id=1, source_target_pairs={{0,16},{8,24},{16,0},{24,8},{1,17},{9,25},{17,1},{25,9},{2,18},{10... | collective-permute-start | bytes 98312 | tf_op jit(solution)/shard_map/ppermute | solution.py:331
  14.9 4.9 %collective-permute-start.2 = (bf16[256,128]{1,0:T(8,128)(2,1)S(1)}, bf16[256,128]{1,0:T(8,128)(2,1)S(1)}, u32[]{:S(2)}, u32[]{:S(2)}) collective-permute-start(bf16[256,128]{1,0:T(8,128)(2,1)S(1)} %join.5.rest_1_.refs_0_), channel_id=1, source_target_pairs={{0,2},{1,3},{2,0},{3,1},{4,6},{5,7},{6,4},{7,5},{8,10},{9,11},{10,... | collective-permute-start | bytes 196616 | tf_op jit(solution)/shard_map/ppermute | solution.py:331
  17.4 11.8 %collective-permute-start.7 = (bf16[1152,128]{1,0:T(8,128)(2,1)S(1)}, bf16[1152,128]{1,0:T(8,128)(2,1)S(1)}, u32[]{:S(2)}, u32[]{:S(2)}) collective-permute-start(bf16[1152,128]{1,0:T(8,128)(2,1)S(1)} %get-tuple-element.23.rest_2_), channel_id=1, source_target_pairs={{0,8},{8,0},{16,24},{24,16},{1,9},{9,1},{17,25},{25,17},{2,10},{10... | collective-permute-start | bytes 884744 | tf_op jit(solution)/shard_map/ppermute | solution.py:331
  19.9 5.6 %collective-permute-start.5 = (bf16[512,128]{1,0:T(8,128)(2,1)S(1)}, bf16[512,128]{1,0:T(8,128)(2,1)S(1)}, u32[]{:S(2)}, u32[]{:S(2)}) collective-permute-start(bf16[512,128]{1,0:T(8,128)(2,1)S(1)} %join.6.rest_1_.refs_0_), channel_id=1, source_target_pairs={{0,4},{1,5},{2,6},{3,7},{4,0},{5,1},{6,2},{7,3},{8,12},{9,13},{10,... | collective-permute-start | bytes 393224 | tf_op jit(solution)/shard_map/ppermute | solution.py:331
  22.0 7.2 %collective-permute-start.8 = (bf16[1152,128]{1,0:T(8,128)(2,1)S(1)}, bf16[1152,128]{1,0:T(8,128)(2,1)S(1)}, u32[]{:S(2)}, u32[]{:S(2)}) collective-permute-start(bf16[1152,128]{1,0:T(8,128)(2,1)S(1)} %get-tuple-element.26), channel_id=1, source_target_pairs={{0,1},{1,0},{2,3},{3,2},{4,5},{5,4},{6,7},{7,6},{8,16},{9,17},{10,... | collective-permute-start | bytes 884744 | tf_op jit(solution)/shard_map/ppermute | solution.py:402
  25.5 6.0 %collective-permute-start.6 = (bf16[1024,128]{1,0:T(8,128)(2,1)S(1)}, bf16[1024,128]{1,0:T(8,128)(2,1)S(1)}, u32[]{:S(2)}, u32[]{:S(2)}) collective-permute-start(bf16[1024,128]{1,0:T(8,128)(2,1)S(1)} %join.7.rest_0_.refs_0_), channel_id=1, source_target_pairs={{0,1},{1,0},{2,3},{3,2},{4,5},{5,4},{6,7},{7,6},{8,9},{9,8},{10,11... | collective-permute-start | bytes 786440 | tf_op jit(solution)/shard_map/ppermute | solution.py:331
  29.1 2.4 %copy-start = (bf16[128,128]{1,0:T(8,128)(2,1)S(1)}, bf16[128,128]{1,0:T(8,128)(2,1)}, u32[]{:S(2)}) copy-start(bf16[128,128]{1,0:T(8,128)(2,1)} %refs_3_.1) | copy-start | bytes 98308
  29.1 2.4 %copy-start.1 = (bf16[128,128]{1,0:T(8,128)(2,1)S(1)}, bf16[128,128]{1,0:T(8,128)(2,1)}, u32[]{:S(2)}) copy-start(bf16[128,128]{1,0:T(8,128)(2,1)} %refs_4_.1) | copy-start | bytes 98308
  29.1 2.4 %copy-start.2 = (bf16[128,128]{1,0:T(8,128)(2,1)S(1)}, bf16[128,128]{1,0:T(8,128)(2,1)}, u32[]{:S(2)}) copy-start(bf16[128,128]{1,0:T(8,128)(2,1)} %refs_5_.1) | copy-start | bytes 98308
  29.1 2.4 %copy-start.3 = (bf16[128,128]{1,0:T(8,128)(2,1)S(1)}, bf16[128,128]{1,0:T(8,128)(2,1)}, u32[]{:S(2)}) copy-start(bf16[128,128]{1,0:T(8,128)(2,1)} %refs_6_.1) | copy-start | bytes 98308
  29.1 2.4 %copy-start.4 = (s32[32,8]{0,1:T(8,128)S(1)}, s32[32,8]{0,1:T(8,128)}, u32[]{:S(2)}) copy-start(s32[32,8]{0,1:T(8,128)} %param.13) | copy-start | bytes 3076

commit v9 on v8

--- a/solution.py
+++ b/solution.py
@@ -12,7 +12,7 @@
 F32 = jnp.float32
 S = 64
 DEPTH = 2
-CUTS = (4, 7, 10, 14)
+CUTS = (3, 6, 9, 12)
 IN_VMEM = pl.BlockSpec(memory_space=pltpu.VMEM)
 IN_HBM = pl.BlockSpec(memory_space=pltpu.HBM)
 
@@ -91,13 +91,14 @@
             for ref, low_side in ((inward_ref, my % 2), (outward_ref, 1 - my % 2)):
                 column = pl.ds(pl.multiple_of((1 - low_side) * (span - tile), tile), tile)
                 ref[tile * r : tile * (r + 1)] = fv_ref[r, column]
-    pooled_ref[...] = (total * math.sqrt(S / (rows * span))).astype(BF16)
+    pooled = (total * math.sqrt(S / (rows * span))).astype(BF16)
+    pooled_ref[...] = pooled
+    inward_ref[tile * rows :] = pooled
 
 
 def pool(nx, ny, features, tile_mask, pool_map, w_query, w_key):
     cx, cy, tile, chan = features.shape
     span = cy * tile
-    edge = pltpu.VMEM((cx * tile, chan), BF16)
     return pl.pallas_call(
         functools.partial(pool_kernel, tile, nx, ny),
         in_specs=[IN_HBM] * 5,
@@ -108,8 +109,8 @@
             pltpu.VMEM((cx * cy, 12 * tile), F32),
             pltpu.VMEM((chan, chan), BF16),
             pltpu.VMEM((S, chan), BF16),
-            edge,
-            edge,
+            pltpu.VMEM((cx * tile + S, chan), BF16),
+            pltpu.VMEM((cx * tile, chan), BF16),
         ],
         scratch_shapes=[
             pltpu.VMEM((9 * cx, cy), jnp.int32),
@@ -284,9 +285,8 @@
     count = nodes.shape[0]
     mx, my = lax.axis_index("gx"), lax.axis_index("gy")
     block = lax.broadcasted_iota(jnp.int32, (readers_ref.shape[0], count), 1) // S
-    rest = block // nx
-    turn = (rest % (ny // 2)) * 2 + rest // (ny // 2)
-    domain = ((block % nx) ^ mx) * ny + (turn ^ my)
+    turn = block // (2 * nx) * 2 + block % 2
+    domain = ((block // 2 % nx) ^ mx) * ny + (turn ^ my)
     lane = lax.broadcasted_iota(jnp.int32, readers_ref.shape, 1)
     mine = jnp.sum(jnp.where(lane == mx * ny + my, readers_ref[...], 0), axis=1, keepdims=True)
     live = jnp.sum(jnp.where(domain == mine, 1.0, 0.0), axis=0, keepdims=True)
@@ -331,24 +331,22 @@
     return lax.ppermute(array, axis, [(i, i ^ bits) for i in range(lax.axis_size(axis))])
 
 
-def join_kernel(count, *refs):
-    parts, out = refs[:count], refs[-1]
-    at = 0
-    for part in parts:
-        out[at : at + part.shape[0]] = part[...]
-        at += part.shape[0]
-
-
-def join(parts, ties):
-    rows = sum(part.shape[0] for part in parts)
+def join_kernel(size, *refs):
+    first_ref, second_ref, *_, out_ref = refs
+    out_ref[:size] = first_ref[...]
+    out_ref[size:] = second_ref[second_ref.shape[0] - size :]
+
+
+def join(first, second, ties):
+    size, chan = first.shape
     return pl.pallas_call(
-        functools.partial(join_kernel, len(parts)),
-        in_specs=[IN_VMEM] * len(parts) + [pl.BlockSpec(memory_space=pl.ANY)] * len(ties),
+        functools.partial(join_kernel, size),
+        in_specs=[IN_VMEM] * 2 + [pl.BlockSpec(memory_space=pl.ANY)] * len(ties),
         out_specs=IN_VMEM,
-        out_shape=pltpu.VMEM((rows, parts[0].shape[1]), BF16),
+        out_shape=pltpu.VMEM((2 * size, chan), BF16),
         compiler_params=params(4),
         name="join",
-    )(*parts, *ties)
+    )(first, second, *ties)
 
 
 def edge_rows_kernel(tile, fv_ref, paired_ref, other_ref, *rest):
@@ -357,13 +355,13 @@
 
     @pl.when(lax.axis_index("gy") % 2 == 1)
     def _():
-        left_ref[...] = paired_ref[...]
+        left_ref[...] = paired_ref[: rows * tile]
         right_ref[...] = other_ref[...]
 
     @pl.when(lax.axis_index("gy") % 2 == 0)
     def _():
         left_ref[...] = other_ref[...]
-        right_ref[...] = paired_ref[...]
+        right_ref[...] = paired_ref[: rows * tile]
 
     odd = lax.axis_index("gx") % 2
     for ref, low in ((inward_ref, odd), (outward_ref, 1 - odd)):
@@ -410,10 +408,12 @@
     cuts = [1] + [1 + (cx - 2) * part // 14 for part in CUTS] + [cx - 1]
     rows = [range(lo, hi) for lo, hi in zip(cuts, cuts[1:])]
     steps = [("gx", 1 << b) for b in range(nx.bit_length() - 1)]
-    steps += [("gy", 1 << b) for b in range(1, ny.bit_length() - 1)] + [("gy", 1)]
+    steps += [("gy", 1 << b) for b in range(1, ny.bit_length() - 1)]
     paired_column = swap(inward, "gy", 1)
     other_column = swap_across(outward, "gy", nx, ny)
-    out, first, ties = None, pooled, (pooled,)
+    out = piece(functools.partial(inner_kernel, rows[0]), len(rows[0]), "inner_0", base, None, (), (pooled,))
+    first = join(pooled, paired_column, (out,))
+    ties = (first,)
     for step, (axis, bit) in enumerate(steps):
         second = swap(first, axis, bit)
         if step == 2:
@@ -423,10 +423,10 @@
             ties += (inward,)
         if step == len(steps) - 1:
             break
-        if step < len(rows) - 1:
-            kernel = functools.partial(inner_kernel, rows[step])
-            out = piece(kernel, len(rows[step]), f"inner_{step}", base, out, (), ties)
-        first = join((first, second), (out,))
+        if step + 1 < len(rows) - 1:
+            kernel = functools.partial(inner_kernel, rows[step + 1])
+            out = piece(kernel, len(rows[step + 1]), f"inner_{step + 1}", base, out, (), ties)
+        first = join(first, second, (out,))
         ties = (first,)
     out = piece(functools.partial(sides_kernel, rows[-1]), len(rows[-1]) + 3.5, "sides", base, out, (left, right), ties)
     out = piece(ends_kernel, 2, "ends", base, out, (left, right, paired_row, other_row), (), [pltpu.VMEM(inward.shape, BF16)] * 2)

time: 36 us -> 37.2 us (1.033); the launches traced: 35.8 us -> 36.6 us
  waiting for transfers between devices: 0.45 us -> 3.4 us
  starting transfers between devices: 10.8 us -> 8.76 us
    ppermute x7 -> x6, starting transfers between devices: 10.6 us -> 6.1 us  [swap(): lax.ppermute(array, axis, [(i, i ^ bits) for i in range(lax.axis_size(axi...]
    ppermute x7 -> x6, waiting for transfers between devices: 0.44 us -> 3.39 us  [swap(): lax.ppermute(array, axis, [(i, i ^ bits) for i in range(lax.axis_size(axi...]
    ppermute x2, starting transfers between devices: 0.16 us -> 2.65 us  [swap_across(): return lax.ppermute(array, ('gx', 'gy'), moves)]
  transfers between devices with their start and end apart: 9 -> 8, of which waited for: 2 -> 4; matrix products, arithmetic and copies ran while one was open for 0% -> 0% of each run, Pallas kernels for 47% -> 46%
where the time goes in v9:
time: 37.2 us; the launch traced here: 36.6 us
  Pallas kernels  24.1 us (65%)
  starting transfers between devices  8.76 us (24%)
  waiting for transfers between devices  3.4 us (9%)
    pallas_call x6, Pallas kernels, piece(): pl.pallas_call(kernel, in_specs=[IN_VMEM] * (4 + len(done) + len(near)) +...  16.5 us
    ppermute x6, starting transfers between devices, swap(): lax.ppermute(array, axis, [(i, i ^ bits) for i in range(lax.axis_size(axi...  6.1 us
    pallas_call x1, Pallas kernels, final(): pl.pallas_call(functools.partial(final_kernel, nx, ny, len(blocks)), in_s...  4.07 us
    ppermute x6, waiting for transfers between devices, swap(): lax.ppermute(array, axis, [(i, i ^ bits) for i in range(lax.axis_size(axi...  3.39 us
    pallas_call x1, Pallas kernels, pool(): pl.pallas_call(functools.partial(pool_kernel, tile, nx, ny), in_specs=[IN...  3.23 us
    ppermute x2, starting transfers between devices, swap_across(): return lax.ppermute(array, ('gx', 'gy'), moves)  2.65 us
  transfers between devices with their start and end apart: 8, of which 4 were waited for; matrix products, arithmetic and copies ran while one was open for 0% of the time, Pallas kernels for 46%

profile of v9, /device:TPU:0, one launch (start us, length us, event | category | flops | bytes accessed | tf_op | source)
XLA Modules:
  0.0 36.6 jit_solution(17032730970240357509)
XLA Ops:
  0.0 3.2 %pool.1 = (bf16[16,1024,128]{2,1,0:T(8,128)(2,1)S(1)}, s32[16,16,64]{2,1,0:T(8,128)S(1)}, f32[256,768]{1,0:T(8,128)S(1)}, bf16[128,128]{1,0:T(8,128)(2,1)S(1)}, ...) custom-call(bf16[16,1024,128]{2,1,0:T(8,128)(2,1)} %bitcast.7, ...), custom_call_target="tpu_custom_call" | custom-call | tf_op jit(solution)/shard_map/pool/pallas_call | solution.py:102
  3.2 0.5 %collective-permute-start = (bf16[1088,128]{1,0:T(8,128)(2,1)S(1)}, bf16[1088,128]{1,0:T(8,128)(2,1)S(1)}, u32[]{:S(2)}, u32[]{:S(2)}) collective-permute-start(bf16[1088,128]{1,0:T(8,128)(2,1)S(1)} %get-tuple-element.17), channel_id=1, source_target_pairs={{0,1},{1,0},{2,3},{3,2},{4,5},{5,4},{6,7},{7,6},{8,9},{9,8},{10,11... | collective-permute-start | bytes 835592 | tf_op jit(solution)/shard_map/ppermute | solution.py:331
  3.8 2.7 %collective-permute-start.4 = (bf16[1024,128]{1,0:T(8,128)(2,1)S(1)}, bf16[1024,128]{1,0:T(8,128)(2,1)S(1)}, u32[]{:S(2)}, u32[]{:S(2)}) collective-permute-start(bf16[1024,128]{1,0:T(8,128)(2,1)S(1)} %get-tuple-element.22), channel_id=1, source_target_pairs={{0,8},{1,2},{2,1},{3,4},{4,3},{5,6},{6,5},{7,15},{8,0},{9,10},{10,... | collective-permute-start | bytes 786440 | tf_op jit(solution)/shard_map/ppermute | solution.py:400
  6.4 2.3 %inner_0.1.refs_2_.rest_0_ = bf16[16,1024,256]{2,1,0:T(8,128)(2,1)S(1)} custom-call(bf16[16,1024,128]{2,1,0:T(8,128)(2,1)S(1)} %get-tuple-element.18.fv.fv_ref, s32[16,16,64]{2,1,0:T(8,128)S(1)} %get-tuple-element.19.pv, f32[256,768]{1,0:T(8,128)S(1)} %get-tuple-element.20.mv, bf16[128,128]{1,0:T(8,128)(2,1)S(1)} %get-tuple-element.21.m, ...), custom_call_target="tpu_custom_call" | custom-call | flops 1200000000 | bytes 1000000 | tf_op jit(solution)/shard_map/inner_0/pallas_call | solution.py:267
  8.8 0.1 collective-permute-start.1
  8.9 2.3 %inner_1.1.refs_2_.rest_0_ = bf16[16,1024,256]{2,1,0:T(8,128)(2,1)S(1)} custom-call(bf16[16,1024,128]{2,1,0:T(8,128)(2,1)S(1)} %get-tuple-element.18.fv.fv_ref, s32[16,16,64]{2,1,0:T(8,128)S(1)} %get-tuple-element.19.pv, f32[256,768]{1,0:T(8,128)S(1)} %get-tuple-element.20.mv, ...), custom_call_target="tpu_custom_call", output_to_operand_aliasing={{}: (4, {})} | custom-call | flops 1200000000 | bytes 1000000 | tf_op jit(solution)/shard_map/inner_1/pallas_call | solution.py:267
  11.2 1.6 %collective-permute-done.1.refs_1_ = bf16[128,128]{1,0:T(8,128)(2,1)S(1)} collective-permute-done((bf16[128,128]{1,0:T(8,128)(2,1)S(1)}, bf16[128,128]{1,0:T(8,128)(2,1)S(1)}, u32[]{:S(2)}, u32[]{:S(2)}) %collective-permute-start.1) | collective-permute-done | bytes 32800 | tf_op jit(solution)/shard_map/ppermute | solution.py:331
  12.8 2.6 %collective-permute-start.2 = (bf16[256,128]{1,0:T(8,128)(2,1)S(1)}, bf16[256,128]{1,0:T(8,128)(2,1)S(1)}, u32[]{:S(2)}, u32[]{:S(2)}) collective-permute-start(bf16[256,128]{1,0:T(8,128)(2,1)S(1)} %join.5.rest_1_.refs_0_), channel_id=1, source_target_pairs={{0,16},{8,24},{16,0},{24,8},{1,17},{9,25},{17,1},{25,9},{2,18},{10... | collective-permute-start | bytes 196616 | tf_op jit(solution)/shard_map/ppermute | solution.py:331
  15.3 2.3 %inner_2.1.refs_2_.rest_0_ = bf16[16,1024,256]{2,1,0:T(8,128)(2,1)S(1)} custom-call(bf16[16,1024,128]{2,1,0:T(8,128)(2,1)S(1)} %get-tuple-element.18.fv.fv_ref, s32[16,16,64]{2,1,0:T(8,128)S(1)} %get-tuple-element.19.pv, f32[256,768]{1,0:T(8,128)S(1)} %get-tuple-element.20.mv, ...), custom_call_target="tpu_custom_call", output_to_operand_aliasing={{}: (4, {})} | custom-call | flops 1200000000 | bytes 1000000 | tf_op jit(solution)/shard_map/inner_2/pallas_call | solution.py:267
  17.7 1.2 %collective-permute-done.2.refs_1_ = bf16[256,128]{1,0:T(8,128)(2,1)S(1)} collective-permute-done((bf16[256,128]{1,0:T(8,128)(2,1)S(1)}, bf16[256,128]{1,0:T(8,128)(2,1)S(1)}, u32[]{:S(2)}, u32[]{:S(2)}) %collective-permute-start.2) | collective-permute-done | bytes 65568 | tf_op jit(solution)/shard_map/ppermute | solution.py:331
  18.9 1.6 %collective-permute-start.3 = (bf16[512,128]{1,0:T(8,128)(2,1)S(1)}, bf16[512,128]{1,0:T(8,128)(2,1)S(1)}, u32[]{:S(2)}, u32[]{:S(2)}) collective-permute-start(bf16[512,128]{1,0:T(8,128)(2,1)S(1)} %join.6.rest_1_.refs_0_), channel_id=1, source_target_pairs={{0,2},{1,3},{2,0},{3,1},{4,6},{5,7},{6,4},{7,5},{8,10},{9,11},{10,... | collective-permute-start | bytes 393224 | tf_op jit(solution)/shard_map/ppermute | solution.py:331
  20.5 0.3 edge_rows.1
  20.7 0.4 %collective-permute-start.6 = (bf16[1152,128]{1,0:T(8,128)(2,1)S(1)}, bf16[1152,128]{1,0:T(8,128)(2,1)S(1)}, u32[]{:S(2)}, u32[]{:S(2)}) collective-permute-start(bf16[1152,128]{1,0:T(8,128)(2,1)S(1)} %get-tuple-element.23.rest_2_), channel_id=1, source_target_pairs={{0,8},{8,0},{16,24},{24,16},{1,9},{9,1},{17,25},{25,17},{2,10},{10... | collective-permute-start | bytes 884744 | tf_op jit(solution)/shard_map/ppermute | solution.py:331
  21.1 2.3 %inner_3.1.refs_2_.out_in = bf16[16,1024,256]{2,1,0:T(8,128)(2,1)S(1)} custom-call(bf16[16,1024,128]{2,1,0:T(8,128)(2,1)S(1)} %get-tuple-element.18.fv.fv_ref, s32[16,16,64]{2,1,0:T(8,128)S(1)} %get-tuple-element.19.pv, f32[256,768]{1,0:T(8,128)S(1)} %get-tuple-element.20.mv, ...), custom_call_target="tpu_custom_call", output_to_operand_aliasing={{}: (4, {})} | custom-call | flops 1200000000 | bytes 1000000 | tf_op jit(solution)/shard_map/inner_3/pallas_call | solution.py:267
  23.5 0.6 %collective-permute-done.3.refs_1_ = bf16[512,128]{1,0:T(8,128)(2,1)S(1)} collective-permute-done((bf16[512,128]{1,0:T(8,128)(2,1)S(1)}, bf16[512,128]{1,0:T(8,128)(2,1)S(1)}, u32[]{:S(2)}, u32[]{:S(2)}) %collective-permute-start.3) | collective-permute-done | bytes 131104 | tf_op jit(solution)/shard_map/ppermute | solution.py:331
  24.1 1.0 %collective-permute-start.5 = (bf16[1024,128]{1,0:T(8,128)(2,1)S(1)}, bf16[1024,128]{1,0:T(8,128)(2,1)S(1)}, u32[]{:S(2)}, u32[]{:S(2)}) collective-permute-start(bf16[1024,128]{1,0:T(8,128)(2,1)S(1)} %join.7.rest_0_.refs_0_), channel_id=1, source_target_pairs={{0,4},{1,5},{2,6},{3,7},{4,0},{5,1},{6,2},{7,3},{8,12},{9,13},{10,... | collective-permute-start | bytes 786440 | tf_op jit(solution)/shard_map/ppermute | solution.py:331
  25.0 4.8 %sides.1.out_in = bf16[16,1024,256]{2,1,0:T(8,128)(2,1)S(1)} custom-call(bf16[16,1024,128]{2,1,0:T(8,128)(2,1)S(1)} %get-tuple-element.18.fv.fv_ref, s32[16,16,64]{2,1,0:T(8,128)S(1)} %get-tuple-element.19.pv, f32[256,768]{1,0:T(8,128)S(1)} %get-tuple-element.20.mv, bf16[128,128]{1,0:T(8,128)(2,1)S(1)} %get-tuple-element.21.m, ...), custom_call_target="tpu_custom_call", output_to_operand_aliasing={{}: (4, {})} | custom-call | flops 2200000000 | bytes 1000000 | tf_op jit(solution)/shard_map/sides/pallas_call | solution.py:267
  29.9 0.0 copy-start
  29.9 0.0 copy-start.1
  29.9 0.0 copy-start.2
  29.9 0.0 copy-start.4
  29.9 2.3 %ends.1.refs_7_ = bf16[16,1024,256]{2,1,0:T(8,128)(2,1)S(1)} custom-call(bf16[16,1024,128]{2,1,0:T(8,128)(2,1)S(1)} %get-tuple-element.18.fv.fv_ref, s32[16,16,64]{2,1,0:T(8,128)S(1)} %get-tuple-element.19.pv, f32[256,768]{1,0:T(8,128)S(1)} %get-tuple-element.20.mv, bf16[128,128]{1,0:T(8,128)(2,1)S(1)} %get-tuple-element.21.m, ...), custom_call_target="tpu_custom_call", output_to_operand_aliasing={{}: (4, {})} | custom-call | flops 800000000 | bytes 1000000 | tf_op jit(solution)/shard_map/ends/pallas_call | solution.py:267
  32.3 0.1 collective-permute-done.5.refs_1_
  32.3 4.1 %final.1 = bf16[16,1024,128]{2,1,0:T(8,128)(2,1)} custom-call(bf16[1024,128]{1,0:T(8,128)(2,1)S(1)} %join.7.rest_0_.refs_0_, bf16[1024,128]{1,0:T(8,128)(2,1)S(1)} %collective-permute-done.5.refs_1_, s32[8,32]{1,0:T(8,128)S(1)} %bitcast.6, bf16[128,128]{1,0:T(8,128)(2,1)S(1)} %copy-done, bf16[128,128]{1,0:T(8,128)(2,1)S(1)} %copy-done.1, ...), custom_call_target="tpu_custom_call" | custom-call | tf_op jit(solution)/shard_map/final/pallas_call | solution.py:315
  (15 shorter events, 0.1 us)
Async XLA Ops:
  3.2 5.5 %collective-permute-start = (bf16[1088,128]{1,0:T(8,128)(2,1)S(1)}, bf16[1088,128]{1,0:T(8,128)(2,1)S(1)}, u32[]{:S(2)}, u32[]{:S(2)}) collective-permute-start(bf16[1088,128]{1,0:T(8,128)(2,1)S(1)} %get-tuple-element.17), channel_id=1, source_target_pairs={{0,1},{1,0},{2,3},{3,2},{4,5},{5,4},{6,7},{7,6},{8,9},{9,8},{10,11... | collective-permute-start | bytes 835592 | tf_op jit(solution)/shard_map/ppermute | solution.py:331
  3.8 16.7 %collective-permute-start.4 = (bf16[1024,128]{1,0:T(8,128)(2,1)S(1)}, bf16[1024,128]{1,0:T(8,128)(2,1)S(1)}, u32[]{:S(2)}, u32[]{:S(2)}) collective-permute-start(bf16[1024,128]{1,0:T(8,128)(2,1)S(1)} %get-tuple-element.22), channel_id=1, source_target_pairs={{0,8},{1,2},{2,1},{3,4},{4,3},{5,6},{6,5},{7,15},{8,0},{9,10},{10,... | collective-permute-start | bytes 786440 | tf_op jit(solution)/shard_map/ppermute | solution.py:400
  8.8 4.0 %collective-permute-start.1 = (bf16[128,128]{1,0:T(8,128)(2,1)S(1)}, bf16[128,128]{1,0:T(8,128)(2,1)S(1)}, u32[]{:S(2)}, u32[]{:S(2)}) collective-permute-start(bf16[128,128]{1,0:T(8,128)(2,1)S(1)} %join.4.rest_1_.refs_0_), channel_id=1, source_target_pairs={{0,8},{8,0},{16,24},{24,16},{1,9},{9,1},{17,25},{25,17},{2,10},{10... | collective-permute-start | bytes 98312 | tf_op jit(solution)/shard_map/ppermute | solution.py:331
  12.8 6.1 %collective-permute-start.2 = (bf16[256,128]{1,0:T(8,128)(2,1)S(1)}, bf16[256,128]{1,0:T(8,128)(2,1)S(1)}, u32[]{:S(2)}, u32[]{:S(2)}) collective-permute-start(bf16[256,128]{1,0:T(8,128)(2,1)S(1)} %join.5.rest_1_.refs_0_), channel_id=1, source_target_pairs={{0,16},{8,24},{16,0},{24,8},{1,17},{9,25},{17,1},{25,9},{2,18},{10... | collective-permute-start | bytes 196616 | tf_op jit(solution)/shard_map/ppermute | solution.py:331
  18.9 5.2 %collective-permute-start.3 = (bf16[512,128]{1,0:T(8,128)(2,1)S(1)}, bf16[512,128]{1,0:T(8,128)(2,1)S(1)}, u32[]{:S(2)}, u32[]{:S(2)}) collective-permute-start(bf16[512,128]{1,0:T(8,128)(2,1)S(1)} %join.6.rest_1_.refs_0_), channel_id=1, source_target_pairs={{0,2},{1,3},{2,0},{3,1},{4,6},{5,7},{6,4},{7,5},{8,10},{9,11},{10,... | collective-permute-start | bytes 393224 | tf_op jit(solution)/shard_map/ppermute | solution.py:331
  20.7 9.2 %collective-permute-start.6 = (bf16[1152,128]{1,0:T(8,128)(2,1)S(1)}, bf16[1152,128]{1,0:T(8,128)(2,1)S(1)}, u32[]{:S(2)}, u32[]{:S(2)}) collective-permute-start(bf16[1152,128]{1,0:T(8,128)(2,1)S(1)} %get-tuple-element.23.rest_2_), channel_id=1, source_target_pairs={{0,8},{8,0},{16,24},{24,16},{1,9},{9,1},{17,25},{25,17},{2,10},{10... | collective-permute-start | bytes 884744 | tf_op jit(solution)/shard_map/ppermute | solution.py:331
  21.1 8.8 %collective-permute-start.7 = (bf16[1152,128]{1,0:T(8,128)(2,1)S(1)}, bf16[1152,128]{1,0:T(8,128)(2,1)S(1)}, u32[]{:S(2)}, u32[]{:S(2)}) collective-permute-start(bf16[1152,128]{1,0:T(8,128)(2,1)S(1)} %get-tuple-element.26), channel_id=1, source_target_pairs={{0,1},{1,0},{2,3},{3,2},{4,5},{5,4},{6,7},{7,6},{8,16},{9,17},{10,... | collective-permute-start | bytes 884744 | tf_op jit(solution)/shard_map/ppermute | solution.py:400
  24.1 8.2 %collective-permute-start.5 = (bf16[1024,128]{1,0:T(8,128)(2,1)S(1)}, bf16[1024,128]{1,0:T(8,128)(2,1)S(1)}, u32[]{:S(2)}, u32[]{:S(2)}) collective-permute-start(bf16[1024,128]{1,0:T(8,128)(2,1)S(1)} %join.7.rest_0_.refs_0_), channel_id=1, source_target_pairs={{0,4},{1,5},{2,6},{3,7},{4,0},{5,1},{6,2},{7,3},{8,12},{9,13},{10,... | collective-permute-start | bytes 786440 | tf_op jit(solution)/shard_map/ppermute | solution.py:331
  29.9 2.5 %copy-start = (bf16[128,128]{1,0:T(8,128)(2,1)S(1)}, bf16[128,128]{1,0:T(8,128)(2,1)}, u32[]{:S(2)}) copy-start(bf16[128,128]{1,0:T(8,128)(2,1)} %refs_3_.1) | copy-start | bytes 98308
  29.9 2.4 %copy-start.1 = (bf16[128,128]{1,0:T(8,128)(2,1)S(1)}, bf16[128,128]{1,0:T(8,128)(2,1)}, u32[]{:S(2)}) copy-start(bf16[128,128]{1,0:T(8,128)(2,1)} %refs_4_.1) | copy-start | bytes 98308
  29.9 2.4 %copy-start.2 = (bf16[128,128]{1,0:T(8,128)(2,1)S(1)}, bf16[128,128]{1,0:T(8,128)(2,1)}, u32[]{:S(2)}) copy-start(bf16[128,128]{1,0:T(8,128)(2,1)} %refs_5_.1) | copy-start | bytes 98308
  29.9 2.4 %copy-start.3 = (bf16[128,128]{1,0:T(8,128)(2,1)S(1)}, bf16[128,128]{1,0:T(8,128)(2,1)}, u32[]{:S(2)}) copy-start(bf16[128,128]{1,0:T(8,128)(2,1)} %refs_6_.1) | copy-start | bytes 98308
  29.9 2.4 %copy-start.4 = (s32[32,8]{0,1:T(8,128)S(1)}, s32[32,8]{0,1:T(8,128)}, u32[]{:S(2)}) copy-start(s32[32,8]{0,1:T(8,128)} %param.13) | copy-start | bytes 3076

commit v10 on v8

--- a/solution.py
+++ b/solution.py
@@ -226,8 +226,8 @@
     attend(tile, tasks)
 
 
-def ends_kernel(fv, pv, mv, m, out_in, left, right, paired_row, other_row, *rest):
-    *_, o, above, below = rest
+def ends_kernel(nx, ny, fv, pv, mv, m, out_in, left, right, paired_row, other_row, *rest):
+    first, second, *weights, o, mix, above, below = rest
     cy, tile = pv.shape[1:]
     rows = fv.shape[0]
     refs = (fv, pv, mv, m, o)
@@ -249,6 +249,7 @@
             return (above if r < 0 else below)[2 * tile * j : 2 * tile * (j + 2)]
         return near(r, j)
 
+    coarse(nx, ny, (first, second), *weights, mix)
     tasks = []
     for row in (0, rows - 1):
         node_rows(refs, row)
@@ -260,7 +261,7 @@
     return pl.CostEstimate(flops=int(rows * 400_000_000), bytes_accessed=1_000_000, transcendentals=0)
 
 
-def piece(kernel, rows_done, name, base, out, near=(), ties=(), scratch=()):
+def piece(kernel, rows_done, name, base, out, near=(), ties=()):
     cx, span, chan = base[0].shape
     done = [] if out is None else [out]
     return pl.pallas_call(
@@ -268,7 +269,6 @@
         in_specs=[IN_VMEM] * (4 + len(done) + len(near)) + [pl.BlockSpec(memory_space=pl.ANY)] * len(ties),
         out_specs=IN_VMEM,
         out_shape=pltpu.VMEM((cx, span, 2 * chan), BF16),
-        scratch_shapes=list(scratch),
         input_output_aliases={4: 0} if done else {},
         compiler_params=params(16),
         cost_estimate=estimate(rows_done),
@@ -276,12 +276,9 @@
     )(*base, *done, *near, *ties)
 
 
-def final_kernel(nx, ny, n_blocks, *refs):
-    blocks = refs[:n_blocks]
-    readers_ref, wcq_ref, wck_ref, wcv_ref, wv_ref, o_ref, out_ref, mix, rows_out, sems = refs[n_blocks:]
-    cx, span, chan = rows_out.shape
+def coarse(nx, ny, blocks, readers_ref, wcq_ref, wck_ref, wcv_ref, wv_ref, mix):
     nodes = jnp.concatenate([ref[...] for ref in blocks], axis=0)
-    count = nodes.shape[0]
+    count, chan = nodes.shape
     mx, my = lax.axis_index("gx"), lax.axis_index("gy")
     block = lax.broadcasted_iota(jnp.int32, (readers_ref.shape[0], count), 1) // S
     rest = block // nx
@@ -299,32 +296,48 @@
     mix[chan : chan + S] = (dot(weight.astype(BF16), value) / math.sqrt(S)).astype(BF16)
     mix[chan + S :] = jnp.zeros((chan - S, chan), BF16)
 
+
+def ends(nx, ny, base, out, halos, blocks, readers, w_cquery, w_ckey, w_cvalue, w_value):
+    chan = base[0].shape[2]
+    operands = (*base, out, *halos, *blocks, readers.T, w_cquery, w_ckey, w_cvalue, w_value)
+    return pl.pallas_call(
+        functools.partial(ends_kernel, nx, ny),
+        in_specs=[IN_VMEM] * len(operands),
+        out_specs=[IN_VMEM] * 2,
+        out_shape=[pltpu.VMEM(out.shape, BF16), pltpu.VMEM((2 * chan, chan), BF16)],
+        scratch_shapes=[pltpu.VMEM(halos[-1].shape, BF16)] * 2,
+        input_output_aliases={4: 0},
+        compiler_params=params(16),
+        cost_estimate=estimate(2),
+        name="ends",
+    )(*operands)
+
+
+def final_kernel(o_ref, mix, out_ref, rows_out, sems):
+    rows = rows_out.shape[0]
+
     def send(r):
         return pltpu.make_async_copy(rows_out.at[r], out_ref.at[r], sems.at[r])
 
-    for r in range(cx):
+    for r in range(rows):
         rows_out[r] = dot(o_ref[r], mix[...]).astype(BF16)
         send(r).start()
-    for r in range(cx):
+    for r in range(rows):
         send(r).wait()
 
 
-def final(nx, ny, blocks, readers, w_cquery, w_ckey, w_cvalue, w_value, out):
+def final(out, mix):
     cx, span, wide = out.shape
     chan = wide // 2
     return pl.pallas_call(
-        functools.partial(final_kernel, nx, ny, len(blocks)),
-        in_specs=[IN_VMEM] * (len(blocks) + 6),
+        final_kernel,
+        in_specs=[IN_VMEM] * 2,
         out_specs=IN_HBM,
         out_shape=jax.ShapeDtypeStruct((cx, span, chan), BF16),
-        scratch_shapes=[
-            pltpu.VMEM((2 * chan, chan), BF16),
-            pltpu.VMEM((cx, span, chan), BF16),
-            pltpu.SemaphoreType.DMA((cx,)),
-        ],
+        scratch_shapes=[pltpu.VMEM((cx, span, chan), BF16), pltpu.SemaphoreType.DMA((cx,))],
         compiler_params=params(16),
         name="final",
-    )(*blocks, readers.T, w_cquery, w_ckey, w_cvalue, w_value, out)
+    )(out, mix)
 
 
 def swap(array, axis, bits):
@@ -429,8 +442,9 @@
         first = join((first, second), (out,))
         ties = (first,)
     out = piece(functools.partial(sides_kernel, rows[-1]), len(rows[-1]) + 3.5, "sides", base, out, (left, right), ties)
-    out = piece(ends_kernel, 2, "ends", base, out, (left, right, paired_row, other_row), (), [pltpu.VMEM(inward.shape, BF16)] * 2)
-    update = final(nx, ny, (first, second), readers, w_cquery, w_ckey, w_cvalue, w_value, out)
+    halos = (left, right, paired_row, other_row)
+    out, mix = ends(nx, ny, base, out, halos, (first, second), readers, w_cquery, w_ckey, w_cvalue, w_value)
+    update = final(out, mix)
     return update.reshape(features.shape)
 
 

time: 36 us -> 36 us (level)
    pallas_call x6 -> x5, Pallas kernels: 16.6 us -> 14.3 us  [piece(): pl.pallas_call(kernel, in_specs=[IN_VMEM] * (4 + len(done) + len(near)) +...]
    pallas_call x1 -> x2, Pallas kernels: 4.08 us -> 6.34 us  [the longest x1 3.47 us: final(): pl.pallas_call(final_kernel, in_specs=[IN_VMEM] * 2, out_specs=IN_HBM, ou...]
  transfers between devices with their start and end apart: 9 -> 9, of which waited for: 2 -> 2; matrix products, arithmetic and copies ran while one was open for 0% -> 0% of each run, Pallas kernels for 47% -> 41%
where the time goes in v10:
time: 36 us; the launch traced here: 35.7 us
  Pallas kernels  24.1 us (67%)
  starting transfers between devices  10.8 us (30%)
  waiting for transfers between devices  0.45 us (1%)
    pallas_call x5, Pallas kernels, piece(): pl.pallas_call(kernel, in_specs=[IN_VMEM] * (4 + len(done) + len(near)) +...  14.3 us
    ppermute x7, starting transfers between devices, swap(): lax.ppermute(array, axis, [(i, i ^ bits) for i in range(lax.axis_size(axi...  10.6 us
    pallas_call x1, Pallas kernels, final(): pl.pallas_call(final_kernel, in_specs=[IN_VMEM] * 2, out_specs=IN_HBM, ou...  3.47 us
    pallas_call x1, Pallas kernels, pool(): pl.pallas_call(functools.partial(pool_kernel, tile, nx, ny), in_specs=[IN...  3.23 us
    pallas_call x1, Pallas kernels, ends(): pl.pallas_call(functools.partial(ends_kernel, nx, ny), in_specs=[IN_VMEM]...  2.87 us
  transfers between devices with their start and end apart: 9, of which 2 were waited for; matrix products, arithmetic and copies ran while one was open for 0% of the time, Pallas kernels for 41%

profile of v10, /device:TPU:0, one launch (start us, length us, event | category | flops | bytes accessed | tf_op | source)
XLA Modules:
  0.0 35.7 jit_solution(16712123630303787903)
XLA Ops:
  0.0 3.2 %pool.1 = (bf16[16,1024,128]{2,1,0:T(8,128)(2,1)S(1)}, s32[16,16,64]{2,1,0:T(8,128)S(1)}, f32[256,768]{1,0:T(8,128)S(1)}, bf16[128,128]{1,0:T(8,128)(2,1)S(1)}, ...) custom-call(bf16[16,1024,128]{2,1,0:T(8,128)(2,1)} %bitcast.7, ...), custom_call_target="tpu_custom_call" | custom-call | tf_op jit(solution)/shard_map/pool/pallas_call | solution.py:101
  3.2 3.1 %collective-permute-start = (bf16[64,128]{1,0:T(8,128)(2,1)S(1)}, bf16[64,128]{1,0:T(8,128)(2,1)S(1)}, u32[]{:S(2)}, u32[]{:S(2)}) collective-permute-start(bf16[64,128]{1,0:T(8,128)(2,1)S(1)} %get-tuple-element.22.rest_0_.refs_0_), channel_id=1, source_target_pairs={{0,8},{8,0},{16,24},{24,16},{1,9},{9,1},{17,25},{25,17},{2,10},{10... | collective-permute-start | bytes 49160 | tf_op jit(solution)/shard_map/ppermute | solution.py:344
  6.3 0.0 collective-permute-start.2
  6.3 0.2 collective-permute-start.3
  6.5 3.1 %inner_0.1.refs_2_.rest_0_ = bf16[16,1024,256]{2,1,0:T(8,128)(2,1)S(1)} custom-call(bf16[16,1024,128]{2,1,0:T(8,128)(2,1)S(1)} %get-tuple-element.18.fv.fv_ref, s32[16,16,64]{2,1,0:T(8,128)S(1)} %get-tuple-element.19.pv, f32[256,768]{1,0:T(8,128)S(1)} %get-tuple-element.20.mv, bf16[128,128]{1,0:T(8,128)(2,1)S(1)} %get-tuple-element.21.m, ...), custom_call_target="tpu_custom_call" | custom-call | flops 1600000000 | bytes 1000000 | tf_op jit(solution)/shard_map/inner_0/pallas_call | solution.py:267
  9.6 2.9 %collective-permute-start.1 = (bf16[128,128]{1,0:T(8,128)(2,1)S(1)}, bf16[128,128]{1,0:T(8,128)(2,1)S(1)}, u32[]{:S(2)}, u32[]{:S(2)}) collective-permute-start(bf16[128,128]{1,0:T(8,128)(2,1)S(1)} %join.4.rest_1_.refs_0_), channel_id=1, source_target_pairs={{0,16},{8,24},{16,0},{24,8},{1,17},{9,25},{17,1},{25,9},{2,18},{10... | collective-permute-start | bytes 98312 | tf_op jit(solution)/shard_map/ppermute | solution.py:344
  12.6 2.3 %inner_1.1.refs_2_.rest_0_ = bf16[16,1024,256]{2,1,0:T(8,128)(2,1)S(1)} custom-call(bf16[16,1024,128]{2,1,0:T(8,128)(2,1)S(1)} %get-tuple-element.18.fv.fv_ref, s32[16,16,64]{2,1,0:T(8,128)S(1)} %get-tuple-element.19.pv, f32[256,768]{1,0:T(8,128)S(1)} %get-tuple-element.20.mv, ...), custom_call_target="tpu_custom_call", output_to_operand_aliasing={{}: (4, {})} | custom-call | flops 1200000000 | bytes 1000000 | tf_op jit(solution)/shard_map/inner_1/pallas_call | solution.py:267
  14.9 0.0 collective-permute-done.1.refs_1_
  14.9 2.1 %collective-permute-start.4 = (bf16[256,128]{1,0:T(8,128)(2,1)S(1)}, bf16[256,128]{1,0:T(8,128)(2,1)S(1)}, u32[]{:S(2)}, u32[]{:S(2)}) collective-permute-start(bf16[256,128]{1,0:T(8,128)(2,1)S(1)} %join.5.rest_1_.refs_0_), channel_id=1, source_target_pairs={{0,2},{1,3},{2,0},{3,1},{4,6},{5,7},{6,4},{7,5},{8,10},{9,11},{10,... | collective-permute-start | bytes 196616 | tf_op jit(solution)/shard_map/ppermute | solution.py:344
  17.1 0.0 collective-permute-done.2.paired_ref
  17.1 0.0 collective-permute-done.3.other_ref
  17.1 0.3 edge_rows.1
  17.4 0.1 collective-permute-start.6
  17.5 2.3 %inner_2.1.refs_2_.rest_0_ = bf16[16,1024,256]{2,1,0:T(8,128)(2,1)S(1)} custom-call(bf16[16,1024,128]{2,1,0:T(8,128)(2,1)S(1)} %get-tuple-element.18.fv.fv_ref, s32[16,16,64]{2,1,0:T(8,128)S(1)} %get-tuple-element.19.pv, f32[256,768]{1,0:T(8,128)S(1)} %get-tuple-element.20.mv, ...), custom_call_target="tpu_custom_call", output_to_operand_aliasing={{}: (4, {})} | custom-call | flops 1200000000 | bytes 1000000 | tf_op jit(solution)/shard_map/inner_2/pallas_call | solution.py:267
  19.8 0.1 collective-permute-done.4.refs_1_
  19.9 2.1 %collective-permute-start.5 = (bf16[512,128]{1,0:T(8,128)(2,1)S(1)}, bf16[512,128]{1,0:T(8,128)(2,1)S(1)}, u32[]{:S(2)}, u32[]{:S(2)}) collective-permute-start(bf16[512,128]{1,0:T(8,128)(2,1)S(1)} %join.6.rest_1_.refs_0_), channel_id=1, source_target_pairs={{0,4},{1,5},{2,6},{3,7},{4,0},{5,1},{6,2},{7,3},{8,12},{9,13},{10,... | collective-permute-start | bytes 393224 | tf_op jit(solution)/shard_map/ppermute | solution.py:344
  22.0 3.1 %inner_3.1.refs_2_.out_in = bf16[16,1024,256]{2,1,0:T(8,128)(2,1)S(1)} custom-call(bf16[16,1024,128]{2,1,0:T(8,128)(2,1)S(1)} %get-tuple-element.18.fv.fv_ref, s32[16,16,64]{2,1,0:T(8,128)S(1)} %get-tuple-element.19.pv, f32[256,768]{1,0:T(8,128)S(1)} %get-tuple-element.20.mv, ...), custom_call_target="tpu_custom_call", output_to_operand_aliasing={{}: (4, {})} | custom-call | flops 1600000000 | bytes 1000000 | tf_op jit(solution)/shard_map/inner_3/pallas_call | solution.py:267
  25.1 0.4 %collective-permute-done.5.refs_1_ = bf16[512,128]{1,0:T(8,128)(2,1)S(1)} collective-permute-done((bf16[512,128]{1,0:T(8,128)(2,1)S(1)}, bf16[512,128]{1,0:T(8,128)(2,1)S(1)}, u32[]{:S(2)}, u32[]{:S(2)}) %collective-permute-start.5) | collective-permute-done | bytes 131104 | tf_op jit(solution)/shard_map/ppermute | solution.py:344
  25.5 0.2 collective-permute-start.8
  25.7 0.0 copy-start.4
  25.7 3.4 %sides.1.out_in = bf16[16,1024,256]{2,1,0:T(8,128)(2,1)S(1)} custom-call(bf16[16,1024,128]{2,1,0:T(8,128)(2,1)S(1)} %get-tuple-element.18.fv.fv_ref, s32[16,16,64]{2,1,0:T(8,128)S(1)} %get-tuple-element.19.pv, f32[256,768]{1,0:T(8,128)S(1)} %get-tuple-element.20.mv, bf16[128,128]{1,0:T(8,128)(2,1)S(1)} %get-tuple-element.21.m, ...), custom_call_target="tpu_custom_call", output_to_operand_aliasing={{}: (4, {})} | custom-call | flops 1400000000 | bytes 1000000 | tf_op jit(solution)/shard_map/sides/pallas_call | solution.py:267
  29.1 0.0 collective-permute-done.7.other_row
  29.2 2.9 %ends.1 = (bf16[16,1024,256]{2,1,0:T(8,128)(2,1)S(1)}, bf16[256,128]{1,0:T(8,128)(2,1)S(1)}) custom-call(bf16[16,1024,128]{2,1,0:T(8,128)(2,1)S(1)} %get-tuple-element.18.fv.fv_ref, s32[16,16,64]{2,1,0:T(8,128)S(1)} %get-tuple-element.19.pv, f32[256,768]{1,0:T(8,128)S(1)} %get-tuple-element.20.mv, ...), custom_call_target="tpu_custom_call", output_to_operand_aliasing={{0}: (4, {})} | custom-call | flops 800000000 | bytes 1000000 | tf_op jit(solution)/shard_map/ends/pallas_call | solution.py:303
  32.1 3.5 %final.1 = bf16[16,1024,128]{2,1,0:T(8,128)(2,1)} custom-call(bf16[16,1024,256]{2,1,0:T(8,128)(2,1)S(1)} %get-tuple-element.29.o_ref, bf16[256,128]{1,0:T(8,128)(2,1)S(1)} %get-tuple-element.30.mix), custom_call_target="tpu_custom_call" | custom-call | tf_op jit(solution)/shard_map/final/pallas_call | solution.py:332
  (17 shorter events, 0.1 us)
Async XLA Ops:
  3.2 6.4 %collective-permute-start = (bf16[64,128]{1,0:T(8,128)(2,1)S(1)}, bf16[64,128]{1,0:T(8,128)(2,1)S(1)}, u32[]{:S(2)}, u32[]{:S(2)}) collective-permute-start(bf16[64,128]{1,0:T(8,128)(2,1)S(1)} %get-tuple-element.22.rest_0_.refs_0_), channel_id=1, source_target_pairs={{0,8},{8,0},{16,24},{24,16},{1,9},{9,1},{17,25},{25,17},{2,10},{10... | collective-permute-start | bytes 49160 | tf_op jit(solution)/shard_map/ppermute | solution.py:344
  6.3 10.8 %collective-permute-start.2 = (bf16[1024,128]{1,0:T(8,128)(2,1)S(1)}, bf16[1024,128]{1,0:T(8,128)(2,1)S(1)}, u32[]{:S(2)}, u32[]{:S(2)}) collective-permute-start(bf16[1024,128]{1,0:T(8,128)(2,1)S(1)} %get-tuple-element.23), channel_id=1, source_target_pairs={{0,1},{1,0},{2,3},{3,2},{4,5},{5,4},{6,7},{7,6},{8,9},{9,8},{10,11... | collective-permute-start | bytes 786440 | tf_op jit(solution)/shard_map/ppermute | solution.py:344
  6.3 10.8 %collective-permute-start.3 = (bf16[1024,128]{1,0:T(8,128)(2,1)S(1)}, bf16[1024,128]{1,0:T(8,128)(2,1)S(1)}, u32[]{:S(2)}, u32[]{:S(2)}) collective-permute-start(bf16[1024,128]{1,0:T(8,128)(2,1)S(1)} %get-tuple-element.24), channel_id=1, source_target_pairs={{0,8},{1,2},{2,1},{3,4},{4,3},{5,6},{6,5},{7,15},{8,0},{9,10},{10,... | collective-permute-start | bytes 786440 | tf_op jit(solution)/shard_map/ppermute | solution.py:415
  9.6 5.3 %collective-permute-start.1 = (bf16[128,128]{1,0:T(8,128)(2,1)S(1)}, bf16[128,128]{1,0:T(8,128)(2,1)S(1)}, u32[]{:S(2)}, u32[]{:S(2)}) collective-permute-start(bf16[128,128]{1,0:T(8,128)(2,1)S(1)} %join.4.rest_1_.refs_0_), channel_id=1, source_target_pairs={{0,16},{8,24},{16,0},{24,8},{1,17},{9,25},{17,1},{25,9},{2,18},{10... | collective-permute-start | bytes 98312 | tf_op jit(solution)/shard_map/ppermute | solution.py:344
  14.9 4.9 %collective-permute-start.4 = (bf16[256,128]{1,0:T(8,128)(2,1)S(1)}, bf16[256,128]{1,0:T(8,128)(2,1)S(1)}, u32[]{:S(2)}, u32[]{:S(2)}) collective-permute-start(bf16[256,128]{1,0:T(8,128)(2,1)S(1)} %join.5.rest_1_.refs_0_), channel_id=1, source_target_pairs={{0,2},{1,3},{2,0},{3,1},{4,6},{5,7},{6,4},{7,5},{8,10},{9,11},{10,... | collective-permute-start | bytes 196616 | tf_op jit(solution)/shard_map/ppermute | solution.py:344
  17.4 11.8 %collective-permute-start.6 = (bf16[1152,128]{1,0:T(8,128)(2,1)S(1)}, bf16[1152,128]{1,0:T(8,128)(2,1)S(1)}, u32[]{:S(2)}, u32[]{:S(2)}) collective-permute-start(bf16[1152,128]{1,0:T(8,128)(2,1)S(1)} %get-tuple-element.25.rest_2_), channel_id=1, source_target_pairs={{0,8},{8,0},{16,24},{24,16},{1,9},{9,1},{17,25},{25,17},{2,10},{10... | collective-permute-start | bytes 884744 | tf_op jit(solution)/shard_map/ppermute | solution.py:344
  19.9 5.6 %collective-permute-start.5 = (bf16[512,128]{1,0:T(8,128)(2,1)S(1)}, bf16[512,128]{1,0:T(8,128)(2,1)S(1)}, u32[]{:S(2)}, u32[]{:S(2)}) collective-permute-start(bf16[512,128]{1,0:T(8,128)(2,1)S(1)} %join.6.rest_1_.refs_0_), channel_id=1, source_target_pairs={{0,4},{1,5},{2,6},{3,7},{4,0},{5,1},{6,2},{7,3},{8,12},{9,13},{10,... | collective-permute-start | bytes 393224 | tf_op jit(solution)/shard_map/ppermute | solution.py:344
  22.0 7.1 %collective-permute-start.7 = (bf16[1152,128]{1,0:T(8,128)(2,1)S(1)}, bf16[1152,128]{1,0:T(8,128)(2,1)S(1)}, u32[]{:S(2)}, u32[]{:S(2)}) collective-permute-start(bf16[1152,128]{1,0:T(8,128)(2,1)S(1)} %get-tuple-element.28), channel_id=1, source_target_pairs={{0,1},{1,0},{2,3},{3,2},{4,5},{5,4},{6,7},{7,6},{8,16},{9,17},{10,... | collective-permute-start | bytes 884744 | tf_op jit(solution)/shard_map/ppermute | solution.py:415
  25.5 3.6 %collective-permute-start.8 = (bf16[1024,128]{1,0:T(8,128)(2,1)S(1)}, bf16[1024,128]{1,0:T(8,128)(2,1)S(1)}, u32[]{:S(2)}, u32[]{:S(2)}) collective-permute-start(bf16[1024,128]{1,0:T(8,128)(2,1)S(1)} %join.7.rest_0_), channel_id=1, source_target_pairs={{0,1},{1,0},{2,3},{3,2},{4,5},{5,4},{6,7},{7,6},{8,9},{9,8},{10,11... | collective-permute-start | bytes 786440 | tf_op jit(solution)/shard_map/ppermute | solution.py:344
  25.7 3.4 %copy-start = (bf16[128,128]{1,0:T(8,128)(2,1)S(1)}, bf16[128,128]{1,0:T(8,128)(2,1)}, u32[]{:S(2)}) copy-start(bf16[128,128]{1,0:T(8,128)(2,1)} %rest_3_.1) | copy-start | bytes 98308
  25.7 3.4 %copy-start.1 = (bf16[128,128]{1,0:T(8,128)(2,1)S(1)}, bf16[128,128]{1,0:T(8,128)(2,1)}, u32[]{:S(2)}) copy-start(bf16[128,128]{1,0:T(8,128)(2,1)} %rest_4_.1) | copy-start | bytes 98308
  25.7 3.5 %copy-start.2 = (bf16[128,128]{1,0:T(8,128)(2,1)S(1)}, bf16[128,128]{1,0:T(8,128)(2,1)}, u32[]{:S(2)}) copy-start(bf16[128,128]{1,0:T(8,128)(2,1)} %rest_5_.1) | copy-start | bytes 98308
  25.7 3.5 %copy-start.3 = (bf16[128,128]{1,0:T(8,128)(2,1)S(1)}, bf16[128,128]{1,0:T(8,128)(2,1)}, u32[]{:S(2)}) copy-start(bf16[128,128]{1,0:T(8,128)(2,1)} %rest_6_.1) | copy-start | bytes 98308
  25.7 3.5 %copy-start.4 = (s32[32,8]{0,1:T(8,128)S(1)}, s32[32,8]{0,1:T(8,128)}, u32[]{:S(2)}) copy-start(s32[32,8]{0,1:T(8,128)} %param.13) | copy-start | bytes 3076

commit v11 on v10

--- a/solution.py
+++ b/solution.py
@@ -128,7 +128,7 @@
     )
 
 
-def attend(tile, tasks):
+def attend(tile, tasks, between=()):
     waiting = []
 
     def finish(task, weights):
@@ -136,7 +136,9 @@
         near = jnp.concatenate([window() for window in windows], axis=0)
         store(dot(jnp.concatenate(weights, axis=1), near).astype(BF16))
 
-    for task in tasks:
+    for at, task in enumerate(tasks):
+        if at in between:
+            between[at]()
         query, windows, masks, _ = task
         weights = []
         for r, window in enumerate(windows):
@@ -249,12 +251,12 @@
             return (above if r < 0 else below)[2 * tile * j : 2 * tile * (j + 2)]
         return near(r, j)
 
-    coarse(nx, ny, (first, second), *weights, mix)
+    between = coarse(nx, ny, (first, second), *weights, mix)
     tasks = []
     for row in (0, rows - 1):
         node_rows(refs, row)
         tasks += row_tasks(refs, row, 0, cy // 2, window)
-    attend(tile, tasks)
+    attend(tile, tasks, between)
 
 
 def estimate(rows):
@@ -287,14 +289,24 @@
     lane = lax.broadcasted_iota(jnp.int32, readers_ref.shape, 1)
     mine = jnp.sum(jnp.where(lane == mx * ny + my, readers_ref[...], 0), axis=1, keepdims=True)
     live = jnp.sum(jnp.where(domain == mine, 1.0, 0.0), axis=0, keepdims=True)
-    query = dot(nodes[:S], wcq_ref[...]).astype(BF16)
-    key = dot(nodes, wck_ref[...]).astype(BF16)
-    value = dot(nodes, wcv_ref[...]).astype(BF16)
-    half = dot_t(query, key) * (0.5 / math.sqrt(chan))
-    weight = (half * jnp.tanh(half) + half).astype(BF16).astype(F32) * live
-    mix[:chan] = wv_ref[...]
-    mix[chan : chan + S] = (dot(weight.astype(BF16), value) / math.sqrt(S)).astype(BF16)
-    mix[chan + S :] = jnp.zeros((chan - S, chan), BF16)
+    held = {}
+
+    def project():
+        held["query"] = dot(nodes[:S], wcq_ref[...]).astype(BF16)
+        held["key"] = dot(nodes, wck_ref[...]).astype(BF16)
+        held["value"] = dot(nodes, wcv_ref[...]).astype(BF16)
+
+    def weigh():
+        half = dot_t(held["query"], held["key"]) * (0.5 / math.sqrt(chan))
+        weight = (half * jnp.tanh(half) + half).astype(BF16).astype(F32) * live
+        held["weight"] = weight.astype(BF16)
+
+    def gather():
+        mix[:chan] = wv_ref[...]
+        mix[chan : chan + S] = (dot(held["weight"], held["value"]) / math.sqrt(S)).astype(BF16)
+        mix[chan + S :] = jnp.zeros((chan - S, chan), BF16)
+
+    return {2: project, 6: weigh, 10: gather}
 
 
 def ends(nx, ny, base, out, halos, blocks, readers, w_cquery, w_ckey, w_cvalue, w_value):

time: 36 us -> 36 us (level)
  no operation moved by 1% of the time
where the time goes in v11:
time: 36 us; the launch traced here: 35.7 us
  Pallas kernels  24.1 us (67%)
  starting transfers between devices  10.8 us (30%)
  waiting for transfers between devices  0.45 us (1%)
    pallas_call x5, Pallas kernels, piece(): pl.pallas_call(kernel, in_specs=[IN_VMEM] * (4 + len(done) + len(near)) +...  14.3 us
    ppermute x7, starting transfers between devices, swap(): lax.ppermute(array, axis, [(i, i ^ bits) for i in range(lax.axis_size(axi...  10.6 us
    pallas_call x1, Pallas kernels, final(): pl.pallas_call(final_kernel, in_specs=[IN_VMEM] * 2, out_specs=IN_HBM, ou...  3.48 us
    pallas_call x1, Pallas kernels, pool(): pl.pallas_call(functools.partial(pool_kernel, tile, nx, ny), in_specs=[IN...  3.23 us
    pallas_call x1, Pallas kernels, ends(): pl.pallas_call(functools.partial(ends_kernel, nx, ny), in_specs=[IN_VMEM]...  2.87 us
  transfers between devices with their start and end apart: 9, of which 2 were waited for; matrix products, arithmetic and copies ran while one was open for 0% of the time, Pallas kernels for 41%

profile of v11, /device:TPU:0, one launch (start us, length us, event | category | flops | bytes accessed | tf_op | source)
XLA Modules:
  0.0 35.7 jit_solution(11806971902150988654)
XLA Ops:
  0.0 3.2 %pool.1 = (bf16[16,1024,128]{2,1,0:T(8,128)(2,1)S(1)}, s32[16,16,64]{2,1,0:T(8,128)S(1)}, f32[256,768]{1,0:T(8,128)S(1)}, bf16[128,128]{1,0:T(8,128)(2,1)S(1)}, ...) custom-call(bf16[16,1024,128]{2,1,0:T(8,128)(2,1)} %bitcast.7, ...), custom_call_target="tpu_custom_call" | custom-call | tf_op jit(solution)/shard_map/pool/pallas_call | solution.py:101
  3.2 3.1 %collective-permute-start = (bf16[64,128]{1,0:T(8,128)(2,1)S(1)}, bf16[64,128]{1,0:T(8,128)(2,1)S(1)}, u32[]{:S(2)}, u32[]{:S(2)}) collective-permute-start(bf16[64,128]{1,0:T(8,128)(2,1)S(1)} %get-tuple-element.22.rest_0_.refs_0_), channel_id=1, source_target_pairs={{0,8},{8,0},{16,24},{24,16},{1,9},{9,1},{17,25},{25,17},{2,10},{10... | collective-permute-start | bytes 49160 | tf_op jit(solution)/shard_map/ppermute | solution.py:356
  6.3 0.0 collective-permute-start.2
  6.3 0.2 collective-permute-start.3
  6.5 3.1 %inner_0.1.refs_2_.rest_0_ = bf16[16,1024,256]{2,1,0:T(8,128)(2,1)S(1)} custom-call(bf16[16,1024,128]{2,1,0:T(8,128)(2,1)S(1)} %get-tuple-element.18.fv.fv_ref, s32[16,16,64]{2,1,0:T(8,128)S(1)} %get-tuple-element.19.pv, f32[256,768]{1,0:T(8,128)S(1)} %get-tuple-element.20.mv, bf16[128,128]{1,0:T(8,128)(2,1)S(1)} %get-tuple-element.21.m, ...), custom_call_target="tpu_custom_call" | custom-call | flops 1600000000 | bytes 1000000 | tf_op jit(solution)/shard_map/inner_0/pallas_call | solution.py:269
  9.6 0.0 collective-permute-done.refs_1_
  9.6 2.9 %collective-permute-start.1 = (bf16[128,128]{1,0:T(8,128)(2,1)S(1)}, bf16[128,128]{1,0:T(8,128)(2,1)S(1)}, u32[]{:S(2)}, u32[]{:S(2)}) collective-permute-start(bf16[128,128]{1,0:T(8,128)(2,1)S(1)} %join.4.rest_1_.refs_0_), channel_id=1, source_target_pairs={{0,16},{8,24},{16,0},{24,8},{1,17},{9,25},{17,1},{25,9},{2,18},{10... | collective-permute-start | bytes 98312 | tf_op jit(solution)/shard_map/ppermute | solution.py:356
  12.6 2.3 %inner_1.1.refs_2_.rest_0_ = bf16[16,1024,256]{2,1,0:T(8,128)(2,1)S(1)} custom-call(bf16[16,1024,128]{2,1,0:T(8,128)(2,1)S(1)} %get-tuple-element.18.fv.fv_ref, s32[16,16,64]{2,1,0:T(8,128)S(1)} %get-tuple-element.19.pv, f32[256,768]{1,0:T(8,128)S(1)} %get-tuple-element.20.mv, ...), custom_call_target="tpu_custom_call", output_to_operand_aliasing={{}: (4, {})} | custom-call | flops 1200000000 | bytes 1000000 | tf_op jit(solution)/shard_map/inner_1/pallas_call | solution.py:269
  14.9 2.1 %collective-permute-start.4 = (bf16[256,128]{1,0:T(8,128)(2,1)S(1)}, bf16[256,128]{1,0:T(8,128)(2,1)S(1)}, u32[]{:S(2)}, u32[]{:S(2)}) collective-permute-start(bf16[256,128]{1,0:T(8,128)(2,1)S(1)} %join.5.rest_1_.refs_0_), channel_id=1, source_target_pairs={{0,2},{1,3},{2,0},{3,1},{4,6},{5,7},{6,4},{7,5},{8,10},{9,11},{10,... | collective-permute-start | bytes 196616 | tf_op jit(solution)/shard_map/ppermute | solution.py:356
  17.1 0.3 edge_rows.1
  17.4 0.1 collective-permute-start.6
  17.5 2.3 %inner_2.1.refs_2_.rest_0_ = bf16[16,1024,256]{2,1,0:T(8,128)(2,1)S(1)} custom-call(bf16[16,1024,128]{2,1,0:T(8,128)(2,1)S(1)} %get-tuple-element.18.fv.fv_ref, s32[16,16,64]{2,1,0:T(8,128)S(1)} %get-tuple-element.19.pv, f32[256,768]{1,0:T(8,128)S(1)} %get-tuple-element.20.mv, ...), custom_call_target="tpu_custom_call", output_to_operand_aliasing={{}: (4, {})} | custom-call | flops 1200000000 | bytes 1000000 | tf_op jit(solution)/shard_map/inner_2/pallas_call | solution.py:269
  19.8 0.1 collective-permute-done.4.refs_1_
  19.9 2.1 %collective-permute-start.5 = (bf16[512,128]{1,0:T(8,128)(2,1)S(1)}, bf16[512,128]{1,0:T(8,128)(2,1)S(1)}, u32[]{:S(2)}, u32[]{:S(2)}) collective-permute-start(bf16[512,128]{1,0:T(8,128)(2,1)S(1)} %join.6.rest_1_.refs_0_), channel_id=1, source_target_pairs={{0,4},{1,5},{2,6},{3,7},{4,0},{5,1},{6,2},{7,3},{8,12},{9,13},{10,... | collective-permute-start | bytes 393224 | tf_op jit(solution)/shard_map/ppermute | solution.py:356
  22.0 0.0 collective-permute-start.7
  22.0 3.1 %inner_3.1.refs_2_.out_in = bf16[16,1024,256]{2,1,0:T(8,128)(2,1)S(1)} custom-call(bf16[16,1024,128]{2,1,0:T(8,128)(2,1)S(1)} %get-tuple-element.18.fv.fv_ref, s32[16,16,64]{2,1,0:T(8,128)S(1)} %get-tuple-element.19.pv, f32[256,768]{1,0:T(8,128)S(1)} %get-tuple-element.20.mv, ...), custom_call_target="tpu_custom_call", output_to_operand_aliasing={{}: (4, {})} | custom-call | flops 1600000000 | bytes 1000000 | tf_op jit(solution)/shard_map/inner_3/pallas_call | solution.py:269
  25.1 0.4 %collective-permute-done.5.refs_1_ = bf16[512,128]{1,0:T(8,128)(2,1)S(1)} collective-permute-done((bf16[512,128]{1,0:T(8,128)(2,1)S(1)}, bf16[512,128]{1,0:T(8,128)(2,1)S(1)}, u32[]{:S(2)}, u32[]{:S(2)}) %collective-permute-start.5) | collective-permute-done | bytes 131104 | tf_op jit(solution)/shard_map/ppermute | solution.py:356
  25.5 0.2 collective-permute-start.8
  25.7 0.0 copy-start.4
  25.7 3.4 %sides.1.out_in = bf16[16,1024,256]{2,1,0:T(8,128)(2,1)S(1)} custom-call(bf16[16,1024,128]{2,1,0:T(8,128)(2,1)S(1)} %get-tuple-element.18.fv.fv_ref, s32[16,16,64]{2,1,0:T(8,128)S(1)} %get-tuple-element.19.pv, f32[256,768]{1,0:T(8,128)S(1)} %get-tuple-element.20.mv, bf16[128,128]{1,0:T(8,128)(2,1)S(1)} %get-tuple-element.21.m, ...), custom_call_target="tpu_custom_call", output_to_operand_aliasing={{}: (4, {})} | custom-call | flops 1400000000 | bytes 1000000 | tf_op jit(solution)/shard_map/sides/pallas_call | solution.py:269
  29.1 0.0 collective-permute-done.7.other_row
  29.1 0.0 collective-permute-done.6.paired_row
  29.2 2.9 %ends.1 = (bf16[16,1024,256]{2,1,0:T(8,128)(2,1)S(1)}, bf16[256,128]{1,0:T(8,128)(2,1)S(1)}) custom-call(bf16[16,1024,128]{2,1,0:T(8,128)(2,1)S(1)} %get-tuple-element.18.fv.fv_ref, s32[16,16,64]{2,1,0:T(8,128)S(1)} %get-tuple-element.19.pv, f32[256,768]{1,0:T(8,128)S(1)} %get-tuple-element.20.mv, ...), custom_call_target="tpu_custom_call", output_to_operand_aliasing={{0}: (4, {})} | custom-call | flops 800000000 | bytes 1000000 | tf_op jit(solution)/shard_map/ends/pallas_call | solution.py:315
  32.1 3.5 %final.1 = bf16[16,1024,128]{2,1,0:T(8,128)(2,1)} custom-call(bf16[16,1024,256]{2,1,0:T(8,128)(2,1)S(1)} %get-tuple-element.29.o_ref, bf16[256,128]{1,0:T(8,128)(2,1)S(1)} %get-tuple-element.30.mix), custom_call_target="tpu_custom_call" | custom-call | tf_op jit(solution)/shard_map/final/pallas_call | solution.py:344
  (17 shorter events, 0.1 us)
Async XLA Ops:
  3.2 6.4 %collective-permute-start = (bf16[64,128]{1,0:T(8,128)(2,1)S(1)}, bf16[64,128]{1,0:T(8,128)(2,1)S(1)}, u32[]{:S(2)}, u32[]{:S(2)}) collective-permute-start(bf16[64,128]{1,0:T(8,128)(2,1)S(1)} %get-tuple-element.22.rest_0_.refs_0_), channel_id=1, source_target_pairs={{0,8},{8,0},{16,24},{24,16},{1,9},{9,1},{17,25},{25,17},{2,10},{10... | collective-permute-start | bytes 49160 | tf_op jit(solution)/shard_map/ppermute | solution.py:356
  6.3 10.8 %collective-permute-start.2 = (bf16[1024,128]{1,0:T(8,128)(2,1)S(1)}, bf16[1024,128]{1,0:T(8,128)(2,1)S(1)}, u32[]{:S(2)}, u32[]{:S(2)}) collective-permute-start(bf16[1024,128]{1,0:T(8,128)(2,1)S(1)} %get-tuple-element.23), channel_id=1, source_target_pairs={{0,1},{1,0},{2,3},{3,2},{4,5},{5,4},{6,7},{7,6},{8,9},{9,8},{10,11... | collective-permute-start | bytes 786440 | tf_op jit(solution)/shard_map/ppermute | solution.py:356
  6.3 10.8 %collective-permute-start.3 = (bf16[1024,128]{1,0:T(8,128)(2,1)S(1)}, bf16[1024,128]{1,0:T(8,128)(2,1)S(1)}, u32[]{:S(2)}, u32[]{:S(2)}) collective-permute-start(bf16[1024,128]{1,0:T(8,128)(2,1)S(1)} %get-tuple-element.24), channel_id=1, source_target_pairs={{0,8},{1,2},{2,1},{3,4},{4,3},{5,6},{6,5},{7,15},{8,0},{9,10},{10,... | collective-permute-start | bytes 786440 | tf_op jit(solution)/shard_map/ppermute | solution.py:427
  9.6 5.3 %collective-permute-start.1 = (bf16[128,128]{1,0:T(8,128)(2,1)S(1)}, bf16[128,128]{1,0:T(8,128)(2,1)S(1)}, u32[]{:S(2)}, u32[]{:S(2)}) collective-permute-start(bf16[128,128]{1,0:T(8,128)(2,1)S(1)} %join.4.rest_1_.refs_0_), channel_id=1, source_target_pairs={{0,16},{8,24},{16,0},{24,8},{1,17},{9,25},{17,1},{25,9},{2,18},{10... | collective-permute-start | bytes 98312 | tf_op jit(solution)/shard_map/ppermute | solution.py:356
  14.9 4.9 %collective-permute-start.4 = (bf16[256,128]{1,0:T(8,128)(2,1)S(1)}, bf16[256,128]{1,0:T(8,128)(2,1)S(1)}, u32[]{:S(2)}, u32[]{:S(2)}) collective-permute-start(bf16[256,128]{1,0:T(8,128)(2,1)S(1)} %join.5.rest_1_.refs_0_), channel_id=1, source_target_pairs={{0,2},{1,3},{2,0},{3,1},{4,6},{5,7},{6,4},{7,5},{8,10},{9,11},{10,... | collective-permute-start | bytes 196616 | tf_op jit(solution)/shard_map/ppermute | solution.py:356
  17.4 11.8 %collective-permute-start.6 = (bf16[1152,128]{1,0:T(8,128)(2,1)S(1)}, bf16[1152,128]{1,0:T(8,128)(2,1)S(1)}, u32[]{:S(2)}, u32[]{:S(2)}) collective-permute-start(bf16[1152,128]{1,0:T(8,128)(2,1)S(1)} %get-tuple-element.25.rest_2_), channel_id=1, source_target_pairs={{0,8},{8,0},{16,24},{24,16},{1,9},{9,1},{17,25},{25,17},{2,10},{10... | collective-permute-start | bytes 884744 | tf_op jit(solution)/shard_map/ppermute | solution.py:356
  19.9 5.6 %collective-permute-start.5 = (bf16[512,128]{1,0:T(8,128)(2,1)S(1)}, bf16[512,128]{1,0:T(8,128)(2,1)S(1)}, u32[]{:S(2)}, u32[]{:S(2)}) collective-permute-start(bf16[512,128]{1,0:T(8,128)(2,1)S(1)} %join.6.rest_1_.refs_0_), channel_id=1, source_target_pairs={{0,4},{1,5},{2,6},{3,7},{4,0},{5,1},{6,2},{7,3},{8,12},{9,13},{10,... | collective-permute-start | bytes 393224 | tf_op jit(solution)/shard_map/ppermute | solution.py:356
  22.0 7.1 %collective-permute-start.7 = (bf16[1152,128]{1,0:T(8,128)(2,1)S(1)}, bf16[1152,128]{1,0:T(8,128)(2,1)S(1)}, u32[]{:S(2)}, u32[]{:S(2)}) collective-permute-start(bf16[1152,128]{1,0:T(8,128)(2,1)S(1)} %get-tuple-element.28), channel_id=1, source_target_pairs={{0,1},{1,0},{2,3},{3,2},{4,5},{5,4},{6,7},{7,6},{8,16},{9,17},{10,... | collective-permute-start | bytes 884744 | tf_op jit(solution)/shard_map/ppermute | solution.py:427
  25.5 3.6 %collective-permute-start.8 = (bf16[1024,128]{1,0:T(8,128)(2,1)S(1)}, bf16[1024,128]{1,0:T(8,128)(2,1)S(1)}, u32[]{:S(2)}, u32[]{:S(2)}) collective-permute-start(bf16[1024,128]{1,0:T(8,128)(2,1)S(1)} %join.7.rest_0_), channel_id=1, source_target_pairs={{0,1},{1,0},{2,3},{3,2},{4,5},{5,4},{6,7},{7,6},{8,9},{9,8},{10,11... | collective-permute-start | bytes 786440 | tf_op jit(solution)/shard_map/ppermute | solution.py:356
  25.7 3.4 %copy-start = (bf16[128,128]{1,0:T(8,128)(2,1)S(1)}, bf16[128,128]{1,0:T(8,128)(2,1)}, u32[]{:S(2)}) copy-start(bf16[128,128]{1,0:T(8,128)(2,1)} %rest_3_.1) | copy-start | bytes 98308
  25.7 3.4 %copy-start.1 = (bf16[128,128]{1,0:T(8,128)(2,1)S(1)}, bf16[128,128]{1,0:T(8,128)(2,1)}, u32[]{:S(2)}) copy-start(bf16[128,128]{1,0:T(8,128)(2,1)} %rest_4_.1) | copy-start | bytes 98308
  25.7 3.5 %copy-start.2 = (bf16[128,128]{1,0:T(8,128)(2,1)S(1)}, bf16[128,128]{1,0:T(8,128)(2,1)}, u32[]{:S(2)}) copy-start(bf16[128,128]{1,0:T(8,128)(2,1)} %rest_5_.1) | copy-start | bytes 98308
  25.7 3.5 %copy-start.3 = (bf16[128,128]{1,0:T(8,128)(2,1)S(1)}, bf16[128,128]{1,0:T(8,128)(2,1)}, u32[]{:S(2)}) copy-start(bf16[128,128]{1,0:T(8,128)(2,1)} %rest_6_.1) | copy-start | bytes 98308
  25.7 3.5 %copy-start.4 = (s32[32,8]{0,1:T(8,128)S(1)}, s32[32,8]{0,1:T(8,128)}, u32[]{:S(2)}) copy-start(s32[32,8]{0,1:T(8,128)} %param.13) | copy-start | bytes 3076
